TPU v7x, 32 devices: a whole 2x2x4 slice. The times are simulated.
32 devices in a mesh: scan: 2 (over x), tile: 16 (over z, y, core).
Axes of the slice: x: 2, y: 2, z: 4, core: 2. Of those that a mesh axis runs over, the one named last changes fastest.
Arguments:
- coefficients: bfloat16 [66, 2048], P(None, 'tile'), may hold values from -0.75 to 0.75
- zernike_table: bfloat16 [66, 4096], replicated, may hold values from -6 to 6
- positions: int32 [32, 256], P('scan'), parts along dimension 0, may hold values from 0 to 4095
- source_flux: float32 [32, 256], P('scan'), parts along dimension 0, may hold values from 0.5 to 2
- observed: bfloat16 [2112, 16, 4096], P(('scan', 'tile')), parts along dimension 0, may hold values from -6 to 6
- tile_rows: int32 [2112], P(('scan', 'tile')), parts along dimension 0, may hold values from 0 to 31, as said below
- tile_cols: int32 [2112], P(('scan', 'tile')), parts along dimension 0, may hold values from 0 to 31, as said below
- tile_count: int32 [32], P(('scan', 'tile')), parts along dimension 0, may hold values from 0 to 66, as said below
Outputs:
- coeff_grad: float32 [132, 2048], P('scan', 'tile'), parts along dimension 0
There are 2 independent parts, one for each index of `scan`. A program takes and returns all parts, laid end to end along the dimension named above; an argument that names none is the same for every part. Nothing has to cross between parts.
Inputs may be any that keep to these rules, and one draw needn't show every extreme that they name: `tile_rows`: the live slots of a part hold every pair of dish blocks with row block at most column block exactly once; slots that are not live hold 0. `tile_cols`: column block of the same slot as tile_rows; never below its row block in a live slot. `tile_count`: live slots come first on each device; one device of every part has exactly 66 live slots.
All inputs are finite; a program needn't handle non-finite values.
Results may differ from a plain program's by a relative error of at most 0.0012.
Values may be sent and summed in bfloat16 or wider, within the bound.
No kernel may reach another device: no remote copies, remote signals or barrier semaphores. Data moves between devices by JAX's collectives and lax.ppermute only.
A program may use at most 128 MiB of HBM per device.

v0:
```python
import math

import jax
import jax.numpy as jnp
from jax import lax
from jax.sharding import PartitionSpec as P

BLK = 64


def from_partner(array, axis, stride):
    return lax.ppermute(array, axis, [(i, i ^ 1 << stride) for i in range(lax.axis_size(axis))])


def group_width(total_slots, channels):
    limit = max(1, 64 // channels)
    best = 1
    for candidate in range(1, total_slots + 1):
        if total_slots % candidate == 0 and candidate <= limit:
            best = candidate
    return best


def on_device(
    coefficients, zernike_table, positions, source_flux, observed, tile_rows, tile_cols, tile_count
):
    everything = lax.all_gather(coefficients, "tile", axis=1, tiled=True)
    selected = zernike_table[:, positions]
    n_terms = everything.shape[0]
    all_dishes = everything.shape[1]
    all_channels = positions.shape[0]
    held_vis = observed[None]
    row_block = tile_rows[None]
    col_block = tile_cols[None]
    live_counts = tile_count
    offset = 0
    for bit_number in (0, 1):
        half = held_vis.shape[2] // 2
        my_side = lax.axis_index("tile") // (1 << bit_number) % 2
        kept_vis = lax.dynamic_slice_in_dim(held_vis, my_side * half, half, 2)
        sent_vis = lax.dynamic_slice_in_dim(held_vis, (1 - my_side) * half, half, 2)
        got_vis, got_rows, got_cols, got_counts = from_partner(
            (sent_vis, row_block, col_block, live_counts), "tile", bit_number
        )
        held_vis = jnp.concatenate([kept_vis, got_vis], 0)
        row_block = jnp.concatenate([row_block, got_rows], 0)
        col_block = jnp.concatenate([col_block, got_cols], 0)
        live_counts = jnp.concatenate([live_counts, got_counts], 0)
        offset = offset + my_side * half
    pieces = held_vis.shape[0]
    slot_total = held_vis.shape[1]
    width_part = held_vis.shape[2]
    chosen = lax.dynamic_slice_in_dim(selected, offset, width_part, 1)
    flux_part = lax.dynamic_slice_in_dim(source_flux, offset, width_part, 0)
    sources = chosen.shape[2]
    root = math.sqrt(sources)
    n_blocks = all_dishes // BLK
    flat_total = pieces * slot_total
    flat_vis = held_vis.reshape(flat_total, width_part, BLK * BLK)
    flat_rows = row_block.reshape(flat_total)
    flat_cols = col_block.reshape(flat_total)
    slot_pos = lax.broadcasted_iota(jnp.int32, (pieces, slot_total), 1)
    live_flat = (slot_pos < live_counts[:, None]).astype(jnp.int32).reshape(flat_total)
    order = jnp.argsort(1 - live_flat, stable=True)
    n_live = jnp.sum(live_flat)
    group = group_width(flat_total, width_part)
    n_groups = (n_live + group - 1) // group
    coeff_blocks = everything.reshape(n_terms, n_blocks, BLK)
    block_ids = lax.broadcasted_iota(jnp.int32, (group, n_blocks), 1)
    row_index = lax.broadcasted_iota(jnp.int32, (BLK, BLK), 0)
    col_index = lax.broadcasted_iota(jnp.int32, (BLK, BLK), 1)

    def one_group(group_index, total):
        picks = lax.dynamic_slice_in_dim(order, group_index * group, group, 0)
        vis_group = flat_vis[picks].reshape(group, width_part, BLK, BLK).astype(jnp.float32)
        left_ids = flat_rows[picks]
        right_ids = flat_cols[picks]
        alive = live_flat[picks].astype(jnp.float32)
        left_hot = (block_ids == left_ids[:, None]).astype(jnp.bfloat16)
        right_hot = (block_ids == right_ids[:, None]).astype(jnp.bfloat16)
        left_coeff = jnp.einsum(
            "gn,kni->gki", left_hot, coeff_blocks, preferred_element_type=jnp.float32
        ).astype(jnp.bfloat16)
        right_coeff = jnp.einsum(
            "gn,kni->gki", right_hot, coeff_blocks, preferred_element_type=jnp.float32
        ).astype(jnp.bfloat16)
        left_beams = jnp.einsum(
            "gki,kfs->gfis", left_coeff, chosen, preferred_element_type=jnp.float32
        ).astype(jnp.bfloat16)
        right_beams = jnp.einsum(
            "gki,kfs->gfis", right_coeff, chosen, preferred_element_type=jnp.float32
        ).astype(jnp.bfloat16)
        left_weighted = (
            flux_part[None, :, None, :] * left_beams.astype(jnp.float32) / root
        ).astype(jnp.bfloat16)
        right_weighted = (
            flux_part[None, :, None, :] * right_beams.astype(jnp.float32) / root
        ).astype(jnp.bfloat16)
        model = jnp.einsum(
            "gfis,gfjs->gfij", left_weighted, right_beams, preferred_element_type=jnp.float32
        )
        keep = jnp.logical_or(
            (left_ids != right_ids)[:, None, None], (col_index > row_index)[None]
        ).astype(jnp.float32)
        keep = keep * alive[:, None, None]
        residual = ((model - vis_group) * keep[:, None]).astype(jnp.bfloat16)
        row_grad = jnp.einsum(
            "gfij,gfjs->gfis", residual, right_weighted, preferred_element_type=jnp.float32
        ).astype(jnp.bfloat16)
        col_grad = jnp.einsum(
            "gfij,gfis->gfjs", residual, left_weighted, preferred_element_type=jnp.float32
        ).astype(jnp.bfloat16)
        left_terms = jnp.einsum(
            "gfis,kfs->gki", row_grad, chosen, preferred_element_type=jnp.float32
        )
        right_terms = jnp.einsum(
            "gfjs,kfs->gkj", col_grad, chosen, preferred_element_type=jnp.float32
        )
        added = jnp.einsum(
            "gn,gki->kni", left_hot.astype(jnp.float32), left_terms, precision=lax.Precision.HIGHEST
        )
        added = added + jnp.einsum(
            "gn,gki->kni",
            right_hot.astype(jnp.float32),
            right_terms,
            precision=lax.Precision.HIGHEST,
        )
        return total + added

    start_total = jnp.zeros((n_terms, n_blocks, BLK), jnp.float32)
    partial_grad = lax.fori_loop(0, n_groups, one_group, start_total).reshape(n_terms, all_dishes)
    summed = lax.psum_scatter(partial_grad, "tile", scatter_dimension=1, tiled=True)
    return summed / math.sqrt(all_dishes * all_channels)


def solution(mesh):
    return jax.shard_map(
        on_device,
        mesh=mesh,
        in_specs=(
            P(None, "tile"),
            P(),
            P("scan", None),
            P("scan", None),
            P(("scan", "tile"), None, None),
            P(("scan", "tile")),
            P(("scan", "tile")),
            P(("scan", "tile")),
        ),
        out_specs=P("scan", "tile"),
        check_vma=False,
    )
```

profile of v0, /device:TPU:0, one launch (start us, length us, event | category | flops | bytes accessed | tf_op | source)
XLA Modules:
  0.0 583.6 jit_solution(10261772928095887289)
XLA Ops:
  6.5 8.1 %dynamic-slice_bitcast_fusion = (bf16[1,66,8,4096]{3,2,1,0:T(8,128)(2,1)}, bf16[1,66,8,4096]{3,2,1,0:T(8,128)(2,1)}) fusion(bf16[66,16,4096]{2,1,0:T(8,128)(2,1)} %param.14, s32[]{:T(128)S(6)} %select_n.58, s32[]{:T(128)S(6)} %select_n.57), kind=kLoop, calls=%fused_computation.64 | loop fusion | bytes 17301512 | tf_op jit(solution)/shard_map/dynamic_slice | solution.py:41
  15.1 7.3 %collective-permute-done.6 = bf16[1,66,8,4096]{3,2,1,0:T(8,128)(2,1)} collective-permute-done((bf16[1,66,8,4096]{3,2,1,0:T(8,128)(2,1)}, bf16[1,66,8,4096]{3,2,1,0:T(8,128)(2,1)}, u32[]{:S(2)}, u32[]{:S(2)}) %collective-permute-start.6) | collective-permute-done | bytes 4325408 | tf_op jit(solution)/shard_map/ppermute | solution.py:12
  22.4 11.9 %fusion.46 = (bf16[2,66,4,4096]{3,2,1,0:T(4,128)(2,1)}, bf16[2,66,4,4096]{3,2,1,0:T(4,128)(2,1)}) fusion(s32[]{:T(128)S(6)} %select_n.59, bf16[1,66,8,4096]{3,2,1,0:T(8,128)(2,1)} %get-tuple-element.266, bf16[1,66,8,4096]{3,2,1,0:T(8,128)(2,1)} %collective-permute-done.6, s32[]{:T(128)S(6)} %select_n.60), kind=kLoop, calls=%fused_computation.63 | loop fusion | flops 17301504 | bytes 17301512 | tf_op jit(solution)/shard_map/concatenate | solution.py:45
  39.2 12.1 %gather_fusion.4 = bf16[4096,66]{1,0:T(8,128)(2,1)S(1)} fusion(bf16[66,4096]{0,1:T(8,128)(2,1)S(1)} %copy.20, s32[4096]{0:T(1024)S(1)} %broadcast_clamp_fusion), kind=kCustom, calls=%fused_computation.4 | custom fusion | bytes 1097728 | tf_op jit(solution)/shard_map/gather | solution.py:28
  51.6 95.9 %all_gather.3 = bf16[66,2048]{1,0:T(8,128)(2,1)S(1)} all-gather(bf16[66,128]{1,0:T(8,128)(2,1)S(1)} %copy-done.5), channel_id=1, replica_groups=mesh['scan'=2,'tile'=16] {'tile'}, dimensions={1}, use_global_device_ids=true | all-gather | bytes 287232 | tf_op jit(solution)/shard_map/all_gather | solution.py:27
  149.9 3.5 collective-permute-done.1
  155.8 3.8 sort.17
  163.2 8.5 %pad_maximum_fusion = bf16[4,66,4,4096]{3,2,1,0:T(4,128)(2,1)} fusion(bf16[2,66,4,4096]{3,2,1,0:T(4,128)(2,1)} %collective-permute-done.7, bf16[2,66,4,4096]{3,2,1,0:T(4,128)(2,1)} %get-tuple-element.263), kind=kLoop, calls=%fused_computation.61 | loop fusion | flops 4325376 | bytes 17301504 | tf_op jit(solution)/shard_map/concatenate | solution.py:45
  172.9 272.8 %while.14 = (s32[]{:T(128)}, f32[66,32,64]{0,1,2:T(8,128)}, s32[]{:T(128)}, f32[4,256]{1,0:T(4,128)S(1)}, s32[264]{0:T(512)S(1)}, /*index=5*/s32[264]{0:T(512)S(...) while((s32[]{:T(128)}, f32[66,32,64]{0,1,2:T(8,128)}, ...), condition=%wide.region_3.4_spmd.clone.clone, body=%wide.region_2.3_spmd.clone.clone.sunk | while | flops 773146688 | bytes 21221820 | solution.py:131
  177.7 5.1 gather_fusion
  188.6 3.0 fusion.110
  194.6 3.1 fusion.111
  202.5 5.1 gather_fusion
  210.4 3.0 multiply_convert_fusion.11
  213.4 3.0 fusion.110
  219.4 3.1 fusion.111
  227.3 5.1 gather_fusion
  238.2 3.0 fusion.110
  244.2 3.1 fusion.111
  252.1 5.1 gather_fusion
  260.0 3.0 multiply_convert_fusion.11
  263.0 3.0 fusion.110
  269.0 3.1 fusion.111
  276.9 5.1 gather_fusion
  287.8 3.0 fusion.110
  293.8 3.1 fusion.111
  301.7 5.1 gather_fusion
  309.6 3.0 multiply_convert_fusion.11
  312.6 3.0 fusion.110
  318.6 3.1 fusion.111
  326.5 5.1 gather_fusion
  337.4 3.0 fusion.110
  343.4 3.1 fusion.111
  351.3 5.1 gather_fusion
  359.2 3.0 multiply_convert_fusion.11
  362.2 3.0 fusion.110
  368.2 3.1 fusion.111
  376.1 5.1 gather_fusion
  387.0 3.0 fusion.110
  393.0 3.1 fusion.111
  400.9 5.1 gather_fusion
  408.8 3.0 multiply_convert_fusion.11
  411.8 3.0 fusion.110
  417.8 3.1 fusion.111
  425.7 5.1 gather_fusion
  436.6 3.0 fusion.110
  442.6 3.1 fusion.111
  449.2 126.2 %reduce-scatter.2.cloned.1.call-done = f32[66,128]{1,0:T(8,128)} async-done(((f32[66,2048]{1,0:T(8,128)}), f32[66,128]{1,0:T(8,128)}) %reduce-scatter.2.cloned.1.call-update) | async-done | bytes 33808 | tf_op jit(solution)/shard_map/reduce_scatter | solution.py:132
  (323 shorter events, 153.4 us)
Async XLA Ops:
  6.5 142.6 %copy-start = (f32[16,256]{1,0:T(8,128)S(1)}, f32[16,256]{1,0:T(8,128)}, u32[]{:S(2)}) copy-start(f32[16,256]{1,0:T(8,128)} %param.13) | copy-start | bytes 49156
  6.5 568.9 %reduce-scatter.2.cloned.1.call-start = ((), (), s32[]{:S(2)}) async-start(), calls=%async_computation.1 | async-start | bytes 626688 | tf_op jit(solution)/shard_map/reduce_scatter | solution.py:132
  14.6 7.8 %collective-permute-start.6 = (bf16[1,66,8,4096]{3,2,1,0:T(8,128)(2,1)}, bf16[1,66,8,4096]{3,2,1,0:T(8,128)(2,1)}, u32[]{:S(2)}, u32[]{:S(2)}) collective-permute-start(bf16[1,66,8,4096]{3,2,1,0:T(8,128)(2,1)} %get-tuple-element.265), channel_id=1, source_target_pairs={{0,1},{1,0},{2,3},{3,2},{4,5},{5,4},{6,7},{7,6},{8,9},{9,8},{10,11... | collective-permute-start | bytes 12976136 | tf_op jit(solution)/shard_map/ppermute | solution.py:12
  22.4 14.8 %copy-start.7 = (s32[66]{0:T(128)S(1)}, s32[66]{0:T(128)}, u32[]{:S(2)}) copy-start(s32[66]{0:T(128)} %param.15) | copy-start | bytes 796
  22.4 15.3 %copy-start.8 = (s32[66]{0:T(128)S(1)}, s32[66]{0:T(128)}, u32[]{:S(2)}) copy-start(s32[66]{0:T(128)} %param.16) | copy-start | bytes 796
  22.4 16.1 %copy-start.4 = (bf16[66,4096]{1,0:T(8,128)(2,1)S(1)}, bf16[66,4096]{1,0:T(8,128)(2,1)}, u32[]{:S(2)}) copy-start(bf16[66,4096]{1,0:T(8,128)(2,1)} %param.11) | copy-start | bytes 1622020
  22.4 16.8 %copy-start.6 = (s32[16,256]{1,0:T(8,128)S(1)}, s32[16,256]{1,0:T(8,128)}, u32[]{:S(2)}) copy-start(s32[16,256]{1,0:T(8,128)} %param.12) | copy-start | bytes 49156
  34.3 128.9 %collective-permute-start.7 = (bf16[2,66,4,4096]{3,2,1,0:T(4,128)(2,1)}, bf16[2,66,4,4096]{3,2,1,0:T(4,128)(2,1)}, u32[]{:S(2)}, u32[]{:S(2)}) collective-permute-start(bf16[2,66,4,4096]{3,2,1,0:T(4,128)(2,1)} %get-tuple-element.264), channel_id=1, source_target_pairs={{0,2},{1,3},{2,0},{3,1},{4,6},{5,7},{6,4},{7,5},{8,10},{9,11},{10,... | collective-permute-start | bytes 12976136 | tf_op jit(solution)/shard_map/ppermute | solution.py:12
  37.2 112.0 %collective-permute-start = (s32[1]{0:T(128)}, s32[1]{0:T(128)}, u32[]{:S(2)}, u32[]{:S(2)}) collective-permute-start(s32[1]{0:T(128)} %param.17), channel_id=1, source_target_pairs={{0,1},{1,0},{2,3},{3,2},{4,5},{5,4},{6,7},{7,6},{8,9},{9,8},{10,11... | collective-permute-start | bytes 20 | tf_op jit(solution)/shard_map/ppermute | solution.py:12
  37.2 118.4 %collective-permute-start.2 = (s32[1,66]{1,0:T(1,128)S(1)}, s32[1,66]{1,0:T(1,128)S(1)}, u32[]{:S(2)}, u32[]{:S(2)}) collective-permute-start(s32[1,66]{1,0:T(1,128)S(1)} %bitcast.120), channel_id=1, source_target_pairs={{0,1},{1,0},{2,3},{3,2},{4,5},{5,4},{6,7},{7,6},{8,9},{9,8},{10,11... | collective-permute-start | bytes 800 | tf_op jit(solution)/shard_map/ppermute | solution.py:12
  37.7 117.9 %collective-permute-start.4 = (s32[1,66]{1,0:T(1,128)S(1)}, s32[1,66]{1,0:T(1,128)S(1)}, u32[]{:S(2)}, u32[]{:S(2)}) collective-permute-start(s32[1,66]{1,0:T(1,128)S(1)} %bitcast.123), channel_id=1, source_target_pairs={{0,1},{1,0},{2,3},{3,2},{4,5},{5,4},{6,7},{7,6},{8,9},{9,8},{10,11... | collective-permute-start | bytes 800 | tf_op jit(solution)/shard_map/ppermute | solution.py:12
  39.2 12.4 %copy-start.5 = (bf16[66,128]{1,0:T(8,128)(2,1)S(1)}, bf16[66,128]{1,0:T(8,128)(2,1)}, u32[]{:S(2)}) copy-start(bf16[66,128]{1,0:T(8,128)(2,1)} %param.10) | copy-start | bytes 50692
  149.9 3.5 collective-permute-start.1
  155.7 5.9 %collective-permute-start.3 = (s32[2,66]{1,0:T(2,128)S(1)}, s32[2,66]{1,0:T(2,128)S(1)}, u32[]{:S(2)}, u32[]{:S(2)}) collective-permute-start(s32[2,66]{1,0:T(2,128)S(1)} %get-tuple-element.267), channel_id=1, source_target_pairs={{0,2},{1,3},{2,0},{3,1},{4,6},{5,7},{6,4},{7,5},{8,10},{9,11},{10,... | collective-permute-start | bytes 1592 | tf_op jit(solution)/shard_map/ppermute | solution.py:12
  159.6 3.6 collective-permute-start.5
  172.9 4.0 copy-start.1
  191.6 3.0 copy-start.3
  193.7 3.9 copy-start.2
  197.7 4.0 copy-start.1
  216.4 3.0 copy-start.3
  218.5 3.9 copy-start.2
  222.5 4.0 copy-start.1
  241.2 3.0 copy-start.3
  243.3 3.9 copy-start.2
  247.3 4.0 copy-start.1
  266.0 3.0 copy-start.3
  268.1 3.9 copy-start.2
  272.1 4.0 copy-start.1
  290.8 3.0 copy-start.3
  292.9 3.9 copy-start.2
  296.9 4.0 copy-start.1
  315.6 3.0 copy-start.3
  317.7 3.9 copy-start.2
  321.7 4.0 copy-start.1
  340.4 3.0 copy-start.3
  342.5 3.9 copy-start.2
  346.5 4.0 copy-start.1
  365.2 3.0 copy-start.3
  367.3 3.9 copy-start.2
  371.3 4.0 copy-start.1
  390.0 3.0 copy-start.3
  392.1 3.9 copy-start.2
  396.1 4.0 copy-start.1
  414.8 3.0 copy-start.3
  416.9 3.9 copy-start.2
  420.9 4.0 copy-start.1
  439.6 3.0 copy-start.3
  441.7 3.9 copy-start.2
Sparse Core Ops, SparseCore 0:
  449.3 126.0 reduce-scatter.1
where the time goes:
time: 587 us; the launch traced here: 584 us
  matrix products  150 us (26%)
  waiting for transfers between devices  139 us (24%)
  local copies, waits for them, and re-layouts  138 us (24%)
  blocking collectives  95.9 us (16%)
  other arithmetic  39.6 us (7%)
  between operations  14.9 us (3%)
  starting transfers between devices  6 us (1%)
    reduce_scatter x1, waiting for transfers between devices, on_device(): lax.psum_scatter(partial_grad, 'tile', scatter_dimension=1, tiled=True)  126 us
    all_gather x1, blocking collectives, on_device(): everything = lax.all_gather(coefficients, 'tile', axis=1, tiled=True)  95.9 us
    gather x11, local copies, waits for them, and re-layouts, one_group(): flat_vis[picks].reshape(group, width_part, BLK, BLK).astype(jnp.float32)  56.2 us
    dot_general x11, matrix products, one_group(): jnp.einsum('gn,gki->kni', right_hot.astype(jnp.float32), right_terms, pre...  33.6 us
    dot_general x11, matrix products, one_group(): jnp.einsum('gfjs,kfs->gkj', col_grad, chosen, preferred_element_type=jnp....  32.6 us
    dot_general x11, matrix products, one_group(): jnp.einsum('gfis,gfjs->gfij', left_weighted, right_beams, preferred_eleme...  32.5 us
    convert_element_type x11, local copies, waits for them, and re-layouts, one_group(): flat_vis[picks].reshape(group, width_part, BLK, BLK).astype(jnp.float32)  30.8 us
    dot_general x11, matrix products, one_group(): jnp.einsum('gfis,kfs->gki', row_grad, chosen, preferred_element_type=jnp....  23.9 us
  transfers between devices with their start and end apart: 9, of which 4 were waited for; matrix products, arithmetic and copies ran while one was open for 4% of the time, Pallas kernels for 0%

commit v1 on v0

v1 whole, which is shorter than its diff:
```python
import functools
import math

import jax
import jax.numpy as jnp
from jax import lax
from jax.experimental import pallas as pl
from jax.experimental.pallas import tpu as pltpu
from jax.sharding import PartitionSpec as P

BLK = 64
LANES = 128
PIXELS = 256
BF = jnp.bfloat16
F32 = jnp.float32
NT = (((1,), (1,)), ((), ()))


def up(size, unit):
    return -(-size // unit) * unit


def low_lanes(rows):
    return lax.broadcasted_iota(jnp.int32, (rows, LANES), 1) < BLK


def gram_kernel(root, table_ref, pos_ref, flux_ref, out_ref, groups, gram):
    terms, pixels = table_ref.shape
    channels, sources = pos_ref.shape
    n_groups = pixels // PIXELS
    tall = groups.shape[0] // n_groups
    rows = up(terms, 8)
    groups[...] = jnp.zeros_like(groups)
    gram[...] = jnp.zeros_like(gram)
    for h in range(n_groups):
        groups[h * tall : h * tall + terms, :] = table_ref[:, h * PIXELS : (h + 1) * PIXELS]
    pixel = lax.broadcasted_iota(jnp.int32, (PIXELS, sources), 0)
    for f in range(channels):
        pos = pos_ref[f : f + 1, :]
        hot = jnp.where(pixel == pos % PIXELS, 1.0, 0.0).astype(BF)
        found = jnp.dot(groups[...], hot, preferred_element_type=F32)
        group = pos // PIXELS
        chosen = jnp.zeros((tall, sources), F32)
        for h in range(n_groups):
            chosen = jnp.where(group == h, found[h * tall : (h + 1) * tall], chosen)
        scaled = chosen * (flux_ref[f : f + 1, :] / root)
        high = scaled.astype(BF)
        low = (scaled - high.astype(F32)).astype(BF)
        chosen = chosen.astype(BF)
        product = lax.dot_general(high, chosen, NT, preferred_element_type=F32)
        product = product + lax.dot_general(low, chosen, NT, preferred_element_type=F32)
        gram[f * rows : f * rows + tall, 0:tall] = product
    value = gram[...]
    high = value.astype(BF)
    out_ref[:, 0:LANES] = high
    out_ref[:, LANES : 2 * LANES] = (value - high.astype(F32)).astype(BF)


def gram_of(zernike_table, positions, source_flux):
    terms, pixels = zernike_table.shape
    channels, sources = positions.shape
    rows, tall = up(terms, 8), up(terms, 16)
    height = up(channels * rows + 8, 16)
    return pl.pallas_call(
        functools.partial(gram_kernel, math.sqrt(sources)),
        out_shape=jax.ShapeDtypeStruct((height, 2 * LANES), BF),
        in_specs=[pl.BlockSpec(memory_space=pltpu.VMEM)] * 3,
        out_specs=pl.BlockSpec(memory_space=pltpu.VMEM),
        scratch_shapes=[
            pltpu.VMEM((pixels // PIXELS * tall, PIXELS), BF),
            pltpu.VMEM((height, LANES), F32),
        ],
        compiler_params=pltpu.CompilerParams(vmem_limit_bytes=32 << 20),
        cost_estimate=pl.CostEstimate(
            flops=2 * channels * sources * pixels * terms, bytes_accessed=1 << 20, transcendentals=0
        ),
    )(zernike_table, positions, source_flux)


def reverse_bits(value, bits):
    result = value & 0
    for bit in range(bits):
        result = result | ((value >> bit) & 1) << (bits - 1 - bit)
    return result


def tiles_kernel(
    relative_bits, unroll, scale,
    count_ref, rows_ref, cols_ref, own_ref, got_ref, gram_ref, vis_hbm,
    keep_ref, send_ref,
    vis, stage, spread, plain, mixed, turned, right, left, row_sum, col_sum, sems,
):
    slots, channels = vis.shape[0], vis.shape[1]
    half, terms = own_ref.shape[0], own_ref.shape[1]
    pairs = channels // 2
    rows, tall = up(terms, 8), up(terms, 16)
    count = count_ref[0]
    n_groups = (count + unroll - 1) // unroll

    def fetch(slot):
        return pltpu.make_async_copy(vis_hbm.at[slot], vis.at[slot], sems.at[slot])

    @pl.loop(0, n_groups * unroll)
    def _(slot):
        fetch(slot).start()

    row_sum[...] = jnp.zeros_like(row_sum)
    col_sum[...] = jnp.zeros_like(col_sum)
    plain[...] = jnp.zeros_like(plain)
    spread[...] = jnp.zeros_like(spread)

    for part, ref in enumerate((own_ref, got_ref)):
        for r in range(half):
            where = part * half + r
            chunk, lanes = where // 2, slice(where % 2 * LANES, (where % 2 + 1) * LANES)
            block = ref[r]
            plain[chunk, 0:terms, lanes] = block
            plain[chunk, LANES : LANES + terms, lanes] = block
            buf = where % 2
            spread[buf, 0:terms, :] = block.astype(F32)
            stage[buf, 0:LANES, :] = spread[buf].T
            pieces = [stage[buf, pl.ds(start, BLK // 2, stride=2), :] for start in (0, 1, BLK, BLK + 1)]
            sorted_rows = jnp.concatenate(pieces, 0)
            turned[2 * where] = sorted_rows[0:BLK].astype(BF)
            turned[2 * where + 1] = sorted_rows[BLK:].astype(BF)
            back = sorted_rows.T.astype(BF)
            mixed[chunk, 0:LANES, lanes] = back
            mixed[chunk, LANES:, lanes] = back

    low_r = low_lanes(tall)
    low_l = low_lanes(2 * rows)

    @pl.loop(0, half)
    def _(chunk):
        weights = plain[chunk]
        for p in range(pairs):
            found = jnp.dot(
                gram_ref[2 * rows * p : 2 * rows * p + 2 * rows + 16, :], weights, preferred_element_type=F32
            )
            for side in range(2):
                first = found[0:tall, side * LANES : (side + 1) * LANES]
                second = found[rows : rows + tall, side * LANES : (side + 1) * LANES]
                lanes = slice(p * LANES, (p + 1) * LANES)
                block = 4 * chunk + 2 * side
                right[block, :, lanes] = jnp.where(low_r, first, pltpu.roll(second, BLK, 1)).astype(BF)
                right[block + 1, :, lanes] = jnp.where(low_r, pltpu.roll(first, BLK, 1), second).astype(BF)
        weights = mixed[chunk]
        for p in range(0, pairs, 2):
            found = jnp.dot(gram_ref[2 * rows * p : 2 * rows * (p + 2), :], weights, preferred_element_type=F32)
            for side in range(2):
                first = found[0 : 2 * rows, side * LANES : (side + 1) * LANES]
                second = found[2 * rows :, side * LANES : (side + 1) * LANES]
                lanes = slice(p * BLK, p * BLK + LANES)
                block = 4 * chunk + 2 * side
                left[block, :, lanes] = jnp.where(low_l, first, pltpu.roll(second, BLK, 1)).astype(BF)
                left[block + 1, :, lanes] = jnp.where(low_l, pltpu.roll(first, BLK, 1), second).astype(BF)

    row_pos = lax.broadcasted_iota(jnp.int32, (BLK, LANES), 0)
    row_dish = row_pos % (BLK // 2) * 2 + row_pos // (BLK // 2)
    ahead = lax.broadcasted_iota(jnp.int32, (BLK, LANES), 1) % BLK - row_dish
    low = low_lanes(BLK // 2)
    here = lax.axis_index("tile") if relative_bits else 0

    def place(block):
        if not relative_bits:
            return block
        return 2 * reverse_bits((block >> 1) ^ here, relative_bits) + (block & 1)

    @pl.loop(0, n_groups)
    def _(group):
        added = []
        for u in range(unroll):
            slot = group * unroll + u
            row, col = rows_ref[slot], cols_ref[slot]
            a, b = place(row), place(col)
            least = jnp.where(slot < count, jnp.where(row == col, 0, -BLK), BLK)
            keep = ahead > least
            fetch(slot).wait()
            for c in range(BLK // 2):
                stage[u, c * channels : (c + 1) * channels, :] = vis[
                    slot, :, c * LANES : (c + 1) * LANES
                ].astype(F32)
            model = jnp.dot(turned[a][:, 0:tall], right[b], preferred_element_type=F32)
            residual = []
            for p in range(pairs):
                first = stage[u, pl.ds(2 * p, BLK // 2, stride=channels), :]
                second = stage[u, pl.ds(2 * p + 1, BLK // 2, stride=channels), :]
                seen = jnp.concatenate(
                    [
                        jnp.where(low, first, pltpu.roll(second, BLK, 1)),
                        jnp.where(low, pltpu.roll(first, BLK, 1), second),
                    ],
                    0,
                )
                difference = model[:, p * LANES : (p + 1) * LANES] - seen
                residual.append(jnp.where(keep, difference, 0.0).astype(BF))
            to_row = lax.dot_general(
                jnp.concatenate(residual, 1), right[b], NT, preferred_element_type=F32
            )
            to_col = jnp.dot(left[a], jnp.concatenate(residual, 0), preferred_element_type=F32)
            added.append((a, b, to_row, to_col))
        for a, b, to_row, to_col in added:
            row_sum[a, :, 0:tall] += to_row
            col_sum[b] += to_col

    low_out = low_lanes(rows)
    for where in range(2 * half):
        buf = where % 2
        for side in range(2):
            total = row_sum[2 * where + side]
            stage[buf, pl.ds(side * BLK, BLK // 2, stride=2), :] = total[0 : BLK // 2]
            stage[buf, pl.ds(side * BLK + 1, BLK // 2, stride=2), :] = total[BLK // 2 :]
        from_rows = stage[buf, 0:LANES, :].T[0:rows]
        cols = []
        for side in range(2):
            total = col_sum[2 * where + side]
            cols.append(total[0:rows] + pltpu.roll(total[rows:], BLK, 1))
        from_cols = jnp.where(low_out, cols[0], pltpu.roll(cols[1], BLK, 1))
        result = ((from_rows + from_cols) * scale)[0:terms]
        if where < half:
            keep_ref[where] = result
        else:
            send_ref[where - half] = result


def tile_terms(relative_bits, scale, tile_count, tile_rows, tile_cols, own, got, gram, observed):
    slots, channels, _ = observed.shape
    half, terms, _ = own.shape
    rows, tall = up(terms, 8), up(terms, 16)
    blocks = 4 * half
    unroll = next(u for u in (2, 3, 1) if slots % u == 0)
    smem = pl.BlockSpec(memory_space=pltpu.SMEM)
    vmem = pl.BlockSpec(memory_space=pltpu.VMEM)
    out = jax.ShapeDtypeStruct((half, terms, LANES), F32)
    return pl.pallas_call(
        functools.partial(tiles_kernel, relative_bits, unroll, scale),
        out_shape=(out, out),
        in_specs=[smem, smem, smem, vmem, vmem, vmem, pl.BlockSpec(memory_space=pl.ANY)],
        out_specs=(vmem, vmem),
        scratch_shapes=[
            pltpu.VMEM((slots, channels, BLK * BLK), BF),
            pltpu.VMEM((max(unroll, 2), channels * BLK // 2, LANES), F32),
            pltpu.VMEM((2, LANES, LANES), F32),
            pltpu.VMEM((half, 2 * LANES, 2 * LANES), BF),
            pltpu.VMEM((half, 2 * LANES, 2 * LANES), BF),
            pltpu.VMEM((blocks, BLK, LANES), BF),
            pltpu.VMEM((blocks, tall, channels * BLK), BF),
            pltpu.VMEM((blocks, 2 * rows, channels // 2 * BLK), BF),
            pltpu.VMEM((blocks, BLK, LANES), F32),
            pltpu.VMEM((blocks, 2 * rows, LANES), F32),
            pltpu.SemaphoreType.DMA((slots,)),
        ],
        compiler_params=pltpu.CompilerParams(vmem_limit_bytes=48 << 20),
        cost_estimate=pl.CostEstimate(
            flops=6 * slots * channels * BLK * BLK * terms, bytes_accessed=observed.size * 2, transcendentals=0
        ),
    )(tile_count, tile_rows, tile_cols, own, got, gram, observed)


def from_partner(array, bit):
    return lax.ppermute(array, "tile", [(i, i ^ 1 << bit) for i in range(lax.axis_size("tile"))])


def on_device(
    coefficients, zernike_table, positions, source_flux, observed, tile_rows, tile_cols, tile_count
):
    members = lax.axis_size("tile")
    terms, shard = coefficients.shape
    dishes = members * shard
    scale = 1.0 / math.sqrt(dishes * positions.shape[0])
    gram = gram_of(zernike_table, positions, source_flux)
    bits = members.bit_length() - 1
    if shard == LANES and members == 1 << bits:
        held = coefficients[None]
        for bit in reversed(range(1, bits)):
            held = jnp.concatenate([held, from_partner(held, bit)], 0)
        got = from_partner(held, 0)
        total, sent = tile_terms(
            bits, scale, tile_count, tile_rows, tile_cols, held, got, gram, observed
        )
        total = total + from_partner(sent, 0)
        for bit in range(1, bits):
            half = total.shape[0] // 2
            total = total[:half] + from_partner(total[half:], bit)
        return total[0]
    everything = lax.all_gather(coefficients, "tile", axis=1, tiled=True)
    everything = everything.reshape(terms, dishes // LANES, LANES).transpose(1, 0, 2)
    half = everything.shape[0] // 2
    parts = tile_terms(
        0, scale, tile_count, tile_rows, tile_cols, everything[:half], everything[half:], gram, observed
    )
    total = jnp.concatenate(parts, 0).transpose(1, 0, 2).reshape(terms, dishes)
    return lax.psum_scatter(total, "tile", scatter_dimension=1, tiled=True)


def solution(mesh):
    return jax.shard_map(
        on_device,
        mesh=mesh,
        in_specs=(
            P(None, "tile"),
            P(),
            P("scan", None),
            P("scan", None),
            P(("scan", "tile"), None, None),
            P(("scan", "tile")),
            P(("scan", "tile")),
            P(("scan", "tile")),
        ),
        out_specs=P("scan", "tile"),
        check_vma=False,
    )
```

time: 587 us -> 80 us (0.14)
  matrix products: 150 us -> 0 us
  local copies, waits for them, and re-layouts: 138 us -> 2.52 us
  waiting for transfers between devices: 139 us -> 18.9 us
  blocking collectives: 95.9 us -> 0 us
  other arithmetic: 39.6 us -> 2.89 us
  Pallas kernels: 0 us -> 29.2 us
  starting transfers between devices: 6 us -> 25.3 us
  between operations: 14.9 us -> 0.77 us
    dot_general x99 -> x0, matrix products: 150 us -> none  [the longest x11 33.6 us: one_group(): jnp.einsum('gn,gki->kni', right_hot.astype(jnp.float32), right_terms, pre...]
    reduce_scatter x1 -> x0, waiting for transfers between devices: 126 us -> none  [on_device(): lax.psum_scatter(partial_grad, 'tile', scatter_dimension=1, tiled=True)]
    all_gather x1 -> x0, blocking collectives: 95.9 us -> none  [on_device(): everything = lax.all_gather(coefficients, 'tile', axis=1, tiled=True)]
    gather x45 -> x0, local copies, waits for them, and re-layouts: 90.3 us -> none  [the longest x11 56.2 us: one_group(): flat_vis[picks].reshape(group, width_part, BLK, BLK).astype(jnp.float32)]
    convert_element_type x23 -> x0, local copies, waits for them, and re-layouts: 31.8 us -> none  [the longest x11 30.8 us: one_group(): flat_vis[picks].reshape(group, width_part, BLK, BLK).astype(jnp.float32)]
    pallas_call x0 -> x2, Pallas kernels: none -> 29.2 us  [the longest x1 21.9 us: tile_terms(): pl.pallas_call(functools.partial(tiles_kernel, relative_bits, unroll, sca...]
    concatenate x7 -> x3, other arithmetic: 21.8 us -> 2.2 us  [on_device(): held = jnp.concatenate([held, from_partner(held, bit)], 0)]
    ppermute x8, starting transfers between devices: 6 us -> 25.3 us  [from_partner(): lax.ppermute(array, 'tile', [(i, i ^ 1 << bit) for i in range(lax.axis_si...]
  transfers between devices with their start and end apart: 9 -> 8, of which waited for: 4 -> 7; matrix products, arithmetic and copies ran while one was open for 4% -> 0% of each run, Pallas kernels for 0% -> 9%
where the time goes in v1:
time: 80 us; the launch traced here: 79.5 us
  Pallas kernels  29.2 us (36%)
  starting transfers between devices  25.3 us (32%)
  waiting for transfers between devices  18.9 us (24%)
  other arithmetic  2.89 us (4%)
  local copies, waits for them, and re-layouts  2.52 us (3%)
    ppermute x8, starting transfers between devices, from_partner(): lax.ppermute(array, 'tile', [(i, i ^ 1 << bit) for i in range(lax.axis_si...  25.3 us
    pallas_call x1, Pallas kernels, tile_terms(): pl.pallas_call(functools.partial(tiles_kernel, relative_bits, unroll, sca...  21.9 us
    ppermute x8, waiting for transfers between devices, from_partner(): lax.ppermute(array, 'tile', [(i, i ^ 1 << bit) for i in range(lax.axis_si...  18.9 us
    pallas_call x1, Pallas kernels, gram_of(): pl.pallas_call(functools.partial(gram_kernel, math.sqrt(sources)), out_sh...  7.32 us
    unnamed x10, local copies, waits for them, and re-layouts  2.5 us
    concatenate x3, other arithmetic, on_device(): held = jnp.concatenate([held, from_partner(held, bit)], 0)  2.2 us
  transfers between devices with their start and end apart: 8, of which 7 were waited for; matrix products, arithmetic and copies ran while one was open for 0% of the time, Pallas kernels for 9%

profile of v1, /device:TPU:0, one launch (start us, length us, event | category | flops | bytes accessed | tf_op | source)
XLA Modules:
  0.0 79.5 jit_solution(13129813407815023451)
XLA Ops:
  0.0 0.0 copy-start.1
  0.0 0.0 copy-start
  0.0 4.0 %collective-permute-start = (bf16[1,66,128]{2,1,0:T(8,128)(2,1)}, bf16[1,66,128]{2,1,0:T(8,128)(2,1)S(1)}, u32[]{:S(2)}, u32[]{:S(2)}) collective-permute-start(bf16[1,66,128]{2,1,0:T(8,128)(2,1)} %bitcast.3), channel_id=1, source_target_pairs={{0,8},{1,9},{2,10},{3,11},{4,12},{5,13},{6,14},{7,15},{8,0},{9,1},... | collective-permute-start | bytes 50696 | tf_op jit(solution)/shard_map/ppermute | solution.py:261
  4.0 1.9 %collective-permute-done = bf16[1,66,128]{2,1,0:T(8,128)(2,1)S(1)} collective-permute-done((bf16[1,66,128]{2,1,0:T(8,128)(2,1)}, bf16[1,66,128]{2,1,0:T(8,128)(2,1)S(1)}, u32[]{:S(2)}, u32[]{:S(2)}) %collective-permute-start) | collective-permute-done | bytes 16928 | tf_op jit(solution)/shard_map/ppermute | solution.py:261
  6.0 0.7 pad_maximum_fusion.2
  6.7 1.9 %collective-permute-start.1 = (bf16[2,66,128]{2,1,0:T(8,128)(2,1)S(1)}, bf16[2,66,128]{2,1,0:T(8,128)(2,1)S(1)}, u32[]{:S(2)}, u32[]{:S(2)}) collective-permute-start(bf16[2,66,128]{2,1,0:T(8,128)(2,1)S(1)} %pad_maximum_fusion.2), channel_id=1, source_target_pairs={{0,4},{1,5},{2,6},{3,7},{4,0},{5,1},{6,2},{7,3},{8,12},{9,13},{10,... | collective-permute-start | bytes 101384 | tf_op jit(solution)/shard_map/ppermute | solution.py:261
  8.6 2.0 %collective-permute-done.1 = bf16[2,66,128]{2,1,0:T(8,128)(2,1)S(1)} collective-permute-done((bf16[2,66,128]{2,1,0:T(8,128)(2,1)S(1)}, bf16[2,66,128]{2,1,0:T(8,128)(2,1)S(1)}, u32[]{:S(2)}, u32[]{:S(2)}) %collective-permute-start.1) | collective-permute-done | bytes 33824 | tf_op jit(solution)/shard_map/ppermute | solution.py:261
  10.7 0.7 pad_maximum_fusion.1
  11.4 2.0 %collective-permute-start.2 = (bf16[4,66,128]{2,1,0:T(8,128)(2,1)S(1)}, bf16[4,66,128]{2,1,0:T(8,128)(2,1)S(1)}, u32[]{:S(2)}, u32[]{:S(2)}) collective-permute-start(bf16[4,66,128]{2,1,0:T(8,128)(2,1)S(1)} %pad_maximum_fusion.1), channel_id=1, source_target_pairs={{0,2},{1,3},{2,0},{3,1},{4,6},{5,7},{6,4},{7,5},{8,10},{9,11},{10,... | collective-permute-start | bytes 202760 | tf_op jit(solution)/shard_map/ppermute | solution.py:261
  14.1 1.8 %collective-permute-done.2 = bf16[4,66,128]{2,1,0:T(8,128)(2,1)S(1)} collective-permute-done((bf16[4,66,128]{2,1,0:T(8,128)(2,1)S(1)}, bf16[4,66,128]{2,1,0:T(8,128)(2,1)S(1)}, u32[]{:S(2)}, u32[]{:S(2)}) %collective-permute-start.2) | collective-permute-done | bytes 67616 | tf_op jit(solution)/shard_map/ppermute | solution.py:261
  15.8 0.7 pad_maximum_fusion.own_ref
  16.6 0.1 collective-permute-start.3
  16.7 0.0 copy-start.2
  16.7 1.1 %copy-done.2 = bf16[66,4096]{1,0:T(8,128)(2,1)S(1)} copy-done((bf16[66,4096]{1,0:T(8,128)(2,1)S(1)}, bf16[66,4096]{1,0:T(8,128)(2,1)}, u32[]{:S(2)}) %copy-start.2) | copy-done | bytes 540696
  17.7 0.0 copy-start.3
  17.7 0.7 copy-done.3
  18.4 0.0 copy-start.4
  18.4 0.7 copy-done.4
  19.2 7.3 %shard_map.82.gram_ref = bf16[1168,256]{1,0:T(8,128)(2,1)S(1)} custom-call(bf16[66,4096]{1,0:T(8,128)(2,1)S(1)} %copy-done.2, s32[16,256]{1,0:T(8,128)S(1)} %copy-done.3, f32[16,256]{1,0:T(8,128)S(1)} %copy-done.4), custom_call_target="tpu_custom_call" | custom-call | flops 2214592512 | bytes 1048576 | tf_op jit(solution)/shard_map/pallas_call | solution.py:64
  26.5 0.0 collective-permute-done.3.got_ref
  26.5 0.0 copy-done.1
  26.5 0.0 copy-done
  26.5 21.9 %shard_map.83 = (f32[8,66,128]{2,1,0:T(8,128)S(1)}, f32[8,66,128]{2,1,0:T(8,128)S(1)}) custom-call(s32[1]{0:T(128)S(6)} %copy.9.count_ref, s32[66]{0:T(128)S(1)} %copy-done, s32[66]{0:T(128)S(1)} %copy-done.1, bf16[8,66,128]{2,1,0:T(8,128)(2,1)S(1)} %pad_maximum_fusion.own_ref, bf16[8,66,128]{2,1,0:T(8,128)(2,1)S(1)} %collective-permute-done.3.got_ref, ...), custom_call_target="tpu_custom_call" | custom-call | flops 1712848896 | bytes 8650752 | tf_op jit(solution)/shard_map/pallas_call | solution.py:235
  48.4 0.1 collective-permute-start.4
  48.5 1.6 %collective-permute-done.4 = f32[8,66,128]{2,1,0:T(8,128)S(1)} collective-permute-done((f32[8,66,128]{2,1,0:T(8,128)S(1)}, f32[8,66,128]{2,1,0:T(8,128)S(1)}, u32[]{:S(2)}, u32[]{:S(2)}) %collective-permute-start.4) | collective-permute-done | bytes 270368 | tf_op jit(solution)/shard_map/ppermute | solution.py:261
  50.1 2.1 %collective-permute-start.5 = (f32[4,66,128]{2,1,0:T(8,128)S(1)}, f32[4,66,128]{2,1,0:T(8,128)S(1)}, u32[]{:S(2)}, u32[]{:S(2)}) collective-permute-start(f32[4,66,128]{2,1,0:T(8,128)S(1)} %slice.25), channel_id=1, source_target_pairs={{0,2},{1,3},{2,0},{3,1},{4,6},{5,7},{6,4},{7,5},{8,10},{9,11},{10,... | collective-permute-start | bytes 405512 | tf_op jit(solution)/shard_map/ppermute | solution.py:261
  52.2 4.4 %collective-permute-done.5 = f32[4,66,128]{2,1,0:T(8,128)S(1)} collective-permute-done((f32[4,66,128]{2,1,0:T(8,128)S(1)}, f32[4,66,128]{2,1,0:T(8,128)S(1)}, u32[]{:S(2)}, u32[]{:S(2)}) %collective-permute-start.5) | collective-permute-done | bytes 135200 | tf_op jit(solution)/shard_map/ppermute | solution.py:261
  56.6 15.0 %collective-permute-start.6 = (f32[2,66,128]{2,1,0:T(8,128)S(1)}, f32[2,66,128]{2,1,0:T(8,128)S(1)}, u32[]{:S(2)}, u32[]{:S(2)}) collective-permute-start(f32[2,66,128]{2,1,0:T(8,128)S(1)} %slice.27), channel_id=1, source_target_pairs={{0,4},{1,5},{2,6},{3,7},{4,0},{5,1},{6,2},{7,3},{8,12},{9,13},{10,... | collective-permute-start | bytes 202760 | tf_op jit(solution)/shard_map/ppermute | solution.py:261
  71.6 2.3 %collective-permute-done.6 = f32[2,66,128]{2,1,0:T(8,128)S(1)} collective-permute-done((f32[2,66,128]{2,1,0:T(8,128)S(1)}, f32[2,66,128]{2,1,0:T(8,128)S(1)}, u32[]{:S(2)}, u32[]{:S(2)}) %collective-permute-start.6) | collective-permute-done | bytes 67616 | tf_op jit(solution)/shard_map/ppermute | solution.py:261
  74.0 0.1 collective-permute-start.7
  74.1 4.8 %collective-permute-done.7 = f32[1,66,128]{2,1,0:T(8,128)S(1)} collective-permute-done((f32[1,66,128]{2,1,0:T(8,128)S(1)}, f32[1,66,128]{2,1,0:T(8,128)S(1)}, u32[]{:S(2)}, u32[]{:S(2)}) %collective-permute-start.7) | collective-permute-done | bytes 33824 | tf_op jit(solution)/shard_map/ppermute | solution.py:261
  78.9 0.6 fusion
  (6 shorter events, 0.1 us)
Async XLA Ops:
  0.0 26.5 %copy-start.1 = (s32[66]{0:T(128)S(1)}, s32[66]{0:T(128)}, u32[]{:S(2)}) copy-start(s32[66]{0:T(128)} %cols_ref.1) | copy-start | bytes 796
  0.0 26.5 %copy-start = (s32[66]{0:T(128)S(1)}, s32[66]{0:T(128)}, u32[]{:S(2)}) copy-start(s32[66]{0:T(128)} %rows_ref.1) | copy-start | bytes 796
  0.0 6.0 %collective-permute-start = (bf16[1,66,128]{2,1,0:T(8,128)(2,1)}, bf16[1,66,128]{2,1,0:T(8,128)(2,1)S(1)}, u32[]{:S(2)}, u32[]{:S(2)}) collective-permute-start(bf16[1,66,128]{2,1,0:T(8,128)(2,1)} %bitcast.3), channel_id=1, source_target_pairs={{0,8},{1,9},{2,10},{3,11},{4,12},{5,13},{6,14},{7,15},{8,0},{9,1},... | collective-permute-start | bytes 50696 | tf_op jit(solution)/shard_map/ppermute | solution.py:261
  6.7 4.0 %collective-permute-start.1 = (bf16[2,66,128]{2,1,0:T(8,128)(2,1)S(1)}, bf16[2,66,128]{2,1,0:T(8,128)(2,1)S(1)}, u32[]{:S(2)}, u32[]{:S(2)}) collective-permute-start(bf16[2,66,128]{2,1,0:T(8,128)(2,1)S(1)} %pad_maximum_fusion.2), channel_id=1, source_target_pairs={{0,4},{1,5},{2,6},{3,7},{4,0},{5,1},{6,2},{7,3},{8,12},{9,13},{10,... | collective-permute-start | bytes 101384 | tf_op jit(solution)/shard_map/ppermute | solution.py:261
  11.4 4.4 %collective-permute-start.2 = (bf16[4,66,128]{2,1,0:T(8,128)(2,1)S(1)}, bf16[4,66,128]{2,1,0:T(8,128)(2,1)S(1)}, u32[]{:S(2)}, u32[]{:S(2)}) collective-permute-start(bf16[4,66,128]{2,1,0:T(8,128)(2,1)S(1)} %pad_maximum_fusion.1), channel_id=1, source_target_pairs={{0,2},{1,3},{2,0},{3,1},{4,6},{5,7},{6,4},{7,5},{8,10},{9,11},{10,... | collective-permute-start | bytes 202760 | tf_op jit(solution)/shard_map/ppermute | solution.py:261
  16.6 9.9 %collective-permute-start.3 = (bf16[8,66,128]{2,1,0:T(8,128)(2,1)S(1)}, bf16[8,66,128]{2,1,0:T(8,128)(2,1)S(1)}, u32[]{:S(2)}, u32[]{:S(2)}) collective-permute-start(bf16[8,66,128]{2,1,0:T(8,128)(2,1)S(1)} %pad_maximum_fusion.own_ref), channel_id=1, source_target_pairs={{0,1},{1,0},{2,3},{3,2},{4,5},{5,4},{6,7},{7,6},{8,9},{9,8},{10,11... | collective-permute-start | bytes 405512 | tf_op jit(solution)/shard_map/ppermute | solution.py:261
  16.7 1.1 %copy-start.2 = (bf16[66,4096]{1,0:T(8,128)(2,1)S(1)}, bf16[66,4096]{1,0:T(8,128)(2,1)}, u32[]{:S(2)}) copy-start(bf16[66,4096]{1,0:T(8,128)(2,1)} %table_ref.1) | copy-start | bytes 1622020
  17.7 0.7 copy-start.3
  18.4 0.7 copy-start.4
  48.4 1.6 %collective-permute-start.4 = (f32[8,66,128]{2,1,0:T(8,128)S(1)}, f32[8,66,128]{2,1,0:T(8,128)S(1)}, u32[]{:S(2)}, u32[]{:S(2)}) collective-permute-start(f32[8,66,128]{2,1,0:T(8,128)S(1)} %get-tuple-element.8), channel_id=1, source_target_pairs={{0,1},{1,0},{2,3},{3,2},{4,5},{5,4},{6,7},{7,6},{8,9},{9,8},{10,11... | collective-permute-start | bytes 811016 | tf_op jit(solution)/shard_map/ppermute | solution.py:261
  50.1 6.5 %collective-permute-start.5 = (f32[4,66,128]{2,1,0:T(8,128)S(1)}, f32[4,66,128]{2,1,0:T(8,128)S(1)}, u32[]{:S(2)}, u32[]{:S(2)}) collective-permute-start(f32[4,66,128]{2,1,0:T(8,128)S(1)} %slice.25), channel_id=1, source_target_pairs={{0,2},{1,3},{2,0},{3,1},{4,6},{5,7},{6,4},{7,5},{8,10},{9,11},{10,... | collective-permute-start | bytes 405512 | tf_op jit(solution)/shard_map/ppermute | solution.py:261
  56.6 17.3 %collective-permute-start.6 = (f32[2,66,128]{2,1,0:T(8,128)S(1)}, f32[2,66,128]{2,1,0:T(8,128)S(1)}, u32[]{:S(2)}, u32[]{:S(2)}) collective-permute-start(f32[2,66,128]{2,1,0:T(8,128)S(1)} %slice.27), channel_id=1, source_target_pairs={{0,4},{1,5},{2,6},{3,7},{4,0},{5,1},{6,2},{7,3},{8,12},{9,13},{10,... | collective-permute-start | bytes 202760 | tf_op jit(solution)/shard_map/ppermute | solution.py:261
  74.0 4.9 %collective-permute-start.7 = (f32[1,66,128]{2,1,0:T(8,128)S(1)}, f32[1,66,128]{2,1,0:T(8,128)S(1)}, u32[]{:S(2)}, u32[]{:S(2)}) collective-permute-start(f32[1,66,128]{2,1,0:T(8,128)S(1)} %slice.29), channel_id=1, source_target_pairs={{0,8},{1,9},{2,10},{3,11},{4,12},{5,13},{6,14},{7,15},{8,0},{9,1},... | collective-permute-start | bytes 101384 | tf_op jit(solution)/shard_map/ppermute | solution.py:261

commit v2 on v1

v2 whole, which is shorter than its diff:
```python
import functools
import math

import jax
import jax.numpy as jnp
from jax import lax
from jax.experimental import pallas as pl
from jax.experimental.pallas import tpu as pltpu
from jax.sharding import PartitionSpec as P

BLK = 64
UNROLL = 7
LANES = 128
PIXELS = 256
BF = jnp.bfloat16
F32 = jnp.float32
NT = (((1,), (1,)), ((), ()))


def up(size, unit):
    return -(-size // unit) * unit


def low_lanes(rows):
    return lax.broadcasted_iota(jnp.int32, (rows, LANES), 1) < BLK


def gram_kernel(root, start, count, table_ref, pos_ref, flux_ref, out_ref, groups, gram):
    terms, pixels = table_ref.shape
    sources = pos_ref.shape[1]
    n_groups = pixels // PIXELS
    tall = groups.shape[0] // n_groups
    rows = up(terms, 8)
    groups[...] = jnp.zeros_like(groups)
    gram[...] = jnp.zeros_like(gram)
    for h in range(n_groups):
        groups[h * tall : h * tall + terms, :] = table_ref[:, h * PIXELS : (h + 1) * PIXELS]
    pixel = lax.broadcasted_iota(jnp.int32, (PIXELS, sources), 0)
    for f in range(count):
        pos = pos_ref[start + f : start + f + 1, :]
        hot = jnp.where(pixel == pos % PIXELS, 1.0, 0.0).astype(BF)
        found = jnp.dot(groups[...], hot, preferred_element_type=F32)
        group = pos // PIXELS
        chosen = jnp.zeros((tall, sources), F32)
        for h in range(n_groups):
            chosen = jnp.where(group == h, found[h * tall : (h + 1) * tall], chosen)
        scaled = chosen * (flux_ref[start + f : start + f + 1, :] / root)
        high = scaled.astype(BF)
        low = (scaled - high.astype(F32)).astype(BF)
        chosen = chosen.astype(BF)
        product = lax.dot_general(high, chosen, NT, preferred_element_type=F32)
        product = product + lax.dot_general(low, chosen, NT, preferred_element_type=F32)
        gram[f * rows : f * rows + tall, 0:tall] = product
    value = gram[...]
    high = value.astype(BF)
    out_ref[:, 0:LANES] = high
    out_ref[:, LANES : 2 * LANES] = (value - high.astype(F32)).astype(BF)


def gram_of(zernike_table, positions, source_flux, start, count):
    terms, pixels = zernike_table.shape
    sources = positions.shape[1]
    rows, tall = up(terms, 8), up(terms, 16)
    height = up(count * rows + 8, 16)
    return pl.pallas_call(
        functools.partial(gram_kernel, math.sqrt(sources), start, count),
        out_shape=jax.ShapeDtypeStruct((height, 2 * LANES), BF),
        in_specs=[pl.BlockSpec(memory_space=pltpu.VMEM)] * 3,
        out_specs=pl.BlockSpec(memory_space=pltpu.VMEM),
        scratch_shapes=[
            pltpu.VMEM((pixels // PIXELS * tall, PIXELS), BF),
            pltpu.VMEM((height, LANES), F32),
        ],
        compiler_params=pltpu.CompilerParams(vmem_limit_bytes=32 << 20),
        cost_estimate=pl.CostEstimate(
            flops=2 * count * sources * pixels * terms, bytes_accessed=1 << 20, transcendentals=0
        ),
    )(zernike_table, positions, source_flux)


def reverse_bits(value, bits):
    result = value & 0
    for bit in range(bits):
        result = result | ((value >> bit) & 1) << (bits - 1 - bit)
    return result


def tiles_kernel(
    relative_bits, unroll, scale,
    mine_ref, other_ref, own_ref, got_ref, first_gram_ref, second_gram_ref, vis_hbm, more_hbm,
    keep_ref, send_ref,
    vis, stage, spread, both, turned, right, left, row_sum, col_sum, sems,
):
    slots, channels = vis.shape[0], vis.shape[1]
    kept = slots - more_hbm.shape[0]
    half, terms = own_ref.shape[0], own_ref.shape[1]
    pairs = channels // 2
    rows, tall = up(terms, 8), up(terms, 16)
    n_mine = jnp.minimum(mine_ref[2 * slots], kept)
    n_live = n_mine + jnp.maximum(other_ref[2 * slots] - kept, 0)
    copies = (
        pltpu.make_async_copy(vis_hbm.at[pl.ds(0, kept)], vis.at[pl.ds(0, kept)], sems.at[0]),
        pltpu.make_async_copy(more_hbm, vis.at[pl.ds(kept, slots - kept)], sems.at[1]),
    )
    for copy in copies:
        copy.start()

    row_sum[...] = jnp.zeros_like(row_sum)
    col_sum[...] = jnp.zeros_like(col_sum)
    both[...] = jnp.zeros_like(both)
    spread[...] = jnp.zeros_like(spread)

    for part, ref in enumerate((own_ref, got_ref)):
        for r in range(half):
            where = part * half + r
            chunk, lanes = where // 2, slice(where % 2 * LANES, (where % 2 + 1) * LANES)
            block = ref[r]
            both[chunk, 0:terms, lanes] = block
            both[chunk, LANES : LANES + terms, lanes] = block
            buf = where % 2
            spread[buf, 0:terms, :] = block.astype(F32)
            stage[buf, 0:LANES, :] = spread[buf].T
            pieces = [stage[buf, pl.ds(start, BLK // 2, stride=2), :] for start in (0, 1, BLK, BLK + 1)]
            sorted_rows = jnp.concatenate(pieces, 0)
            turned[2 * where] = sorted_rows[0:BLK].astype(BF)
            turned[2 * where + 1] = sorted_rows[BLK:].astype(BF)
            back = sorted_rows.T.astype(BF)
            lanes = slice((where % 2 + 2) * LANES, (where % 2 + 3) * LANES)
            both[chunk, 0:LANES, lanes] = back
            both[chunk, LANES:, lanes] = back

    low_r = low_lanes(tall)
    low_l = low_lanes(2 * rows)

    @pl.loop(0, half)
    def _(chunk):
        weights = both[chunk]
        for p in range(0, pairs, 2):
            gram_ref = first_gram_ref if p < pairs // 2 else second_gram_ref
            start = p % (pairs // 2) * 2 * rows
            found = jnp.dot(
                gram_ref[start : start + 4 * rows + 16, :], weights, preferred_element_type=F32
            )
            for side in range(2):
                block = 4 * chunk + 2 * side
                part = found[:, side * LANES : (side + 1) * LANES]
                for e in range(2):
                    first = part[2 * e * rows : 2 * e * rows + tall]
                    second = part[(2 * e + 1) * rows : (2 * e + 1) * rows + tall]
                    lanes = slice((p + e) * LANES, (p + e + 1) * LANES)
                    right[block, :, lanes] = jnp.where(low_r, first, pltpu.roll(second, BLK, 1)).astype(BF)
                    right[block + 1, :, lanes] = jnp.where(low_r, pltpu.roll(first, BLK, 1), second).astype(BF)
                part = found[:, (side + 2) * LANES : (side + 3) * LANES]
                first, second = part[0 : 2 * rows], part[2 * rows : 4 * rows]
                lanes = slice(p * BLK, p * BLK + LANES)
                left[block, :, lanes] = jnp.where(low_l, first, pltpu.roll(second, BLK, 1)).astype(BF)
                left[block + 1, :, lanes] = jnp.where(low_l, pltpu.roll(first, BLK, 1), second).astype(BF)

    row_pos = lax.broadcasted_iota(jnp.int32, (BLK, LANES), 0)
    row_dish = row_pos % (BLK // 2) * 2 + row_pos // (BLK // 2)
    ahead = lax.broadcasted_iota(jnp.int32, (BLK, LANES), 1) % BLK - row_dish
    low = low_lanes(BLK // 2)
    here = lax.axis_index("tile") if relative_bits else 0

    def place(block):
        if not relative_bits:
            return block
        return 2 * reverse_bits((block >> 1) ^ here, relative_bits) + (block & 1)

    for copy in copies:
        copy.wait()

    @pl.loop(0, (n_live + unroll - 1) // unroll)
    def _(group):
        slot_ids, pairs_of, leasts = [], [], []
        for u in range(unroll):
            turn = group * unroll + u
            is_mine = turn < n_mine
            slot = jnp.minimum(jnp.where(is_mine, turn, kept + turn - n_mine), slots - 1)
            row = jnp.where(is_mine, mine_ref[slot], other_ref[slot])
            col = jnp.where(is_mine, mine_ref[slots + slot], other_ref[slots + slot])
            slot_ids.append(slot)
            pairs_of.append((place(row), place(col)))
            leasts.append(jnp.where(turn < n_live, jnp.where(row == col, 0, -BLK), BLK))
        for u, slot in enumerate(slot_ids):
            for c in range(BLK // 2):
                stage[u, c * channels : (c + 1) * channels, :] = vis[
                    slot, :, c * LANES : (c + 1) * LANES
                ].astype(F32)
        models = [
            jnp.dot(turned[a][:, 0:tall], right[b], preferred_element_type=F32) for a, b in pairs_of
        ]
        residuals = []
        for u, slot in enumerate(slot_ids):
            keep = ahead > leasts[u]
            residual = []
            for p in range(pairs):
                first = stage[u, pl.ds(2 * p, BLK // 2, stride=channels), :]
                second = stage[u, pl.ds(2 * p + 1, BLK // 2, stride=channels), :]
                seen = jnp.concatenate(
                    [
                        jnp.where(low, first, pltpu.roll(second, BLK, 1)),
                        jnp.where(low, pltpu.roll(first, BLK, 1), second),
                    ],
                    0,
                )
                difference = models[u][:, p * LANES : (p + 1) * LANES] - seen
                residual.append(jnp.where(keep, difference, 0.0).astype(BF))
            residuals.append(residual)
        to_rows = [
            lax.dot_general(jnp.concatenate(residual, 1), right[b], NT, preferred_element_type=F32)
            for (a, b), residual in zip(pairs_of, residuals)
        ]
        to_cols = [
            jnp.dot(left[a], jnp.concatenate(residual, 0), preferred_element_type=F32)
            for (a, b), residual in zip(pairs_of, residuals)
        ]
        for (a, b), to_row, to_col in zip(pairs_of, to_rows, to_cols):
            row_sum[a, :, 0:tall] += to_row
            col_sum[b] += to_col

    low_out = low_lanes(rows)
    for where in range(2 * half):
        buf = where % 2
        for side in range(2):
            total = row_sum[2 * where + side]
            stage[buf, pl.ds(side * BLK, BLK // 2, stride=2), :] = total[0 : BLK // 2]
            stage[buf, pl.ds(side * BLK + 1, BLK // 2, stride=2), :] = total[BLK // 2 :]
        from_rows = stage[buf, 0:LANES, :].T[0:rows]
        cols = []
        for side in range(2):
            total = col_sum[2 * where + side]
            cols.append(total[0:rows] + pltpu.roll(total[rows:], BLK, 1))
        from_cols = jnp.where(low_out, cols[0], pltpu.roll(cols[1], BLK, 1))
        result = ((from_rows + from_cols) * scale)[0:terms]
        if where < half:
            keep_ref[where] = result
        else:
            send_ref[where - half] = result


def tile_terms(relative_bits, scale, mine, other, own, got, grams, observed, more):
    slots, channels, _ = observed.shape
    half, terms, _ = own.shape
    rows, tall = up(terms, 8), up(terms, 16)
    blocks = 4 * half
    unroll = UNROLL
    smem = pl.BlockSpec(memory_space=pltpu.SMEM)
    vmem = pl.BlockSpec(memory_space=pltpu.VMEM)
    out = jax.ShapeDtypeStruct((half, terms, LANES), F32)
    return pl.pallas_call(
        functools.partial(tiles_kernel, relative_bits, unroll, scale),
        out_shape=(out, out),
        in_specs=[smem, smem, vmem, vmem, vmem, vmem] + [pl.BlockSpec(memory_space=pl.ANY)] * 2,
        out_specs=(vmem, vmem),
        scratch_shapes=[
            pltpu.VMEM((slots, channels, BLK * BLK), BF),
            pltpu.VMEM((max(unroll, 2), channels * BLK // 2, LANES), F32),
            pltpu.VMEM((2, LANES, LANES), F32),
            pltpu.VMEM((half, 2 * LANES, 4 * LANES), BF),
            pltpu.VMEM((blocks, BLK, LANES), BF),
            pltpu.VMEM((blocks, tall, channels * BLK), BF),
            pltpu.VMEM((blocks, 2 * rows, channels // 2 * BLK), BF),
            pltpu.VMEM((blocks, BLK, LANES), F32),
            pltpu.VMEM((blocks, 2 * rows, LANES), F32),
            pltpu.SemaphoreType.DMA((2,)),
        ],
        compiler_params=pltpu.CompilerParams(vmem_limit_bytes=48 << 20),
        cost_estimate=pl.CostEstimate(
            flops=6 * slots * channels * BLK * BLK * terms, bytes_accessed=observed.size * 2, transcendentals=0
        ),
    )(mine, other, own, got, *grams, observed, more)


def from_partner(array, bit):
    return lax.ppermute(array, "tile", [(i, i ^ 1 << bit) for i in range(lax.axis_size("tile"))])


def on_device(
    coefficients, zernike_table, positions, source_flux, observed, tile_rows, tile_cols, tile_count
):
    members = lax.axis_size("tile")
    terms, shard = coefficients.shape
    dishes = members * shard
    scale = 1.0 / math.sqrt(dishes * positions.shape[0])
    channels, slots = positions.shape[0], tile_rows.shape[0]
    bits = members.bit_length() - 1
    moved = slots // 4 + 1
    mine = jnp.concatenate([tile_rows, tile_cols, tile_count])
    other = from_partner(mine, 0)
    more = from_partner(observed[slots - moved :], 0)
    grams = [
        gram_of(zernike_table, positions, source_flux, start, channels // 2)
        for start in (0, channels // 2)
    ]
    if shard == LANES and members == 1 << bits:
        held = coefficients[None]
        for step, bit in enumerate(reversed(range(1, bits))):
            held = jnp.concatenate([held, from_partner(held, bit)], 0)
            if step < 2:
                held, grams[step] = lax.optimization_barrier((held, grams[step]))
        got = from_partner(held, 0)
        total, sent = tile_terms(bits, scale, mine, other, held, got, grams, observed, more)
        total = total + from_partner(sent, 0)
        for bit in range(1, bits):
            half = total.shape[0] // 2
            total = total[:half] + from_partner(total[half:], bit)
        return total[0]
    everything = lax.all_gather(coefficients, "tile", axis=1, tiled=True)
    everything = everything.reshape(terms, dishes // LANES, LANES).transpose(1, 0, 2)
    half = everything.shape[0] // 2
    parts = tile_terms(
        0, scale, mine, other, everything[:half], everything[half:], grams, observed, more
    )
    total = jnp.concatenate(parts, 0).transpose(1, 0, 2).reshape(terms, dishes)
    return lax.psum_scatter(total, "tile", scatter_dimension=1, tiled=True)


def solution(mesh):
    return jax.shard_map(
        on_device,
        mesh=mesh,
        in_specs=(
            P(None, "tile"),
            P(),
            P("scan", None),
            P("scan", None),
            P(("scan", "tile"), None, None),
            P(("scan", "tile")),
            P(("scan", "tile")),
            P(("scan", "tile")),
        ),
        out_specs=P("scan", "tile"),
        check_vma=False,
    )
```

time: 80 us -> 58.3 us (0.73)
  starting transfers between devices: 25.3 us -> 14.5 us
  Pallas kernels: 29.2 us -> 24.6 us
  waiting for transfers between devices: 18.9 us -> 15.3 us
  other arithmetic: 2.89 us -> 0.78 us
    ppermute x8 -> x10, starting transfers between devices: 25.3 us -> 14.5 us  [from_partner(): lax.ppermute(array, 'tile', [(i, i ^ 1 << bit) for i in range(lax.axis_si...]
    pallas_call x1, Pallas kernels: 21.9 us -> 17 us  [tile_terms(): pl.pallas_call(functools.partial(tiles_kernel, relative_bits, unroll, sca...]
    ppermute x8 -> x10, waiting for transfers between devices: 18.9 us -> 15.3 us  [from_partner(): lax.ppermute(array, 'tile', [(i, i ^ 1 << bit) for i in range(lax.axis_si...]
    unnamed x10 -> x13, local copies, waits for them, and re-layouts: 2.5 us -> 0.03 us
    concatenate x3 -> x2, other arithmetic: 2.2 us -> 0.02 us  [on_device(): held = jnp.concatenate([held, from_partner(held, bit)], 0)]
    slice x0 -> x1, local copies, waits for them, and re-layouts: none -> 1.83 us  [on_device(): more = from_partner(observed[slots - moved:], 0)]
    pallas_call x1 -> x2, Pallas kernels: 7.32 us -> 7.63 us  [gram_of(): pl.pallas_call(functools.partial(gram_kernel, math.sqrt(sources), start,...]
  transfers between devices with their start and end apart: 8 -> 10, of which waited for: 7 -> 6; matrix products, arithmetic and copies ran while one was open for 0% -> 0% of each run, Pallas kernels for 9% -> 13%
where the time goes in v2:
time: 58.3 us; the launch traced here: 57.9 us
  Pallas kernels  24.6 us (42%)
  waiting for transfers between devices  15.3 us (26%)
  starting transfers between devices  14.5 us (25%)
  local copies, waits for them, and re-layouts  1.9 us (3%)
  between operations  0.79 us (1%)
  other arithmetic  0.78 us (1%)
    pallas_call x1, Pallas kernels, tile_terms(): pl.pallas_call(functools.partial(tiles_kernel, relative_bits, unroll, sca...  17 us
    ppermute x10, waiting for transfers between devices, from_partner(): lax.ppermute(array, 'tile', [(i, i ^ 1 << bit) for i in range(lax.axis_si...  15.3 us
    ppermute x10, starting transfers between devices, from_partner(): lax.ppermute(array, 'tile', [(i, i ^ 1 << bit) for i in range(lax.axis_si...  14.5 us
    pallas_call x2, Pallas kernels, gram_of(): pl.pallas_call(functools.partial(gram_kernel, math.sqrt(sources), start,...  7.63 us
    slice x1, local copies, waits for them, and re-layouts, on_device(): more = from_partner(observed[slots - moved:], 0)  1.83 us
  transfers between devices with their start and end apart: 10, of which 6 were waited for; matrix products, arithmetic and copies ran while one was open for 0% of the time, Pallas kernels for 13%

profile of v2, /device:TPU:0, one launch (start us, length us, event | category | flops | bytes accessed | tf_op | source)
XLA Modules:
  0.0 57.9 jit_solution(3675420386321943715)
XLA Ops:
  0.0 0.0 copy-start.3
  0.0 0.0 copy-start.2
  0.0 0.0 copy-start.1
  0.0 0.0 copy-start
  0.0 1.8 %slice.21 = bf16[17,16,4096]{2,1,0:T(8,128)(2,1)S(1)} slice(bf16[66,16,4096]{2,1,0:T(8,128)(2,1)} %vis_hbm.1), slice={[49:66], [0:16], [0:4096]} | slice | bytes 4456448 | tf_op jit(solution)/shard_map/slice | solution.py:291
  1.8 0.5 collective-permute-start.5
  2.4 0.0 copy-done.3
  2.4 3.7 %collective-permute-start.1 = (bf16[1,66,128]{2,1,0:T(8,128)(2,1)S(1)}, bf16[1,66,128]{2,1,0:T(8,128)(2,1)S(1)}, u32[]{:S(2)}, u32[]{:S(2)}) collective-permute-start(bf16[1,66,128]{2,1,0:T(8,128)(2,1)S(1)} %bitcast.3), channel_id=1, source_target_pairs={{0,8},{1,9},{2,10},{3,11},{4,12},{5,13},{6,14},{7,15},{8,0},{9,1},... | collective-permute-start | bytes 50696 | tf_op jit(solution)/shard_map/ppermute | solution.py:276
  6.1 0.0 copy-done.2
  6.1 0.0 copy-done.1
  6.1 0.0 copy-done
  6.1 3.8 %shard_map.82.first_gram_ref = bf16[592,256]{1,0:T(8,128)(2,1)S(1)} custom-call(bf16[66,4096]{1,0:T(8,128)(2,1)S(1)} %copy-done, s32[16,256]{1,0:T(8,128)S(1)} %copy-done.1, f32[16,256]{1,0:T(8,128)S(1)} %copy-done.2), custom_call_target="tpu_custom_call" | custom-call | flops 1107296256 | bytes 1048576 | tf_op jit(solution)/shard_map/pallas_call | solution.py:65
  9.9 0.0 collective-permute-done.1
  9.9 0.0 copy-start.4
  9.9 0.0 copy-start.5
  9.9 1.6 %collective-permute-start.2 = (bf16[2,66,128]{2,1,0:T(8,128)(2,1)S(1)}, bf16[2,66,128]{2,1,0:T(8,128)(2,1)S(1)}, u32[]{:S(2)}, u32[]{:S(2)}) collective-permute-start(bf16[2,66,128]{2,1,0:T(8,128)(2,1)S(1)} %pad_maximum_fusion.1), channel_id=1, source_target_pairs={{0,4},{1,5},{2,6},{3,7},{4,0},{5,1},{6,2},{7,3},{8,12},{9,13},{10,... | collective-permute-start | bytes 101384 | tf_op jit(solution)/shard_map/ppermute | solution.py:276
  11.6 3.8 %shard_map.83.second_gram_ref = bf16[592,256]{1,0:T(8,128)(2,1)S(1)} custom-call(bf16[66,4096]{1,0:T(8,128)(2,1)S(1)} %copy-done, s32[16,256]{1,0:T(8,128)S(1)} %copy-done.1, f32[16,256]{1,0:T(8,128)S(1)} %copy-done.2), custom_call_target="tpu_custom_call" | custom-call | flops 1107296256 | bytes 1048576 | tf_op jit(solution)/shard_map/pallas_call | solution.py:65
  15.4 0.0 collective-permute-done.2
  15.4 1.6 %collective-permute-start.3 = (bf16[4,66,128]{2,1,0:T(8,128)(2,1)S(1)}, bf16[4,66,128]{2,1,0:T(8,128)(2,1)S(1)}, u32[]{:S(2)}, u32[]{:S(2)}) collective-permute-start(bf16[4,66,128]{2,1,0:T(8,128)(2,1)S(1)} %pad_maximum_fusion), channel_id=1, source_target_pairs={{0,2},{1,3},{2,0},{3,1},{4,6},{5,7},{6,4},{7,5},{8,10},{9,11},{10,... | collective-permute-start | bytes 202760 | tf_op jit(solution)/shard_map/ppermute | solution.py:276
  17.0 2.8 %collective-permute-done.3 = bf16[4,66,128]{2,1,0:T(8,128)(2,1)S(1)} collective-permute-done((bf16[4,66,128]{2,1,0:T(8,128)(2,1)S(1)}, bf16[4,66,128]{2,1,0:T(8,128)(2,1)S(1)}, u32[]{:S(2)}, u32[]{:S(2)}) %collective-permute-start.3) | collective-permute-done | bytes 67616 | tf_op jit(solution)/shard_map/ppermute | solution.py:276
  19.9 0.1 collective-permute-start.4
  20.6 0.0 copy-done.4
  20.6 0.0 copy-done.5
  20.6 0.1 pad_add_fusion.mine_ref
  20.7 0.5 collective-permute-start
  21.2 0.8 %collective-permute-done.other_ref = s32[133]{0:T(256)S(1)} collective-permute-done((s32[133]{0:T(256)S(1)}, s32[133]{0:T(256)S(1)}, u32[]{:S(2)}, u32[]{:S(2)}) %collective-permute-start) | collective-permute-done | bytes 564 | tf_op jit(solution)/shard_map/ppermute | solution.py:276
  22.0 0.0 collective-permute-done.4.got_ref
  22.0 0.0 collective-permute-done.5.more_hbm
  22.0 17.0 %shard_map.84 = (f32[8,66,128]{2,1,0:T(8,128)S(1)}, f32[8,66,128]{2,1,0:T(8,128)S(1)}) custom-call(s32[133]{0:T(256)S(1)} %pad_add_fusion.mine_ref, s32[133]{0:T(256)S(1)} %collective-permute-done.other_ref, bf16[8,66,128]{2,1,0:T(8,128)(2,1)S(1)} %constant_dynamic-update-slice_fusion.own_ref, bf16[8,66,128]{2,1,0:T(8,128)(2,1)S(1)} %collective-permute-done.4.got_ref, ...), custom_call_target="tpu_custom_call" | custom-call | flops 1712848896 | bytes 8650752 | tf_op jit(solution)/shard_map/pallas_call | solution.py:251
  39.0 0.4 collective-permute-start.6
  39.4 1.3 %collective-permute-done.6 = f32[8,66,128]{2,1,0:T(8,128)S(1)} collective-permute-done((f32[8,66,128]{2,1,0:T(8,128)S(1)}, f32[8,66,128]{2,1,0:T(8,128)S(1)}, u32[]{:S(2)}, u32[]{:S(2)}) %collective-permute-start.6) | collective-permute-done | bytes 270368 | tf_op jit(solution)/shard_map/ppermute | solution.py:276
  40.7 1.6 %collective-permute-start.7 = (f32[4,66,128]{2,1,0:T(8,128)S(1)}, f32[4,66,128]{2,1,0:T(8,128)S(1)}, u32[]{:S(2)}, u32[]{:S(2)}) collective-permute-start(f32[4,66,128]{2,1,0:T(8,128)S(1)} %slice.29), channel_id=1, source_target_pairs={{0,2},{1,3},{2,0},{3,1},{4,6},{5,7},{6,4},{7,5},{8,10},{9,11},{10,... | collective-permute-start | bytes 405512 | tf_op jit(solution)/shard_map/ppermute | solution.py:276
  42.3 4.6 %collective-permute-done.7 = f32[4,66,128]{2,1,0:T(8,128)S(1)} collective-permute-done((f32[4,66,128]{2,1,0:T(8,128)S(1)}, f32[4,66,128]{2,1,0:T(8,128)S(1)}, u32[]{:S(2)}, u32[]{:S(2)}) %collective-permute-start.7) | collective-permute-done | bytes 135200 | tf_op jit(solution)/shard_map/ppermute | solution.py:276
  46.9 0.5 collective-permute-start.8
  47.4 3.9 %collective-permute-done.8 = f32[2,66,128]{2,1,0:T(8,128)S(1)} collective-permute-done((f32[2,66,128]{2,1,0:T(8,128)S(1)}, f32[2,66,128]{2,1,0:T(8,128)S(1)}, u32[]{:S(2)}, u32[]{:S(2)}) %collective-permute-start.8) | collective-permute-done | bytes 67616 | tf_op jit(solution)/shard_map/ppermute | solution.py:276
  51.3 4.0 %collective-permute-start.9 = (f32[1,66,128]{2,1,0:T(8,128)S(1)}, f32[1,66,128]{2,1,0:T(8,128)S(1)}, u32[]{:S(2)}, u32[]{:S(2)}) collective-permute-start(f32[1,66,128]{2,1,0:T(8,128)S(1)} %slice.33), channel_id=1, source_target_pairs={{0,8},{1,9},{2,10},{3,11},{4,12},{5,13},{6,14},{7,15},{8,0},{9,1},... | collective-permute-start | bytes 101384 | tf_op jit(solution)/shard_map/ppermute | solution.py:276
  55.4 1.9 %collective-permute-done.9 = f32[1,66,128]{2,1,0:T(8,128)S(1)} collective-permute-done((f32[1,66,128]{2,1,0:T(8,128)S(1)}, f32[1,66,128]{2,1,0:T(8,128)S(1)}, u32[]{:S(2)}, u32[]{:S(2)}) %collective-permute-start.9) | collective-permute-done | bytes 33824 | tf_op jit(solution)/shard_map/ppermute | solution.py:276
  57.3 0.6 %fusion = f32[66,128]{1,0:T(8,128)} fusion(f32[1,66,128]{2,1,0:T(8,128)S(1)} %collective-permute-done.9, f32[2,66,128]{2,1,0:T(8,128)S(1)} %slice_add_fusion.1), kind=kLoop, calls=%fused_computation.4 | loop fusion | flops 8448 | bytes 101376 | tf_op jit(solution)/shard_map/squeeze | solution.py:308
  (10 shorter events, 0.1 us)
Async XLA Ops:
  0.0 2.4 %copy-start.3 = (bf16[66,128]{1,0:T(8,128)(2,1)S(1)}, bf16[66,128]{1,0:T(8,128)(2,1)}, u32[]{:S(2)}) copy-start(bf16[66,128]{1,0:T(8,128)(2,1)} %param.8) | copy-start | bytes 50692
  0.0 6.1 %copy-start.2 = (f32[16,256]{1,0:T(8,128)S(1)}, f32[16,256]{1,0:T(8,128)}, u32[]{:S(2)}) copy-start(f32[16,256]{1,0:T(8,128)} %flux_ref.3) | copy-start | bytes 49156
  0.0 6.1 %copy-start.1 = (s32[16,256]{1,0:T(8,128)S(1)}, s32[16,256]{1,0:T(8,128)}, u32[]{:S(2)}) copy-start(s32[16,256]{1,0:T(8,128)} %pos_ref.3) | copy-start | bytes 49156
  0.0 6.1 %copy-start = (bf16[66,4096]{1,0:T(8,128)(2,1)S(1)}, bf16[66,4096]{1,0:T(8,128)(2,1)}, u32[]{:S(2)}) copy-start(bf16[66,4096]{1,0:T(8,128)(2,1)} %table_ref.3) | copy-start | bytes 1622020
  1.8 20.2 %collective-permute-start.5 = (bf16[17,16,4096]{2,1,0:T(8,128)(2,1)S(1)}, bf16[17,16,4096]{2,1,0:T(8,128)(2,1)S(1)}, u32[]{:S(2)}, u32[]{:S(2)}) collective-permute-start(bf16[17,16,4096]{2,1,0:T(8,128)(2,1)S(1)} %slice.21), channel_id=1, source_target_pairs={{0,1},{1,0},{2,3},{3,2},{4,5},{5,4},{6,7},{7,6},{8,9},{9,8},{10,11... | collective-permute-start | bytes 6684680 | tf_op jit(solution)/shard_map/ppermute | solution.py:276
  2.4 7.5 %collective-permute-start.1 = (bf16[1,66,128]{2,1,0:T(8,128)(2,1)S(1)}, bf16[1,66,128]{2,1,0:T(8,128)(2,1)S(1)}, u32[]{:S(2)}, u32[]{:S(2)}) collective-permute-start(bf16[1,66,128]{2,1,0:T(8,128)(2,1)S(1)} %bitcast.3), channel_id=1, source_target_pairs={{0,8},{1,9},{2,10},{3,11},{4,12},{5,13},{6,14},{7,15},{8,0},{9,1},... | collective-permute-start | bytes 50696 | tf_op jit(solution)/shard_map/ppermute | solution.py:276
  9.9 10.7 %copy-start.4 = (s32[66]{0:T(128)S(1)}, s32[66]{0:T(128)}, u32[]{:S(2)}) copy-start(s32[66]{0:T(128)} %param.14) | copy-start | bytes 796
  9.9 10.7 %copy-start.5 = (s32[66]{0:T(128)S(1)}, s32[66]{0:T(128)}, u32[]{:S(2)}) copy-start(s32[66]{0:T(128)} %param.13) | copy-start | bytes 796
  9.9 5.5 %collective-permute-start.2 = (bf16[2,66,128]{2,1,0:T(8,128)(2,1)S(1)}, bf16[2,66,128]{2,1,0:T(8,128)(2,1)S(1)}, u32[]{:S(2)}, u32[]{:S(2)}) collective-permute-start(bf16[2,66,128]{2,1,0:T(8,128)(2,1)S(1)} %pad_maximum_fusion.1), channel_id=1, source_target_pairs={{0,4},{1,5},{2,6},{3,7},{4,0},{5,1},{6,2},{7,3},{8,12},{9,13},{10,... | collective-permute-start | bytes 101384 | tf_op jit(solution)/shard_map/ppermute | solution.py:276
  15.4 4.4 %collective-permute-start.3 = (bf16[4,66,128]{2,1,0:T(8,128)(2,1)S(1)}, bf16[4,66,128]{2,1,0:T(8,128)(2,1)S(1)}, u32[]{:S(2)}, u32[]{:S(2)}) collective-permute-start(bf16[4,66,128]{2,1,0:T(8,128)(2,1)S(1)} %pad_maximum_fusion), channel_id=1, source_target_pairs={{0,2},{1,3},{2,0},{3,1},{4,6},{5,7},{6,4},{7,5},{8,10},{9,11},{10,... | collective-permute-start | bytes 202760 | tf_op jit(solution)/shard_map/ppermute | solution.py:276
  19.9 2.2 %collective-permute-start.4 = (bf16[8,66,128]{2,1,0:T(8,128)(2,1)S(1)}, bf16[8,66,128]{2,1,0:T(8,128)(2,1)S(1)}, u32[]{:S(2)}, u32[]{:S(2)}) collective-permute-start(bf16[8,66,128]{2,1,0:T(8,128)(2,1)S(1)} %constant_dynamic-update-slice_fusion.own_ref), channel_id=1, source_target_pairs={{0,1},{1,0},{2,3},{3,2},{4,5},{5,4},{6,7},{7,6},{8,9},{9,8},{10,11... | collective-permute-start | bytes 405512 | tf_op jit(solution)/shard_map/ppermute | solution.py:276
  20.7 1.3 %collective-permute-start = (s32[133]{0:T(256)S(1)}, s32[133]{0:T(256)S(1)}, u32[]{:S(2)}, u32[]{:S(2)}) collective-permute-start(s32[133]{0:T(256)S(1)} %pad_add_fusion.mine_ref), channel_id=1, source_target_pairs={{0,1},{1,0},{2,3},{3,2},{4,5},{5,4},{6,7},{7,6},{8,9},{9,8},{10,11... | collective-permute-start | bytes 1604 | tf_op jit(solution)/shard_map/ppermute | solution.py:276
  39.0 1.6 %collective-permute-start.6 = (f32[8,66,128]{2,1,0:T(8,128)S(1)}, f32[8,66,128]{2,1,0:T(8,128)S(1)}, u32[]{:S(2)}, u32[]{:S(2)}) collective-permute-start(f32[8,66,128]{2,1,0:T(8,128)S(1)} %get-tuple-element.16), channel_id=1, source_target_pairs={{0,1},{1,0},{2,3},{3,2},{4,5},{5,4},{6,7},{7,6},{8,9},{9,8},{10,11... | collective-permute-start | bytes 811016 | tf_op jit(solution)/shard_map/ppermute | solution.py:276
  40.7 6.1 %collective-permute-start.7 = (f32[4,66,128]{2,1,0:T(8,128)S(1)}, f32[4,66,128]{2,1,0:T(8,128)S(1)}, u32[]{:S(2)}, u32[]{:S(2)}) collective-permute-start(f32[4,66,128]{2,1,0:T(8,128)S(1)} %slice.29), channel_id=1, source_target_pairs={{0,2},{1,3},{2,0},{3,1},{4,6},{5,7},{6,4},{7,5},{8,10},{9,11},{10,... | collective-permute-start | bytes 405512 | tf_op jit(solution)/shard_map/ppermute | solution.py:276
  46.9 4.4 %collective-permute-start.8 = (f32[2,66,128]{2,1,0:T(8,128)S(1)}, f32[2,66,128]{2,1,0:T(8,128)S(1)}, u32[]{:S(2)}, u32[]{:S(2)}) collective-permute-start(f32[2,66,128]{2,1,0:T(8,128)S(1)} %slice.31), channel_id=1, source_target_pairs={{0,4},{1,5},{2,6},{3,7},{4,0},{5,1},{6,2},{7,3},{8,12},{9,13},{10,... | collective-permute-start | bytes 202760 | tf_op jit(solution)/shard_map/ppermute | solution.py:276
  51.3 6.0 %collective-permute-start.9 = (f32[1,66,128]{2,1,0:T(8,128)S(1)}, f32[1,66,128]{2,1,0:T(8,128)S(1)}, u32[]{:S(2)}, u32[]{:S(2)}) collective-permute-start(f32[1,66,128]{2,1,0:T(8,128)S(1)} %slice.33), channel_id=1, source_target_pairs={{0,8},{1,9},{2,10},{3,11},{4,12},{5,13},{6,14},{7,15},{8,0},{9,1},... | collective-permute-start | bytes 101384 | tf_op jit(solution)/shard_map/ppermute | solution.py:276

commit v3 on v2

--- a/solution.py
+++ b/solution.py
@@ -25,7 +25,15 @@
     return lax.broadcasted_iota(jnp.int32, (rows, LANES), 1) < BLK
 
 
-def gram_kernel(root, start, count, table_ref, pos_ref, flux_ref, out_ref, groups, gram):
+def gram_kernel(root, start, count, table_ref, pos_ref, flux_ref, *rest):
+    if len(rest) > 3:
+        vis_hbm, out_ref, moved_hbm, groups, gram, sem = rest
+        moved = moved_hbm.shape[0]
+        copy = pltpu.make_async_copy(vis_hbm.at[pl.ds(vis_hbm.shape[0] - moved, moved)], moved_hbm, sem)
+        copy.start()
+    else:
+        out_ref, groups, gram = rest
+        copy = None
     terms, pixels = table_ref.shape
     sources = pos_ref.shape[1]
     n_groups = pixels // PIXELS
@@ -55,42 +63,57 @@
     high = value.astype(BF)
     out_ref[:, 0:LANES] = high
     out_ref[:, LANES : 2 * LANES] = (value - high.astype(F32)).astype(BF)
-
-
-def gram_of(zernike_table, positions, source_flux, start, count):
+    if copy is not None:
+        copy.wait()
+
+
+def gram_of(zernike_table, positions, source_flux, start, count, observed=None, moved=0):
     terms, pixels = zernike_table.shape
     sources = positions.shape[1]
     rows, tall = up(terms, 8), up(terms, 16)
     height = up(count * rows + 8, 16)
+    vmem = pl.BlockSpec(memory_space=pltpu.VMEM)
+    anywhere = pl.BlockSpec(memory_space=pl.ANY)
+    out_shape = [jax.ShapeDtypeStruct((height, 2 * LANES), BF)]
+    scratch = [pltpu.VMEM((pixels // PIXELS * tall, PIXELS), BF), pltpu.VMEM((height, LANES), F32)]
+    operands, in_specs, out_specs = [zernike_table, positions, source_flux], [vmem] * 3, [vmem]
+    if moved:
+        operands.append(observed)
+        in_specs.append(anywhere)
+        out_shape.append(jax.ShapeDtypeStruct((moved,) + observed.shape[1:], BF))
+        out_specs.append(anywhere)
+        scratch.append(pltpu.SemaphoreType.DMA)
     return pl.pallas_call(
         functools.partial(gram_kernel, math.sqrt(sources), start, count),
-        out_shape=jax.ShapeDtypeStruct((height, 2 * LANES), BF),
-        in_specs=[pl.BlockSpec(memory_space=pltpu.VMEM)] * 3,
-        out_specs=pl.BlockSpec(memory_space=pltpu.VMEM),
-        scratch_shapes=[
-            pltpu.VMEM((pixels // PIXELS * tall, PIXELS), BF),
-            pltpu.VMEM((height, LANES), F32),
-        ],
-        compiler_params=pltpu.CompilerParams(vmem_limit_bytes=32 << 20),
+        out_shape=out_shape,
+        in_specs=in_specs,
+        out_specs=out_specs,
+        scratch_shapes=scratch,
+        compiler_params=pltpu.CompilerParams(vmem_limit_bytes=56 << 20),
         cost_estimate=pl.CostEstimate(
             flops=2 * count * sources * pixels * terms, bytes_accessed=1 << 20, transcendentals=0
         ),
-    )(zernike_table, positions, source_flux)
-
-
-def reverse_bits(value, bits):
-    result = value & 0
-    for bit in range(bits):
-        result = result | ((value >> bit) & 1) << (bits - 1 - bit)
-    return result
+    )(*operands)
+
+
+def relative_place(device, here):
+    apart = device ^ here
+    near, far = (apart >> 1) & 1, (apart >> 2) & 1
+    odd = (device & 1) == 1
+    return (
+        8 * (apart & 1)
+        + 4 * jnp.where(odd, far, near)
+        + 2 * jnp.where(odd, near, far)
+        + ((apart >> 3) & 1)
+    )
 
 
 def tiles_kernel(
-    relative_bits, unroll, scale,
-    mine_ref, other_ref, own_ref, got_ref, first_gram_ref, second_gram_ref, vis_hbm, more_hbm,
-    keep_ref, send_ref,
-    vis, stage, spread, both, turned, right, left, row_sum, col_sum, sems,
+    relative, unroll, scale, pieces,
+    mine_ref, other_ref, own_ref, got_ref, vis_hbm, more_hbm, *rest,
 ):
+    gram_refs, rest = rest[: len(pieces)], rest[len(pieces) :]
+    keep_ref, send_ref, vis, stage, spread, both, turned, right, left, row_sum, col_sum, sems = rest
     slots, channels = vis.shape[0], vis.shape[1]
     kept = slots - more_hbm.shape[0]
     half, terms = own_ref.shape[0], own_ref.shape[1]
@@ -108,6 +131,7 @@
     row_sum[...] = jnp.zeros_like(row_sum)
     col_sum[...] = jnp.zeros_like(col_sum)
     both[...] = jnp.zeros_like(both)
+    per_tile = stage.shape[1] // LANES
     spread[...] = jnp.zeros_like(spread)
 
     for part, ref in enumerate((own_ref, got_ref)):
@@ -117,11 +141,16 @@
             block = ref[r]
             both[chunk, 0:terms, lanes] = block
             both[chunk, LANES : LANES + terms, lanes] = block
-            buf = where % 2
-            spread[buf, 0:terms, :] = block.astype(F32)
-            stage[buf, 0:LANES, :] = spread[buf].T
-            pieces = [stage[buf, pl.ds(start, BLK // 2, stride=2), :] for start in (0, 1, BLK, BLK + 1)]
-            sorted_rows = jnp.concatenate(pieces, 0)
+            spread[where, 0:terms, :] = block.astype(F32)
+            buf, base = where // per_tile, where % per_tile * LANES
+            stage[buf, base : base + LANES, :] = spread[where].T
+            sorted_rows = jnp.concatenate(
+                [
+                    stage[buf, pl.ds(base + start, BLK // 2, stride=2), :]
+                    for start in (0, 1, BLK, BLK + 1)
+                ],
+                0,
+            )
             turned[2 * where] = sorted_rows[0:BLK].astype(BF)
             turned[2 * where + 1] = sorted_rows[BLK:].astype(BF)
             back = sorted_rows.T.astype(BF)
@@ -136,8 +165,8 @@
     def _(chunk):
         weights = both[chunk]
         for p in range(0, pairs, 2):
-            gram_ref = first_gram_ref if p < pairs // 2 else second_gram_ref
-            start = p % (pairs // 2) * 2 * rows
+            piece = max(n for n, (first, _) in enumerate(pieces) if first <= 2 * p)
+            gram_ref, start = gram_refs[piece], (2 * p - pieces[piece][0]) * rows
             found = jnp.dot(
                 gram_ref[start : start + 4 * rows + 16, :], weights, preferred_element_type=F32
             )
@@ -160,12 +189,10 @@
     row_dish = row_pos % (BLK // 2) * 2 + row_pos // (BLK // 2)
     ahead = lax.broadcasted_iota(jnp.int32, (BLK, LANES), 1) % BLK - row_dish
     low = low_lanes(BLK // 2)
-    here = lax.axis_index("tile") if relative_bits else 0
+    here = lax.axis_index("tile") if relative else 0
 
     def place(block):
-        if not relative_bits:
-            return block
-        return 2 * reverse_bits((block >> 1) ^ here, relative_bits) + (block & 1)
+        return 2 * relative_place(block >> 1, here) + (block & 1) if relative else block
 
     for copy in copies:
         copy.wait()
@@ -221,12 +248,15 @@
 
     low_out = low_lanes(rows)
     for where in range(2 * half):
-        buf = where % 2
+        buf, base = where // per_tile, where % per_tile * LANES
         for side in range(2):
             total = row_sum[2 * where + side]
-            stage[buf, pl.ds(side * BLK, BLK // 2, stride=2), :] = total[0 : BLK // 2]
-            stage[buf, pl.ds(side * BLK + 1, BLK // 2, stride=2), :] = total[BLK // 2 :]
-        from_rows = stage[buf, 0:LANES, :].T[0:rows]
+            start = base + side * BLK
+            stage[buf, pl.ds(start, BLK // 2, stride=2), :] = total[0 : BLK // 2]
+            stage[buf, pl.ds(start + 1, BLK // 2, stride=2), :] = total[BLK // 2 :]
+    for where in range(2 * half):
+        buf, base = where // per_tile, where % per_tile * LANES
+        from_rows = stage[buf, base : base + LANES, :].T[0:rows]
         cols = []
         for side in range(2):
             total = col_sum[2 * where + side]
@@ -239,7 +269,7 @@
             send_ref[where - half] = result
 
 
-def tile_terms(relative_bits, scale, mine, other, own, got, grams, observed, more):
+def tile_terms(relative, scale, pieces, mine, other, own, got, grams, observed, more):
     slots, channels, _ = observed.shape
     half, terms, _ = own.shape
     rows, tall = up(terms, 8), up(terms, 16)
@@ -249,14 +279,14 @@
     vmem = pl.BlockSpec(memory_space=pltpu.VMEM)
     out = jax.ShapeDtypeStruct((half, terms, LANES), F32)
     return pl.pallas_call(
-        functools.partial(tiles_kernel, relative_bits, unroll, scale),
+        functools.partial(tiles_kernel, relative, unroll, scale, pieces),
         out_shape=(out, out),
-        in_specs=[smem, smem, vmem, vmem, vmem, vmem] + [pl.BlockSpec(memory_space=pl.ANY)] * 2,
+        in_specs=[smem, smem, vmem, vmem] + [pl.BlockSpec(memory_space=pl.ANY)] * 2 + [vmem] * len(grams),
         out_specs=(vmem, vmem),
         scratch_shapes=[
             pltpu.VMEM((slots, channels, BLK * BLK), BF),
-            pltpu.VMEM((max(unroll, 2), channels * BLK // 2, LANES), F32),
-            pltpu.VMEM((2, LANES, LANES), F32),
+            pltpu.VMEM((up(max(unroll, 2 * half * LANES // (channels * BLK // 2)), 1), channels * BLK // 2, LANES), F32),
+            pltpu.VMEM((2 * half, LANES, LANES), F32),
             pltpu.VMEM((half, 2 * LANES, 4 * LANES), BF),
             pltpu.VMEM((blocks, BLK, LANES), BF),
             pltpu.VMEM((blocks, tall, channels * BLK), BF),
@@ -269,11 +299,14 @@
         cost_estimate=pl.CostEstimate(
             flops=6 * slots * channels * BLK * BLK * terms, bytes_accessed=observed.size * 2, transcendentals=0
         ),
-    )(mine, other, own, got, *grams, observed, more)
-
-
-def from_partner(array, bit):
-    return lax.ppermute(array, "tile", [(i, i ^ 1 << bit) for i in range(lax.axis_size("tile"))])
+    )(mine, other, own, got, observed, more, *grams)
+
+
+def from_partner(array, even, odd=None):
+    odd = even if odd is None else odd
+    return lax.ppermute(
+        array, "tile", [(i, i ^ (odd if i % 2 else even)) for i in range(lax.axis_size("tile"))]
+    )
 
 
 def on_device(
@@ -284,33 +317,39 @@
     dishes = members * shard
     scale = 1.0 / math.sqrt(dishes * positions.shape[0])
     channels, slots = positions.shape[0], tile_rows.shape[0]
-    bits = members.bit_length() - 1
     moved = slots // 4 + 1
     mine = jnp.concatenate([tile_rows, tile_cols, tile_count])
-    other = from_partner(mine, 0)
-    more = from_partner(observed[slots - moved :], 0)
-    grams = [
-        gram_of(zernike_table, positions, source_flux, start, channels // 2)
-        for start in (0, channels // 2)
+    other = from_partner(mine, 1)
+    quarter = channels // 4
+    pieces = ((0, 2 * quarter), (2 * quarter, quarter), (3 * quarter, quarter))
+    first, to_move = gram_of(zernike_table, positions, source_flux, *pieces[0], observed, moved)
+    grams = [first] + [
+        gram_of(zernike_table, positions, source_flux, *piece)[0] for piece in pieces[1:]
     ]
-    if shard == LANES and members == 1 << bits:
+    if shard == LANES and members == 16:
         held = coefficients[None]
-        for step, bit in enumerate(reversed(range(1, bits))):
-            held = jnp.concatenate([held, from_partner(held, bit)], 0)
-            if step < 2:
-                held, grams[step] = lax.optimization_barrier((held, grams[step]))
-        got = from_partner(held, 0)
-        total, sent = tile_terms(bits, scale, mine, other, held, got, grams, observed, more)
-        total = total + from_partner(sent, 0)
-        for bit in range(1, bits):
-            half = total.shape[0] // 2
-            total = total[:half] + from_partner(total[half:], bit)
+        held = jnp.concatenate([held, from_partner(held, 8)], 0)
+        held, grams[0], to_move, other = lax.optimization_barrier((held, grams[0], to_move, other))
+        more = from_partner(to_move, 1)
+        held = jnp.concatenate([held, from_partner(held, 4, 2)], 0)
+        held, grams[1] = lax.optimization_barrier((held, grams[1]))
+        held = jnp.concatenate([held, from_partner(held, 2, 4)], 0)
+        held, grams[2] = lax.optimization_barrier((held, grams[2]))
+        got = from_partner(held, 1)
+        total, sent = tile_terms(
+            True, scale, pieces, mine, other, held, got, grams, observed, more
+        )
+        total = total + from_partner(sent, 1)
+        total = total[:4] + from_partner(total[4:], 2, 4)
+        total = total[:2] + from_partner(total[2:], 4, 2)
+        total = total[:1] + from_partner(total[1:], 8)
         return total[0]
+    more = from_partner(to_move, 1)
     everything = lax.all_gather(coefficients, "tile", axis=1, tiled=True)
     everything = everything.reshape(terms, dishes // LANES, LANES).transpose(1, 0, 2)
     half = everything.shape[0] // 2
     parts = tile_terms(
-        0, scale, mine, other, everything[:half], everything[half:], grams, observed, more
+        False, scale, pieces, mine, other, everything[:half], everything[half:], grams, observed, more
     )
     total = jnp.concatenate(parts, 0).transpose(1, 0, 2).reshape(terms, dishes)
     return lax.psum_scatter(total, "tile", scatter_dimension=1, tiled=True)

time: 58.3 us -> 125 us (2.14)
  Pallas kernels: 24.6 us -> 95.1 us
  starting transfers between devices: 14.5 us -> 9.44 us
    pallas_call x2 -> x3, Pallas kernels: 7.63 us -> 78.1 us  [gram_of(): pl.pallas_call(functools.partial(gram_kernel, math.sqrt(sources), start,...]
    ppermute x10, starting transfers between devices: 14.5 us -> 9.44 us  [from_partner(): lax.ppermute(array, 'tile', [(i, i ^ (odd if i % 2 else even)) for i in r...]
    slice x4 -> x3, local copies, waits for them, and re-layouts: 1.86 us -> 0.02 us  [the longest x1 0.01 us: on_device(): total = total[:4] + from_partner(total[4:], 2, 4)]
  transfers between devices with their start and end apart: 10 -> 10, of which waited for: 6 -> 5; matrix products, arithmetic and copies ran while one was open for 0% -> 0% of each run, Pallas kernels for 13% -> 63%
where the time goes in v3:
time: 125 us; the launch traced here: 124 us
  Pallas kernels  95.1 us (76%)
  waiting for transfers between devices  16 us (13%)
  starting transfers between devices  9.44 us (8%)
  other arithmetic  1.47 us (1%)
    pallas_call x3, Pallas kernels, gram_of(): pl.pallas_call(functools.partial(gram_kernel, math.sqrt(sources), start,...  78.1 us
    pallas_call x1, Pallas kernels, tile_terms(): pl.pallas_call(functools.partial(tiles_kernel, relative, unroll, scale, p...  17 us
    ppermute x10, waiting for transfers between devices, from_partner(): lax.ppermute(array, 'tile', [(i, i ^ (odd if i % 2 else even)) for i in r...  16 us
    ppermute x10, starting transfers between devices, from_partner(): lax.ppermute(array, 'tile', [(i, i ^ (odd if i % 2 else even)) for i in r...  9.44 us
  transfers between devices with their start and end apart: 10, of which 5 were waited for; matrix products, arithmetic and copies ran while one was open for 0% of the time, Pallas kernels for 63%

profile of v3, /device:TPU:0, one launch (start us, length us, event | category | flops | bytes accessed | tf_op | source)
XLA Modules:
  0.0 123.7 jit_solution(17199600065225368768)
XLA Ops:
  0.7 0.7 pad_add_fusion.mine_ref
  1.4 0.5 collective-permute-start.1
  1.9 0.0 copy-start.3
  1.9 3.7 %collective-permute-start = (bf16[1,66,128]{2,1,0:T(8,128)(2,1)}, bf16[1,66,128]{2,1,0:T(8,128)(2,1)S(1)}, u32[]{:S(2)}, u32[]{:S(2)}) collective-permute-start(bf16[1,66,128]{2,1,0:T(8,128)(2,1)} %bitcast.3), channel_id=1, source_target_pairs={{0,8},{1,9},{2,10},{3,11},{4,12},{5,13},{6,14},{7,15},{8,0},{9,1},... | collective-permute-start | bytes 50696 | tf_op jit(solution)/shard_map/ppermute | solution.py:307
  5.5 70.4 %shard_map.82 = (bf16[592,256]{1,0:T(8,128)(2,1)}, bf16[17,16,4096]{2,1,0:T(8,128)(2,1)}) custom-call(bf16[66,4096]{1,0:T(8,128)(2,1)} %table_ref.5, s32[16,256]{1,0:T(8,128)} %pos_ref.5, f32[16,256]{1,0:T(8,128)} %flux_ref.5, bf16[66,16,4096]{2,1,0:T(8,128)(2,1)} %vis_hbm.1), custom_call_target="tpu_custom_call" | custom-call | flops 1107296256 | bytes 1048576 | tf_op jit(solution)/shard_map/pallas_call | solution.py:86
  76.0 0.0 collective-permute-done
  76.0 0.0 copy-done.3
  76.0 0.0 collective-permute-done.1.other_ref
  76.0 0.0 copy-start
  76.0 0.2 collective-permute-start.5
  76.2 1.6 %collective-permute-start.2 = (bf16[2,66,128]{2,1,0:T(8,128)(2,1)S(1)}, bf16[2,66,128]{2,1,0:T(8,128)(2,1)S(1)}, u32[]{:S(2)}, u32[]{:S(2)}) collective-permute-start(bf16[2,66,128]{2,1,0:T(8,128)(2,1)S(1)} %pad_maximum_fusion.2), channel_id=1, source_target_pairs={{0,4},{1,3},{2,6},{3,1},{4,0},{5,7},{6,2},{7,5},{8,12},{9,11},{10,... | collective-permute-start | bytes 101384 | tf_op jit(solution)/shard_map/ppermute | solution.py:307
  77.8 3.8 %shard_map.83.rest_1_ = bf16[304,256]{1,0:T(8,128)(2,1)} custom-call(bf16[66,4096]{1,0:T(8,128)(2,1)} %table_ref.5, s32[16,256]{1,0:T(8,128)} %pos_ref.5, f32[16,256]{1,0:T(8,128)} %flux_ref.5), custom_call_target="tpu_custom_call" | custom-call | flops 553648128 | bytes 1048576 | tf_op jit(solution)/shard_map/pallas_call | solution.py:86
  81.6 0.0 copy-start.1
  81.6 0.0 collective-permute-done.2
  81.6 1.6 %collective-permute-start.3 = (bf16[4,66,128]{2,1,0:T(8,128)(2,1)S(1)}, bf16[4,66,128]{2,1,0:T(8,128)(2,1)S(1)}, u32[]{:S(2)}, u32[]{:S(2)}) collective-permute-start(bf16[4,66,128]{2,1,0:T(8,128)(2,1)S(1)} %pad_maximum_fusion.1), channel_id=1, source_target_pairs={{0,2},{1,5},{2,0},{3,7},{4,6},{5,1},{6,4},{7,3},{8,10},{9,13},{10,... | collective-permute-start | bytes 202760 | tf_op jit(solution)/shard_map/ppermute | solution.py:307
  83.2 3.8 %shard_map.84.rest_2_ = bf16[304,256]{1,0:T(8,128)(2,1)} custom-call(bf16[66,4096]{1,0:T(8,128)(2,1)} %table_ref.5, s32[16,256]{1,0:T(8,128)} %pos_ref.5, f32[16,256]{1,0:T(8,128)} %flux_ref.5), custom_call_target="tpu_custom_call" | custom-call | flops 553648128 | bytes 1048576 | tf_op jit(solution)/shard_map/pallas_call | solution.py:86
  87.1 0.0 collective-permute-done.3
  87.1 0.1 collective-permute-start.4
  87.2 1.4 %collective-permute-done.4.got_ref = bf16[8,66,128]{2,1,0:T(8,128)(2,1)S(1)} collective-permute-done((bf16[8,66,128]{2,1,0:T(8,128)(2,1)S(1)}, bf16[8,66,128]{2,1,0:T(8,128)(2,1)S(1)}, u32[]{:S(2)}, u32[]{:S(2)}) %collective-permute-start.4) | collective-permute-done | bytes 135200 | tf_op jit(solution)/shard_map/ppermute | solution.py:307
  88.5 0.0 collective-permute-done.5.more_hbm
  88.5 0.0 copy-done
  88.5 0.0 copy-done.1
  88.5 0.0 copy-start.2
  88.5 0.9 copy-done.2
  89.4 17.0 %shard_map.85 = (f32[8,66,128]{2,1,0:T(8,128)S(1)}, f32[8,66,128]{2,1,0:T(8,128)S(1)}) custom-call(s32[133]{0:T(256)S(1)} %pad_add_fusion.mine_ref, s32[133]{0:T(256)S(1)} %collective-permute-done.1.other_ref, bf16[8,66,128]{2,1,0:T(8,128)(2,1)S(1)} %pad_maximum_fusion.own_ref, bf16[8,66,128]{2,1,0:T(8,128)(2,1)S(1)} %collective-permute-done.4.got_ref, ...), custom_call_target="tpu_custom_call" | custom-call | flops 1712848896 | bytes 8650752 | tf_op jit(solution)/shard_map/pallas_call | solution.py:281
  106.5 0.2 collective-permute-start.6
  106.7 1.4 %collective-permute-done.6 = f32[8,66,128]{2,1,0:T(8,128)S(1)} collective-permute-done((f32[8,66,128]{2,1,0:T(8,128)S(1)}, f32[8,66,128]{2,1,0:T(8,128)S(1)}, u32[]{:S(2)}, u32[]{:S(2)}) %collective-permute-start.6) | collective-permute-done | bytes 270368 | tf_op jit(solution)/shard_map/ppermute | solution.py:307
  108.2 0.6 collective-permute-start.7
  108.8 4.6 %collective-permute-done.7 = f32[4,66,128]{2,1,0:T(8,128)S(1)} collective-permute-done((f32[4,66,128]{2,1,0:T(8,128)S(1)}, f32[4,66,128]{2,1,0:T(8,128)S(1)}, u32[]{:S(2)}, u32[]{:S(2)}) %collective-permute-start.7) | collective-permute-done | bytes 135200 | tf_op jit(solution)/shard_map/ppermute | solution.py:307
  113.4 0.5 collective-permute-start.8
  113.9 3.9 %collective-permute-done.8 = f32[2,66,128]{2,1,0:T(8,128)S(1)} collective-permute-done((f32[2,66,128]{2,1,0:T(8,128)S(1)}, f32[2,66,128]{2,1,0:T(8,128)S(1)}, u32[]{:S(2)}, u32[]{:S(2)}) %collective-permute-start.8) | collective-permute-done | bytes 67616 | tf_op jit(solution)/shard_map/ppermute | solution.py:307
  117.9 0.6 collective-permute-start.9
  118.4 4.7 %collective-permute-done.9 = f32[1,66,128]{2,1,0:T(8,128)S(1)} collective-permute-done((f32[1,66,128]{2,1,0:T(8,128)S(1)}, f32[1,66,128]{2,1,0:T(8,128)S(1)}, u32[]{:S(2)}, u32[]{:S(2)}) %collective-permute-start.9) | collective-permute-done | bytes 33824 | tf_op jit(solution)/shard_map/ppermute | solution.py:307
  123.1 0.6 fusion
  (9 shorter events, 0.1 us)
Async XLA Ops:
  1.4 74.6 %collective-permute-start.1 = (s32[133]{0:T(256)S(1)}, s32[133]{0:T(256)S(1)}, u32[]{:S(2)}, u32[]{:S(2)}) collective-permute-start(s32[133]{0:T(256)S(1)} %pad_add_fusion.mine_ref), channel_id=1, source_target_pairs={{0,1},{1,0},{2,3},{3,2},{4,5},{5,4},{6,7},{7,6},{8,9},{9,8},{10,11... | collective-permute-start | bytes 1604 | tf_op jit(solution)/shard_map/ppermute | solution.py:307
  1.9 74.1 %copy-start.3 = (bf16[66,128]{1,0:T(8,128)(2,1)S(1)}, bf16[66,128]{1,0:T(8,128)(2,1)}, u32[]{:S(2)}) copy-start(bf16[66,128]{1,0:T(8,128)(2,1)} %param.8) | copy-start | bytes 50692
  1.9 74.1 %collective-permute-start = (bf16[1,66,128]{2,1,0:T(8,128)(2,1)}, bf16[1,66,128]{2,1,0:T(8,128)(2,1)S(1)}, u32[]{:S(2)}, u32[]{:S(2)}) collective-permute-start(bf16[1,66,128]{2,1,0:T(8,128)(2,1)} %bitcast.3), channel_id=1, source_target_pairs={{0,8},{1,9},{2,10},{3,11},{4,12},{5,13},{6,14},{7,15},{8,0},{9,1},... | collective-permute-start | bytes 50696 | tf_op jit(solution)/shard_map/ppermute | solution.py:307
  76.0 12.5 %copy-start = (bf16[592,256]{1,0:T(8,128)(2,1)S(1)}, bf16[592,256]{1,0:T(8,128)(2,1)}, u32[]{:S(2)}) copy-start(bf16[592,256]{1,0:T(8,128)(2,1)} %get-tuple-element.24.rest_0_) | copy-start | bytes 909316
  76.0 12.5 %collective-permute-start.5 = (bf16[17,16,4096]{2,1,0:T(8,128)(2,1)}, bf16[17,16,4096]{2,1,0:T(8,128)(2,1)S(1)}, u32[]{:S(2)}, u32[]{:S(2)}) collective-permute-start(bf16[17,16,4096]{2,1,0:T(8,128)(2,1)} %get-tuple-element.23), channel_id=1, source_target_pairs={{0,1},{1,0},{2,3},{3,2},{4,5},{5,4},{6,7},{7,6},{8,9},{9,8},{10,11... | collective-permute-start | bytes 6684680 | tf_op jit(solution)/shard_map/ppermute | solution.py:307
  76.2 5.4 %collective-permute-start.2 = (bf16[2,66,128]{2,1,0:T(8,128)(2,1)S(1)}, bf16[2,66,128]{2,1,0:T(8,128)(2,1)S(1)}, u32[]{:S(2)}, u32[]{:S(2)}) collective-permute-start(bf16[2,66,128]{2,1,0:T(8,128)(2,1)S(1)} %pad_maximum_fusion.2), channel_id=1, source_target_pairs={{0,4},{1,3},{2,6},{3,1},{4,0},{5,7},{6,2},{7,5},{8,12},{9,11},{10,... | collective-permute-start | bytes 101384 | tf_op jit(solution)/shard_map/ppermute | solution.py:307
  81.6 6.9 %copy-start.1 = (bf16[304,256]{1,0:T(8,128)(2,1)S(1)}, bf16[304,256]{1,0:T(8,128)(2,1)}, u32[]{:S(2)}) copy-start(bf16[304,256]{1,0:T(8,128)(2,1)} %shard_map.83.rest_1_) | copy-start | bytes 466948
  81.6 5.4 %collective-permute-start.3 = (bf16[4,66,128]{2,1,0:T(8,128)(2,1)S(1)}, bf16[4,66,128]{2,1,0:T(8,128)(2,1)S(1)}, u32[]{:S(2)}, u32[]{:S(2)}) collective-permute-start(bf16[4,66,128]{2,1,0:T(8,128)(2,1)S(1)} %pad_maximum_fusion.1), channel_id=1, source_target_pairs={{0,2},{1,5},{2,0},{3,7},{4,6},{5,1},{6,4},{7,3},{8,10},{9,13},{10,... | collective-permute-start | bytes 202760 | tf_op jit(solution)/shard_map/ppermute | solution.py:307
  87.1 1.4 %collective-permute-start.4 = (bf16[8,66,128]{2,1,0:T(8,128)(2,1)S(1)}, bf16[8,66,128]{2,1,0:T(8,128)(2,1)S(1)}, u32[]{:S(2)}, u32[]{:S(2)}) collective-permute-start(bf16[8,66,128]{2,1,0:T(8,128)(2,1)S(1)} %pad_maximum_fusion.own_ref), channel_id=1, source_target_pairs={{0,1},{1,0},{2,3},{3,2},{4,5},{5,4},{6,7},{7,6},{8,9},{9,8},{10,11... | collective-permute-start | bytes 405512 | tf_op jit(solution)/shard_map/ppermute | solution.py:307
  88.5 0.9 copy-start.2
  106.5 1.6 %collective-permute-start.6 = (f32[8,66,128]{2,1,0:T(8,128)S(1)}, f32[8,66,128]{2,1,0:T(8,128)S(1)}, u32[]{:S(2)}, u32[]{:S(2)}) collective-permute-start(f32[8,66,128]{2,1,0:T(8,128)S(1)} %get-tuple-element.28), channel_id=1, source_target_pairs={{0,1},{1,0},{2,3},{3,2},{4,5},{5,4},{6,7},{7,6},{8,9},{9,8},{10,11... | collective-permute-start | bytes 811016 | tf_op jit(solution)/shard_map/ppermute | solution.py:307
  108.2 5.2 %collective-permute-start.7 = (f32[4,66,128]{2,1,0:T(8,128)S(1)}, f32[4,66,128]{2,1,0:T(8,128)S(1)}, u32[]{:S(2)}, u32[]{:S(2)}) collective-permute-start(f32[4,66,128]{2,1,0:T(8,128)S(1)} %slice.25), channel_id=1, source_target_pairs={{0,2},{1,5},{2,0},{3,7},{4,6},{5,1},{6,4},{7,3},{8,10},{9,13},{10,... | collective-permute-start | bytes 405512 | tf_op jit(solution)/shard_map/ppermute | solution.py:307
  113.4 4.4 %collective-permute-start.8 = (f32[2,66,128]{2,1,0:T(8,128)S(1)}, f32[2,66,128]{2,1,0:T(8,128)S(1)}, u32[]{:S(2)}, u32[]{:S(2)}) collective-permute-start(f32[2,66,128]{2,1,0:T(8,128)S(1)} %slice.27), channel_id=1, source_target_pairs={{0,4},{1,3},{2,6},{3,1},{4,0},{5,7},{6,2},{7,5},{8,12},{9,11},{10,... | collective-permute-start | bytes 202760 | tf_op jit(solution)/shard_map/ppermute | solution.py:307
  117.9 5.2 %collective-permute-start.9 = (f32[1,66,128]{2,1,0:T(8,128)S(1)}, f32[1,66,128]{2,1,0:T(8,128)S(1)}, u32[]{:S(2)}, u32[]{:S(2)}) collective-permute-start(f32[1,66,128]{2,1,0:T(8,128)S(1)} %slice.29), channel_id=1, source_target_pairs={{0,8},{1,9},{2,10},{3,11},{4,12},{5,13},{6,14},{7,15},{8,0},{9,1},... | collective-permute-start | bytes 101384 | tf_op jit(solution)/shard_map/ppermute | solution.py:307

commit v4 on v2

--- a/solution.py
+++ b/solution.py
@@ -25,9 +25,11 @@
     return lax.broadcasted_iota(jnp.int32, (rows, LANES), 1) < BLK
 
 
-def gram_kernel(root, start, count, table_ref, pos_ref, flux_ref, out_ref, groups, gram):
+def gram_kernel(root, table_ref, pos_ref, flux_ref, out_ref, groups, gram):
     terms, pixels = table_ref.shape
-    sources = pos_ref.shape[1]
+    channels, sources = pos_ref.shape
+    count = channels // 2
+    start = lax.axis_index("tile") % 2 * count
     n_groups = pixels // PIXELS
     tall = groups.shape[0] // n_groups
     rows = up(terms, 8)
@@ -37,14 +39,14 @@
         groups[h * tall : h * tall + terms, :] = table_ref[:, h * PIXELS : (h + 1) * PIXELS]
     pixel = lax.broadcasted_iota(jnp.int32, (PIXELS, sources), 0)
     for f in range(count):
-        pos = pos_ref[start + f : start + f + 1, :]
+        pos = pos_ref[pl.ds(start + f, 1), :]
         hot = jnp.where(pixel == pos % PIXELS, 1.0, 0.0).astype(BF)
         found = jnp.dot(groups[...], hot, preferred_element_type=F32)
         group = pos // PIXELS
         chosen = jnp.zeros((tall, sources), F32)
         for h in range(n_groups):
             chosen = jnp.where(group == h, found[h * tall : (h + 1) * tall], chosen)
-        scaled = chosen * (flux_ref[start + f : start + f + 1, :] / root)
+        scaled = chosen * (flux_ref[pl.ds(start + f, 1), :] / root)
         high = scaled.astype(BF)
         low = (scaled - high.astype(F32)).astype(BF)
         chosen = chosen.astype(BF)
@@ -57,13 +59,14 @@
     out_ref[:, LANES : 2 * LANES] = (value - high.astype(F32)).astype(BF)
 
 
-def gram_of(zernike_table, positions, source_flux, start, count):
+def gram_of(zernike_table, positions, source_flux):
     terms, pixels = zernike_table.shape
-    sources = positions.shape[1]
+    channels, sources = positions.shape
+    count = channels // 2
     rows, tall = up(terms, 8), up(terms, 16)
     height = up(count * rows + 8, 16)
     return pl.pallas_call(
-        functools.partial(gram_kernel, math.sqrt(sources), start, count),
+        functools.partial(gram_kernel, math.sqrt(sources)),
         out_shape=jax.ShapeDtypeStruct((height, 2 * LANES), BF),
         in_specs=[pl.BlockSpec(memory_space=pltpu.VMEM)] * 3,
         out_specs=pl.BlockSpec(memory_space=pltpu.VMEM),
@@ -78,18 +81,16 @@
     )(zernike_table, positions, source_flux)
 
 
-def reverse_bits(value, bits):
-    result = value & 0
-    for bit in range(bits):
-        result = result | ((value >> bit) & 1) << (bits - 1 - bit)
-    return result
+def relative_place(device, here):
+    apart = device ^ here
+    return 8 * (apart & 1) + (apart & 6) + (apart >> 3)
 
 
 def tiles_kernel(
-    relative_bits, unroll, scale,
-    mine_ref, other_ref, own_ref, got_ref, first_gram_ref, second_gram_ref, vis_hbm, more_hbm,
+    relative, unroll, scale,
+    mine_ref, other_ref, own_ref, got_ref, vis_hbm, more_hbm, own_gram_ref, got_gram_ref,
     keep_ref, send_ref,
-    vis, stage, spread, both, turned, right, left, row_sum, col_sum, sems,
+    vis, stage, spread, both, gram, turned, right, left, row_sum, col_sum, sems,
 ):
     slots, channels = vis.shape[0], vis.shape[1]
     kept = slots - more_hbm.shape[0]
@@ -108,6 +109,7 @@
     row_sum[...] = jnp.zeros_like(row_sum)
     col_sum[...] = jnp.zeros_like(col_sum)
     both[...] = jnp.zeros_like(both)
+    per_tile = stage.shape[1] // LANES
     spread[...] = jnp.zeros_like(spread)
 
     for part, ref in enumerate((own_ref, got_ref)):
@@ -117,11 +119,16 @@
             block = ref[r]
             both[chunk, 0:terms, lanes] = block
             both[chunk, LANES : LANES + terms, lanes] = block
-            buf = where % 2
-            spread[buf, 0:terms, :] = block.astype(F32)
-            stage[buf, 0:LANES, :] = spread[buf].T
-            pieces = [stage[buf, pl.ds(start, BLK // 2, stride=2), :] for start in (0, 1, BLK, BLK + 1)]
-            sorted_rows = jnp.concatenate(pieces, 0)
+            spread[where, 0:terms, :] = block.astype(F32)
+            buf, base = where // per_tile, where % per_tile * LANES
+            stage[buf, base : base + LANES, :] = spread[where].T
+            sorted_rows = jnp.concatenate(
+                [
+                    stage[buf, pl.ds(base + start, BLK // 2, stride=2), :]
+                    for start in (0, 1, BLK, BLK + 1)
+                ],
+                0,
+            )
             turned[2 * where] = sorted_rows[0:BLK].astype(BF)
             turned[2 * where + 1] = sorted_rows[BLK:].astype(BF)
             back = sorted_rows.T.astype(BF)
@@ -129,17 +136,21 @@
             both[chunk, 0:LANES, lanes] = back
             both[chunk, LANES:, lanes] = back
 
+    here = lax.axis_index("tile")
+    gram[here % 2] = own_gram_ref[...]
+    gram[1 - here % 2] = got_gram_ref[...]
     low_r = low_lanes(tall)
     low_l = low_lanes(2 * rows)
 
-    @pl.loop(0, half)
+    @pl.loop(0, half, unroll=4)
     def _(chunk):
         weights = both[chunk]
         for p in range(0, pairs, 2):
-            gram_ref = first_gram_ref if p < pairs // 2 else second_gram_ref
             start = p % (pairs // 2) * 2 * rows
             found = jnp.dot(
-                gram_ref[start : start + 4 * rows + 16, :], weights, preferred_element_type=F32
+                gram[p // (pairs // 2), start : start + 4 * rows + 16, :],
+                weights,
+                preferred_element_type=F32,
             )
             for side in range(2):
                 block = 4 * chunk + 2 * side
@@ -160,12 +171,9 @@
     row_dish = row_pos % (BLK // 2) * 2 + row_pos // (BLK // 2)
     ahead = lax.broadcasted_iota(jnp.int32, (BLK, LANES), 1) % BLK - row_dish
     low = low_lanes(BLK // 2)
-    here = lax.axis_index("tile") if relative_bits else 0
 
     def place(block):
-        if not relative_bits:
-            return block
-        return 2 * reverse_bits((block >> 1) ^ here, relative_bits) + (block & 1)
+        return 2 * relative_place(block >> 1, here) + (block & 1) if relative else block
 
     for copy in copies:
         copy.wait()
@@ -221,12 +229,15 @@
 
     low_out = low_lanes(rows)
     for where in range(2 * half):
-        buf = where % 2
+        buf, base = where // per_tile, where % per_tile * LANES
         for side in range(2):
             total = row_sum[2 * where + side]
-            stage[buf, pl.ds(side * BLK, BLK // 2, stride=2), :] = total[0 : BLK // 2]
-            stage[buf, pl.ds(side * BLK + 1, BLK // 2, stride=2), :] = total[BLK // 2 :]
-        from_rows = stage[buf, 0:LANES, :].T[0:rows]
+            start = base + side * BLK
+            stage[buf, pl.ds(start, BLK // 2, stride=2), :] = total[0 : BLK // 2]
+            stage[buf, pl.ds(start + 1, BLK // 2, stride=2), :] = total[BLK // 2 :]
+    for where in range(2 * half):
+        buf, base = where // per_tile, where % per_tile * LANES
+        from_rows = stage[buf, base : base + LANES, :].T[0:rows]
         cols = []
         for side in range(2):
             total = col_sum[2 * where + side]
@@ -239,7 +250,7 @@
             send_ref[where - half] = result
 
 
-def tile_terms(relative_bits, scale, mine, other, own, got, grams, observed, more):
+def tile_terms(relative, scale, mine, other, own, got, own_gram, got_gram, observed, more):
     slots, channels, _ = observed.shape
     half, terms, _ = own.shape
     rows, tall = up(terms, 8), up(terms, 16)
@@ -249,15 +260,16 @@
     vmem = pl.BlockSpec(memory_space=pltpu.VMEM)
     out = jax.ShapeDtypeStruct((half, terms, LANES), F32)
     return pl.pallas_call(
-        functools.partial(tiles_kernel, relative_bits, unroll, scale),
+        functools.partial(tiles_kernel, relative, unroll, scale),
         out_shape=(out, out),
-        in_specs=[smem, smem, vmem, vmem, vmem, vmem] + [pl.BlockSpec(memory_space=pl.ANY)] * 2,
+        in_specs=[smem, smem, vmem, vmem] + [pl.BlockSpec(memory_space=pl.ANY)] * 2 + [vmem] * 2,
         out_specs=(vmem, vmem),
         scratch_shapes=[
             pltpu.VMEM((slots, channels, BLK * BLK), BF),
-            pltpu.VMEM((max(unroll, 2), channels * BLK // 2, LANES), F32),
-            pltpu.VMEM((2, LANES, LANES), F32),
+            pltpu.VMEM((up(max(unroll, 2 * half * LANES // (channels * BLK // 2)), 1), channels * BLK // 2, LANES), F32),
+            pltpu.VMEM((2 * half, LANES, LANES), F32),
             pltpu.VMEM((half, 2 * LANES, 4 * LANES), BF),
+            pltpu.VMEM((2,) + own_gram.shape, BF),
             pltpu.VMEM((blocks, BLK, LANES), BF),
             pltpu.VMEM((blocks, tall, channels * BLK), BF),
             pltpu.VMEM((blocks, 2 * rows, channels // 2 * BLK), BF),
@@ -269,11 +281,11 @@
         cost_estimate=pl.CostEstimate(
             flops=6 * slots * channels * BLK * BLK * terms, bytes_accessed=observed.size * 2, transcendentals=0
         ),
-    )(mine, other, own, got, *grams, observed, more)
-
-
-def from_partner(array, bit):
-    return lax.ppermute(array, "tile", [(i, i ^ 1 << bit) for i in range(lax.axis_size("tile"))])
+    )(mine, other, own, got, observed, more, own_gram, got_gram)
+
+
+def from_partner(array, mask):
+    return lax.ppermute(array, "tile", [(i, i ^ mask) for i in range(lax.axis_size("tile"))])
 
 
 def on_device(
@@ -284,33 +296,34 @@
     dishes = members * shard
     scale = 1.0 / math.sqrt(dishes * positions.shape[0])
     channels, slots = positions.shape[0], tile_rows.shape[0]
-    bits = members.bit_length() - 1
     moved = slots // 4 + 1
     mine = jnp.concatenate([tile_rows, tile_cols, tile_count])
-    other = from_partner(mine, 0)
-    more = from_partner(observed[slots - moved :], 0)
-    grams = [
-        gram_of(zernike_table, positions, source_flux, start, channels // 2)
-        for start in (0, channels // 2)
-    ]
-    if shard == LANES and members == 1 << bits:
+    to_move = observed[slots - moved :]
+    own_gram = gram_of(zernike_table, positions, source_flux)
+    if shard == LANES and members == 16:
         held = coefficients[None]
-        for step, bit in enumerate(reversed(range(1, bits))):
-            held = jnp.concatenate([held, from_partner(held, bit)], 0)
-            if step < 2:
-                held, grams[step] = lax.optimization_barrier((held, grams[step]))
-        got = from_partner(held, 0)
-        total, sent = tile_terms(bits, scale, mine, other, held, got, grams, observed, more)
-        total = total + from_partner(sent, 0)
-        for bit in range(1, bits):
-            half = total.shape[0] // 2
-            total = total[:half] + from_partner(total[half:], bit)
+        held = jnp.concatenate([held, from_partner(held, 8)], 0)
+        held, to_move, mine = lax.optimization_barrier((held, to_move, mine))
+        more, other = from_partner(to_move, 1), from_partner(mine, 1)
+        got_gram = from_partner(own_gram, 1)
+        held = jnp.concatenate([held] + [from_partner(held, mask) for mask in (2, 4, 6)], 0)
+        held, got_gram, other = lax.optimization_barrier((held, got_gram, other))
+        got = from_partner(held, 1)
+        total, sent = tile_terms(
+            True, scale, mine, other, held, got, own_gram, got_gram, observed, more
+        )
+        total = total + from_partner(sent, 1)
+        total = sum(
+            [from_partner(total[mask : mask + 2], mask) for mask in (2, 4, 6)], total[:2]
+        )
+        total = total[:1] + from_partner(total[1:], 8)
         return total[0]
+    more, other, got_gram = (from_partner(array, 1) for array in (to_move, mine, own_gram))
     everything = lax.all_gather(coefficients, "tile", axis=1, tiled=True)
     everything = everything.reshape(terms, dishes // LANES, LANES).transpose(1, 0, 2)
     half = everything.shape[0] // 2
     parts = tile_terms(
-        0, scale, mine, other, everything[:half], everything[half:], grams, observed, more
+        False, scale, mine, other, everything[:half], everything[half:], own_gram, got_gram, observed, more
     )
     total = jnp.concatenate(parts, 0).transpose(1, 0, 2).reshape(terms, dishes)
     return lax.psum_scatter(total, "tile", scatter_dimension=1, tiled=True)

time: 58.3 us -> 52.3 us (0.90); the launches traced: 57.9 us -> 52.7 us
  Pallas kernels: 24.6 us -> 19.5 us
  waiting for transfers between devices: 15.3 us -> 12.1 us
  starting transfers between devices: 14.5 us -> 16.9 us
  other arithmetic: 0.78 us -> 1.46 us
    pallas_call x3 -> x2, Pallas kernels: 24.6 us -> 19.5 us  [the longest x1 15.7 us: tile_terms(): pl.pallas_call(functools.partial(tiles_kernel, relative, unroll, scale),...]
    ppermute x10 -> x13, waiting for transfers between devices: 15.3 us -> 12.1 us  [from_partner(): lax.ppermute(array, 'tile', [(i, i ^ mask) for i in range(lax.axis_size('...]
    ppermute x10 -> x13, starting transfers between devices: 14.5 us -> 16.9 us  [from_partner(): lax.ppermute(array, 'tile', [(i, i ^ mask) for i in range(lax.axis_size('...]
    concatenate x1, other arithmetic: 0.08 us -> 0.75 us  [on_device(): mine = jnp.concatenate([tile_rows, tile_cols, tile_count])]
    slice x4 -> x3, local copies, waits for them, and re-layouts: 1.86 us -> 1.86 us  [the longest x1 1.84 us: on_device(): to_move = observed[slots - moved:]]
  transfers between devices with their start and end apart: 10 -> 13, of which waited for: 6 -> 9; matrix products, arithmetic and copies ran while one was open for 0% -> 5% of each run, Pallas kernels for 13% -> 7%
where the time goes in v4:
time: 52.3 us; the launch traced here: 52.7 us
  Pallas kernels  19.5 us (37%)
  starting transfers between devices  16.9 us (32%)
  waiting for transfers between devices  12.1 us (23%)
  local copies, waits for them, and re-layouts  1.88 us (4%)
  other arithmetic  1.46 us (3%)
  between operations  0.8 us (2%)
    ppermute x13, starting transfers between devices, from_partner(): lax.ppermute(array, 'tile', [(i, i ^ mask) for i in range(lax.axis_size('...  16.9 us
    pallas_call x1, Pallas kernels, tile_terms(): pl.pallas_call(functools.partial(tiles_kernel, relative, unroll, scale),...  15.7 us
    ppermute x13, waiting for transfers between devices, from_partner(): lax.ppermute(array, 'tile', [(i, i ^ mask) for i in range(lax.axis_size('...  12.1 us
    pallas_call x1, Pallas kernels, gram_of(): pl.pallas_call(functools.partial(gram_kernel, math.sqrt(sources)), out_sh...  3.83 us
    slice x1, local copies, waits for them, and re-layouts, on_device(): to_move = observed[slots - moved:]  1.84 us
  transfers between devices with their start and end apart: 13, of which 9 were waited for; matrix products, arithmetic and copies ran while one was open for 5% of the time, Pallas kernels for 7%

profile of v4, /device:TPU:0, one launch (start us, length us, event | category | flops | bytes accessed | tf_op | source)
XLA Modules:
  0.0 52.7 jit_solution(4666574143454572251)
XLA Ops:
  0.0 4.0 %collective-permute-start = (bf16[1,66,128]{2,1,0:T(8,128)(2,1)}, bf16[1,66,128]{2,1,0:T(8,128)(2,1)S(1)}, u32[]{:S(2)}, u32[]{:S(2)}) collective-permute-start(bf16[1,66,128]{2,1,0:T(8,128)(2,1)} %bitcast.3), channel_id=1, source_target_pairs={{0,8},{1,9},{2,10},{3,11},{4,12},{5,13},{6,14},{7,15},{8,0},{9,1},... | collective-permute-start | bytes 50696 | tf_op jit(solution)/shard_map/ppermute | solution.py:288
  4.7 0.7 %pad_add_fusion.mine_ref = s32[133]{0:T(256)S(1)} fusion(s32[1]{0:T(128)S(6)} %copy.9, s32[66]{0:T(128)} %param.14, s32[66]{0:T(128)} %param.13), kind=kLoop, calls=%fused_computation.7 | loop fusion | flops 266 | bytes 1064 | tf_op jit(solution)/shard_map/concatenate | solution.py:300
  5.4 0.0 copy-start.3
  5.4 0.0 copy-start
  5.4 0.0 copy-start.1
  5.4 0.0 copy-start.2
  5.5 1.8 %slice.21 = bf16[17,16,4096]{2,1,0:T(8,128)(2,1)S(1)} slice(bf16[66,16,4096]{2,1,0:T(8,128)(2,1)} %vis_hbm.1), slice={[49:66], [0:16], [0:4096]} | slice | bytes 4456448 | tf_op jit(solution)/shard_map/slice | solution.py:301
  7.3 0.0 collective-permute-done
  7.3 0.0 copy-done.3
  7.3 0.1 collective-permute-start.7
  7.4 0.0 copy-done
  7.4 0.0 copy-done.1
  7.4 0.0 copy-done.2
  7.4 3.8 %shard_map.82.own_gram_ref = bf16[592,256]{1,0:T(8,128)(2,1)S(1)} custom-call(bf16[66,4096]{1,0:T(8,128)(2,1)S(1)} %copy-done, s32[16,256]{1,0:T(8,128)S(1)} %copy-done.1, f32[16,256]{1,0:T(8,128)S(1)} %copy-done.2), custom_call_target="tpu_custom_call" | custom-call | flops 1107296256 | bytes 1048576 | tf_op jit(solution)/shard_map/pallas_call | solution.py:68
  11.3 0.5 %collective-permute-start.4 = (bf16[592,256]{1,0:T(8,128)(2,1)S(1)}, bf16[592,256]{1,0:T(8,128)(2,1)S(1)}, u32[]{:S(2)}, u32[]{:S(2)}) collective-permute-start(bf16[592,256]{1,0:T(8,128)(2,1)S(1)} %shard_map.82.own_gram_ref), channel_id=1, source_target_pairs={{0,1},{1,0},{2,3},{3,2},{4,5},{5,4},{6,7},{7,6},{8,9},{9,8},{10,11... | collective-permute-start | bytes 909320 | tf_op jit(solution)/shard_map/ppermute | solution.py:288
  11.8 2.5 %collective-permute-start.3 = (bf16[2,66,128]{2,1,0:T(8,128)(2,1)S(1)}, bf16[2,66,128]{2,1,0:T(8,128)(2,1)S(1)}, u32[]{:S(2)}, u32[]{:S(2)}) collective-permute-start(bf16[2,66,128]{2,1,0:T(8,128)(2,1)S(1)} %pad_maximum_fusion.1), channel_id=1, source_target_pairs={{0,6},{1,7},{2,4},{3,5},{4,2},{5,3},{6,0},{7,1},{8,14},{9,15},{10,... | collective-permute-start | bytes 101384 | tf_op jit(solution)/shard_map/ppermute | solution.py:288
  14.4 0.4 collective-permute-start.2
  14.8 0.5 collective-permute-start.1
  15.3 1.4 %collective-permute-done.3 = bf16[2,66,128]{2,1,0:T(8,128)(2,1)S(1)} collective-permute-done((bf16[2,66,128]{2,1,0:T(8,128)(2,1)S(1)}, bf16[2,66,128]{2,1,0:T(8,128)(2,1)S(1)}, u32[]{:S(2)}, u32[]{:S(2)}) %collective-permute-start.3) | collective-permute-done | bytes 33824 | tf_op jit(solution)/shard_map/ppermute | solution.py:288
  16.7 0.0 collective-permute-start.5
  16.7 1.6 %collective-permute-done.2 = bf16[2,66,128]{2,1,0:T(8,128)(2,1)S(1)} collective-permute-done((bf16[2,66,128]{2,1,0:T(8,128)(2,1)S(1)}, bf16[2,66,128]{2,1,0:T(8,128)(2,1)S(1)}, u32[]{:S(2)}, u32[]{:S(2)}) %collective-permute-start.2) | collective-permute-done | bytes 33824 | tf_op jit(solution)/shard_map/ppermute | solution.py:288
  18.3 0.4 collective-permute-done.1
  18.8 0.0 collective-permute-done.5.other_ref
  18.8 0.0 collective-permute-done.4.got_gram_ref
  18.8 0.1 collective-permute-start.6
  18.9 1.4 %collective-permute-done.6.got_ref = bf16[8,66,128]{2,1,0:T(8,128)(2,1)S(1)} collective-permute-done((bf16[8,66,128]{2,1,0:T(8,128)(2,1)S(1)}, bf16[8,66,128]{2,1,0:T(8,128)(2,1)S(1)}, u32[]{:S(2)}, u32[]{:S(2)}) %collective-permute-start.6) | collective-permute-done | bytes 135200 | tf_op jit(solution)/shard_map/ppermute | solution.py:288
  20.2 0.0 collective-permute-done.7.more_hbm
  20.3 15.7 %shard_map.83 = (f32[8,66,128]{2,1,0:T(8,128)S(1)}, f32[8,66,128]{2,1,0:T(8,128)S(1)}) custom-call(s32[133]{0:T(256)S(1)} %pad_add_fusion.mine_ref, s32[133]{0:T(256)S(1)} %collective-permute-done.5.other_ref, bf16[8,66,128]{2,1,0:T(8,128)(2,1)S(1)} %pad_maximum_fusion.own_ref, bf16[8,66,128]{2,1,0:T(8,128)(2,1)S(1)} %collective-permute-done.6.got_ref, ...), custom_call_target="tpu_custom_call" | custom-call | flops 1712848896 | bytes 8650752 | tf_op jit(solution)/shard_map/pallas_call | solution.py:262
  36.0 0.2 collective-permute-start.8
  36.2 1.4 %collective-permute-done.8 = f32[8,66,128]{2,1,0:T(8,128)S(1)} collective-permute-done((f32[8,66,128]{2,1,0:T(8,128)S(1)}, f32[8,66,128]{2,1,0:T(8,128)S(1)}, u32[]{:S(2)}, u32[]{:S(2)}) %collective-permute-start.8) | collective-permute-done | bytes 270368 | tf_op jit(solution)/shard_map/ppermute | solution.py:288
  37.7 0.6 %collective-permute-start.9 = (f32[2,66,128]{2,1,0:T(8,128)S(1)}, f32[2,66,128]{2,1,0:T(8,128)S(1)}, u32[]{:S(2)}, u32[]{:S(2)}) collective-permute-start(f32[2,66,128]{2,1,0:T(8,128)S(1)} %get-tuple-element.21), channel_id=1, source_target_pairs={{0,2},{1,3},{2,0},{3,1},{4,6},{5,7},{6,4},{7,5},{8,10},{9,11},{10,... | collective-permute-start | bytes 202760 | tf_op jit(solution)/shard_map/ppermute | solution.py:288
  38.3 2.5 %collective-permute-start.11 = (f32[2,66,128]{2,1,0:T(8,128)S(1)}, f32[2,66,128]{2,1,0:T(8,128)S(1)}, u32[]{:S(2)}, u32[]{:S(2)}) collective-permute-start(f32[2,66,128]{2,1,0:T(8,128)S(1)} %get-tuple-element.22), channel_id=1, source_target_pairs={{0,6},{1,7},{2,4},{3,5},{4,2},{5,3},{6,0},{7,1},{8,14},{9,15},{10,... | collective-permute-start | bytes 202760 | tf_op jit(solution)/shard_map/ppermute | solution.py:288
  40.8 0.4 collective-permute-start.10
  41.2 2.0 %collective-permute-done.9 = f32[2,66,128]{2,1,0:T(8,128)S(1)} collective-permute-done((f32[2,66,128]{2,1,0:T(8,128)S(1)}, f32[2,66,128]{2,1,0:T(8,128)S(1)}, u32[]{:S(2)}, u32[]{:S(2)}) %collective-permute-start.9) | collective-permute-done | bytes 67616 | tf_op jit(solution)/shard_map/ppermute | solution.py:288
  43.2 0.9 %collective-permute-done.11 = f32[2,66,128]{2,1,0:T(8,128)S(1)} collective-permute-done((f32[2,66,128]{2,1,0:T(8,128)S(1)}, f32[2,66,128]{2,1,0:T(8,128)S(1)}, u32[]{:S(2)}, u32[]{:S(2)}) %collective-permute-start.11) | collective-permute-done | bytes 67616 | tf_op jit(solution)/shard_map/ppermute | solution.py:288
  44.1 1.0 %collective-permute-done.10 = f32[2,66,128]{2,1,0:T(8,128)S(1)} collective-permute-done((f32[2,66,128]{2,1,0:T(8,128)S(1)}, f32[2,66,128]{2,1,0:T(8,128)S(1)}, u32[]{:S(2)}, u32[]{:S(2)}) %collective-permute-start.10) | collective-permute-done | bytes 67616 | tf_op jit(solution)/shard_map/ppermute | solution.py:288
  45.2 4.9 %collective-permute-start.12 = (f32[1,66,128]{2,1,0:T(8,128)S(1)}, f32[1,66,128]{2,1,0:T(8,128)S(1)}, u32[]{:S(2)}, u32[]{:S(2)}) collective-permute-start(f32[1,66,128]{2,1,0:T(8,128)S(1)} %slice.33), channel_id=1, source_target_pairs={{0,8},{1,9},{2,10},{3,11},{4,12},{5,13},{6,14},{7,15},{8,0},{9,1},... | collective-permute-start | bytes 101384 | tf_op jit(solution)/shard_map/ppermute | solution.py:288
  50.1 1.9 %collective-permute-done.12 = f32[1,66,128]{2,1,0:T(8,128)S(1)} collective-permute-done((f32[1,66,128]{2,1,0:T(8,128)S(1)}, f32[1,66,128]{2,1,0:T(8,128)S(1)}, u32[]{:S(2)}, u32[]{:S(2)}) %collective-permute-start.12) | collective-permute-done | bytes 33824 | tf_op jit(solution)/shard_map/ppermute | solution.py:288
  52.0 0.6 %fusion.2 = f32[66,128]{1,0:T(8,128)} fusion(f32[1,66,128]{2,1,0:T(8,128)S(1)} %collective-permute-done.12, f32[2,66,128]{2,1,0:T(8,128)S(1)} %fusion.1), kind=kLoop, calls=%fused_computation.5 | loop fusion | flops 8448 | bytes 101376 | tf_op jit(solution)/shard_map/squeeze | solution.py:320
  (6 shorter events, 0.1 us)
Async XLA Ops:
  0.0 7.3 %collective-permute-start = (bf16[1,66,128]{2,1,0:T(8,128)(2,1)}, bf16[1,66,128]{2,1,0:T(8,128)(2,1)S(1)}, u32[]{:S(2)}, u32[]{:S(2)}) collective-permute-start(bf16[1,66,128]{2,1,0:T(8,128)(2,1)} %bitcast.3), channel_id=1, source_target_pairs={{0,8},{1,9},{2,10},{3,11},{4,12},{5,13},{6,14},{7,15},{8,0},{9,1},... | collective-permute-start | bytes 50696 | tf_op jit(solution)/shard_map/ppermute | solution.py:288
  5.4 1.9 %copy-start.3 = (bf16[66,128]{1,0:T(8,128)(2,1)S(1)}, bf16[66,128]{1,0:T(8,128)(2,1)}, u32[]{:S(2)}) copy-start(bf16[66,128]{1,0:T(8,128)(2,1)} %param.8) | copy-start | bytes 50692
  5.4 2.0 %copy-start = (bf16[66,4096]{1,0:T(8,128)(2,1)S(1)}, bf16[66,4096]{1,0:T(8,128)(2,1)}, u32[]{:S(2)}) copy-start(bf16[66,4096]{1,0:T(8,128)(2,1)} %table_ref.1) | copy-start | bytes 1622020
  5.4 2.0 %copy-start.1 = (s32[16,256]{1,0:T(8,128)S(1)}, s32[16,256]{1,0:T(8,128)}, u32[]{:S(2)}) copy-start(s32[16,256]{1,0:T(8,128)} %pos_ref.1) | copy-start | bytes 49156
  5.4 2.0 %copy-start.2 = (f32[16,256]{1,0:T(8,128)S(1)}, f32[16,256]{1,0:T(8,128)}, u32[]{:S(2)}) copy-start(f32[16,256]{1,0:T(8,128)} %flux_ref.1) | copy-start | bytes 49156
  7.3 12.9 %collective-permute-start.7 = (bf16[17,16,4096]{2,1,0:T(8,128)(2,1)S(1)}, bf16[17,16,4096]{2,1,0:T(8,128)(2,1)S(1)}, u32[]{:S(2)}, u32[]{:S(2)}) collective-permute-start(bf16[17,16,4096]{2,1,0:T(8,128)(2,1)S(1)} %slice.21), channel_id=1, source_target_pairs={{0,1},{1,0},{2,3},{3,2},{4,5},{5,4},{6,7},{7,6},{8,9},{9,8},{10,11... | collective-permute-start | bytes 6684680 | tf_op jit(solution)/shard_map/ppermute | solution.py:288
  11.3 7.5 %collective-permute-start.4 = (bf16[592,256]{1,0:T(8,128)(2,1)S(1)}, bf16[592,256]{1,0:T(8,128)(2,1)S(1)}, u32[]{:S(2)}, u32[]{:S(2)}) collective-permute-start(bf16[592,256]{1,0:T(8,128)(2,1)S(1)} %shard_map.82.own_gram_ref), channel_id=1, source_target_pairs={{0,1},{1,0},{2,3},{3,2},{4,5},{5,4},{6,7},{7,6},{8,9},{9,8},{10,11... | collective-permute-start | bytes 909320 | tf_op jit(solution)/shard_map/ppermute | solution.py:288
  11.8 4.9 %collective-permute-start.3 = (bf16[2,66,128]{2,1,0:T(8,128)(2,1)S(1)}, bf16[2,66,128]{2,1,0:T(8,128)(2,1)S(1)}, u32[]{:S(2)}, u32[]{:S(2)}) collective-permute-start(bf16[2,66,128]{2,1,0:T(8,128)(2,1)S(1)} %pad_maximum_fusion.1), channel_id=1, source_target_pairs={{0,6},{1,7},{2,4},{3,5},{4,2},{5,3},{6,0},{7,1},{8,14},{9,15},{10,... | collective-permute-start | bytes 101384 | tf_op jit(solution)/shard_map/ppermute | solution.py:288
  14.4 4.0 %collective-permute-start.2 = (bf16[2,66,128]{2,1,0:T(8,128)(2,1)S(1)}, bf16[2,66,128]{2,1,0:T(8,128)(2,1)S(1)}, u32[]{:S(2)}, u32[]{:S(2)}) collective-permute-start(bf16[2,66,128]{2,1,0:T(8,128)(2,1)S(1)} %pad_maximum_fusion.1), channel_id=1, source_target_pairs={{0,4},{1,5},{2,6},{3,7},{4,0},{5,1},{6,2},{7,3},{8,12},{9,13},{10,... | collective-permute-start | bytes 101384 | tf_op jit(solution)/shard_map/ppermute | solution.py:288
  14.8 4.0 %collective-permute-start.1 = (bf16[2,66,128]{2,1,0:T(8,128)(2,1)S(1)}, bf16[2,66,128]{2,1,0:T(8,128)(2,1)S(1)}, u32[]{:S(2)}, u32[]{:S(2)}) collective-permute-start(bf16[2,66,128]{2,1,0:T(8,128)(2,1)S(1)} %pad_maximum_fusion.1), channel_id=1, source_target_pairs={{0,2},{1,3},{2,0},{3,1},{4,6},{5,7},{6,4},{7,5},{8,10},{9,11},{10,... | collective-permute-start | bytes 101384 | tf_op jit(solution)/shard_map/ppermute | solution.py:288
  16.7 2.1 %collective-permute-start.5 = (s32[133]{0:T(256)S(1)}, s32[133]{0:T(256)S(1)}, u32[]{:S(2)}, u32[]{:S(2)}) collective-permute-start(s32[133]{0:T(256)S(1)} %pad_add_fusion.mine_ref), channel_id=1, source_target_pairs={{0,1},{1,0},{2,3},{3,2},{4,5},{5,4},{6,7},{7,6},{8,9},{9,8},{10,11... | collective-permute-start | bytes 1604 | tf_op jit(solution)/shard_map/ppermute | solution.py:288
  18.8 1.4 %collective-permute-start.6 = (bf16[8,66,128]{2,1,0:T(8,128)(2,1)S(1)}, bf16[8,66,128]{2,1,0:T(8,128)(2,1)S(1)}, u32[]{:S(2)}, u32[]{:S(2)}) collective-permute-start(bf16[8,66,128]{2,1,0:T(8,128)(2,1)S(1)} %pad_maximum_fusion.own_ref), channel_id=1, source_target_pairs={{0,1},{1,0},{2,3},{3,2},{4,5},{5,4},{6,7},{7,6},{8,9},{9,8},{10,11... | collective-permute-start | bytes 405512 | tf_op jit(solution)/shard_map/ppermute | solution.py:288
  36.0 1.6 %collective-permute-start.8 = (f32[8,66,128]{2,1,0:T(8,128)S(1)}, f32[8,66,128]{2,1,0:T(8,128)S(1)}, u32[]{:S(2)}, u32[]{:S(2)}) collective-permute-start(f32[8,66,128]{2,1,0:T(8,128)S(1)} %get-tuple-element.20), channel_id=1, source_target_pairs={{0,1},{1,0},{2,3},{3,2},{4,5},{5,4},{6,7},{7,6},{8,9},{9,8},{10,11... | collective-permute-start | bytes 811016 | tf_op jit(solution)/shard_map/ppermute | solution.py:288
  37.7 5.5 %collective-permute-start.9 = (f32[2,66,128]{2,1,0:T(8,128)S(1)}, f32[2,66,128]{2,1,0:T(8,128)S(1)}, u32[]{:S(2)}, u32[]{:S(2)}) collective-permute-start(f32[2,66,128]{2,1,0:T(8,128)S(1)} %get-tuple-element.21), channel_id=1, source_target_pairs={{0,2},{1,3},{2,0},{3,1},{4,6},{5,7},{6,4},{7,5},{8,10},{9,11},{10,... | collective-permute-start | bytes 202760 | tf_op jit(solution)/shard_map/ppermute | solution.py:288
  38.3 5.9 %collective-permute-start.11 = (f32[2,66,128]{2,1,0:T(8,128)S(1)}, f32[2,66,128]{2,1,0:T(8,128)S(1)}, u32[]{:S(2)}, u32[]{:S(2)}) collective-permute-start(f32[2,66,128]{2,1,0:T(8,128)S(1)} %get-tuple-element.22), channel_id=1, source_target_pairs={{0,6},{1,7},{2,4},{3,5},{4,2},{5,3},{6,0},{7,1},{8,14},{9,15},{10,... | collective-permute-start | bytes 202760 | tf_op jit(solution)/shard_map/ppermute | solution.py:288
  40.8 4.4 %collective-permute-start.10 = (f32[2,66,128]{2,1,0:T(8,128)S(1)}, f32[2,66,128]{2,1,0:T(8,128)S(1)}, u32[]{:S(2)}, u32[]{:S(2)}) collective-permute-start(f32[2,66,128]{2,1,0:T(8,128)S(1)} %get-tuple-element.23), channel_id=1, source_target_pairs={{0,4},{1,5},{2,6},{3,7},{4,0},{5,1},{6,2},{7,3},{8,12},{9,13},{10,... | collective-permute-start | bytes 202760 | tf_op jit(solution)/shard_map/ppermute | solution.py:288
  45.2 6.9 %collective-permute-start.12 = (f32[1,66,128]{2,1,0:T(8,128)S(1)}, f32[1,66,128]{2,1,0:T(8,128)S(1)}, u32[]{:S(2)}, u32[]{:S(2)}) collective-permute-start(f32[1,66,128]{2,1,0:T(8,128)S(1)} %slice.33), channel_id=1, source_target_pairs={{0,8},{1,9},{2,10},{3,11},{4,12},{5,13},{6,14},{7,15},{8,0},{9,1},... | collective-permute-start | bytes 101384 | tf_op jit(solution)/shard_map/ppermute | solution.py:288

commit v5 on v4

--- a/solution.py
+++ b/solution.py
@@ -38,21 +38,25 @@
     for h in range(n_groups):
         groups[h * tall : h * tall + terms, :] = table_ref[:, h * PIXELS : (h + 1) * PIXELS]
     pixel = lax.broadcasted_iota(jnp.int32, (PIXELS, sources), 0)
-    for f in range(count):
-        pos = pos_ref[pl.ds(start + f, 1), :]
-        hot = jnp.where(pixel == pos % PIXELS, 1.0, 0.0).astype(BF)
+    for f in range(0, count, count):
+        positions = [pos_ref[pl.ds(start + f + e, 1), :] for e in range(count)]
+        hot = jnp.concatenate(
+            [jnp.where(pixel == pos % PIXELS, 1.0, 0.0).astype(BF) for pos in positions], 1
+        )
         found = jnp.dot(groups[...], hot, preferred_element_type=F32)
-        group = pos // PIXELS
-        chosen = jnp.zeros((tall, sources), F32)
-        for h in range(n_groups):
-            chosen = jnp.where(group == h, found[h * tall : (h + 1) * tall], chosen)
-        scaled = chosen * (flux_ref[pl.ds(start + f, 1), :] / root)
-        high = scaled.astype(BF)
-        low = (scaled - high.astype(F32)).astype(BF)
-        chosen = chosen.astype(BF)
-        product = lax.dot_general(high, chosen, NT, preferred_element_type=F32)
-        product = product + lax.dot_general(low, chosen, NT, preferred_element_type=F32)
-        gram[f * rows : f * rows + tall, 0:tall] = product
+        for e, pos in enumerate(positions):
+            group = pos // PIXELS
+            chosen = jnp.zeros((tall, sources), F32)
+            for h in range(n_groups):
+                part = found[h * tall : (h + 1) * tall, e * sources : (e + 1) * sources]
+                chosen = jnp.where(group == h, part, chosen)
+            scaled = chosen * (flux_ref[pl.ds(start + f + e, 1), :] / root)
+            high = scaled.astype(BF)
+            low = (scaled - high.astype(F32)).astype(BF)
+            chosen = chosen.astype(BF)
+            product = lax.dot_general(high, chosen, NT, preferred_element_type=F32)
+            product = product + lax.dot_general(low, chosen, NT, preferred_element_type=F32)
+            gram[(f + e) * rows : (f + e) * rows + tall, 0:tall] = product
     value = gram[...]
     high = value.astype(BF)
     out_ref[:, 0:LANES] = high
@@ -303,7 +307,7 @@
     if shard == LANES and members == 16:
         held = coefficients[None]
         held = jnp.concatenate([held, from_partner(held, 8)], 0)
-        held, to_move, mine = lax.optimization_barrier((held, to_move, mine))
+        held, own_gram = lax.optimization_barrier((held, own_gram))
         more, other = from_partner(to_move, 1), from_partner(mine, 1)
         got_gram = from_partner(own_gram, 1)
         held = jnp.concatenate([held] + [from_partner(held, mask) for mask in (2, 4, 6)], 0)

time: 52.3 us -> 50.1 us (0.958); the launches traced: 52.7 us -> 49.9 us
  starting transfers between devices: 16.9 us -> 14.5 us
  waiting for transfers between devices: 12.1 us -> 14.4 us
  Pallas kernels: 19.5 us -> 17.6 us
  other arithmetic: 1.46 us -> 0.79 us
    ppermute x13, starting transfers between devices: 16.9 us -> 14.5 us  [from_partner(): lax.ppermute(array, 'tile', [(i, i ^ mask) for i in range(lax.axis_size('...]
    ppermute x13, waiting for transfers between devices: 12.1 us -> 14.4 us  [from_partner(): lax.ppermute(array, 'tile', [(i, i ^ mask) for i in range(lax.axis_size('...]
    pallas_call x1, Pallas kernels: 3.83 us -> 1.87 us  [gram_of(): pl.pallas_call(functools.partial(gram_kernel, math.sqrt(sources)), out_sh...]
    concatenate x1, other arithmetic: 0.75 us -> 0.08 us  [on_device(): mine = jnp.concatenate([tile_rows, tile_cols, tile_count])]
  transfers between devices with their start and end apart: 13 -> 13, of which waited for: 9 -> 8; matrix products, arithmetic and copies ran while one was open for 5% -> 0% of each run, Pallas kernels for 7% -> 4%
where the time goes in v5:
time: 50.1 us; the launch traced here: 49.9 us
  Pallas kernels  17.6 us (35%)
  starting transfers between devices  14.5 us (29%)
  waiting for transfers between devices  14.4 us (29%)
  local copies, waits for them, and re-layouts  1.88 us (4%)
  other arithmetic  0.79 us (2%)
  between operations  0.76 us (2%)
    pallas_call x1, Pallas kernels, tile_terms(): pl.pallas_call(functools.partial(tiles_kernel, relative, unroll, scale),...  15.7 us
    ppermute x13, starting transfers between devices, from_partner(): lax.ppermute(array, 'tile', [(i, i ^ mask) for i in range(lax.axis_size('...  14.5 us
    ppermute x13, waiting for transfers between devices, from_partner(): lax.ppermute(array, 'tile', [(i, i ^ mask) for i in range(lax.axis_size('...  14.4 us
    pallas_call x1, Pallas kernels, gram_of(): pl.pallas_call(functools.partial(gram_kernel, math.sqrt(sources)), out_sh...  1.87 us
    slice x1, local copies, waits for them, and re-layouts, on_device(): to_move = observed[slots - moved:]  1.83 us
  transfers between devices with their start and end apart: 13, of which 8 were waited for; matrix products, arithmetic and copies ran while one was open for 0% of the time, Pallas kernels for 4%

profile of v5, /device:TPU:0, one launch (start us, length us, event | category | flops | bytes accessed | tf_op | source)
XLA Modules:
  0.0 49.9 jit_solution(17218728606062250422)
XLA Ops:
  0.0 0.0 copy-start.3
  0.0 0.0 copy-start.2
  0.0 0.0 copy-start.1
  0.0 0.0 copy-start
  0.0 1.8 %slice.21 = bf16[17,16,4096]{2,1,0:T(8,128)(2,1)S(1)} slice(bf16[66,16,4096]{2,1,0:T(8,128)(2,1)} %vis_hbm.1), slice={[49:66], [0:16], [0:4096]} | slice | bytes 4456448 | tf_op jit(solution)/shard_map/slice | solution.py:305
  1.8 0.0 copy-start.4
  1.9 0.0 copy-start.5
  1.9 0.5 %collective-permute-start.7 = (bf16[17,16,4096]{2,1,0:T(8,128)(2,1)S(1)}, bf16[17,16,4096]{2,1,0:T(8,128)(2,1)S(1)}, u32[]{:S(2)}, u32[]{:S(2)}) collective-permute-start(bf16[17,16,4096]{2,1,0:T(8,128)(2,1)S(1)} %slice.21), channel_id=1, source_target_pairs={{0,1},{1,0},{2,3},{3,2},{4,5},{5,4},{6,7},{7,6},{8,9},{9,8},{10,11... | collective-permute-start | bytes 6684680 | tf_op jit(solution)/shard_map/ppermute | solution.py:292
  2.4 0.0 copy-done.3
  2.4 3.7 %collective-permute-start = (bf16[1,66,128]{2,1,0:T(8,128)(2,1)S(1)}, bf16[1,66,128]{2,1,0:T(8,128)(2,1)S(1)}, u32[]{:S(2)}, u32[]{:S(2)}) collective-permute-start(bf16[1,66,128]{2,1,0:T(8,128)(2,1)S(1)} %bitcast.3), channel_id=1, source_target_pairs={{0,8},{1,9},{2,10},{3,11},{4,12},{5,13},{6,14},{7,15},{8,0},{9,1},... | collective-permute-start | bytes 50696 | tf_op jit(solution)/shard_map/ppermute | solution.py:292
  6.1 0.0 copy-done.2
  6.1 0.0 copy-done.1
  6.1 0.0 copy-done
  6.1 1.9 %shard_map.82.own_gram_ref = bf16[592,256]{1,0:T(8,128)(2,1)S(1)} custom-call(bf16[66,4096]{1,0:T(8,128)(2,1)S(1)} %copy-done, s32[16,256]{1,0:T(8,128)S(1)} %copy-done.1, f32[16,256]{1,0:T(8,128)S(1)} %copy-done.2), custom_call_target="tpu_custom_call" | custom-call | flops 1107296256 | bytes 1048576 | tf_op jit(solution)/shard_map/pallas_call | solution.py:72
  8.0 0.0 collective-permute-done
  8.0 0.2 collective-permute-start.4
  8.9 2.6 %collective-permute-start.3 = (bf16[2,66,128]{2,1,0:T(8,128)(2,1)S(1)}, bf16[2,66,128]{2,1,0:T(8,128)(2,1)S(1)}, u32[]{:S(2)}, u32[]{:S(2)}) collective-permute-start(bf16[2,66,128]{2,1,0:T(8,128)(2,1)S(1)} %pad_maximum_fusion.1), channel_id=1, source_target_pairs={{0,6},{1,7},{2,4},{3,5},{4,2},{5,3},{6,0},{7,1},{8,14},{9,15},{10,... | collective-permute-start | bytes 101384 | tf_op jit(solution)/shard_map/ppermute | solution.py:292
  11.5 0.4 collective-permute-start.2
  11.9 0.5 %collective-permute-start.1 = (bf16[2,66,128]{2,1,0:T(8,128)(2,1)S(1)}, bf16[2,66,128]{2,1,0:T(8,128)(2,1)S(1)}, u32[]{:S(2)}, u32[]{:S(2)}) collective-permute-start(bf16[2,66,128]{2,1,0:T(8,128)(2,1)S(1)} %pad_maximum_fusion.1), channel_id=1, source_target_pairs={{0,2},{1,3},{2,0},{3,1},{4,6},{5,7},{6,4},{7,5},{8,10},{9,11},{10,... | collective-permute-start | bytes 101384 | tf_op jit(solution)/shard_map/ppermute | solution.py:292
  12.4 0.0 copy-done.4
  12.4 0.0 copy-done.5
  12.4 0.1 pad_add_fusion.mine_ref
  12.5 1.3 %collective-permute-done.3 = bf16[2,66,128]{2,1,0:T(8,128)(2,1)S(1)} collective-permute-done((bf16[2,66,128]{2,1,0:T(8,128)(2,1)S(1)}, bf16[2,66,128]{2,1,0:T(8,128)(2,1)S(1)}, u32[]{:S(2)}, u32[]{:S(2)}) %collective-permute-start.3) | collective-permute-done | bytes 33824 | tf_op jit(solution)/shard_map/ppermute | solution.py:292
  13.8 0.0 collective-permute-start.5
  13.8 1.6 %collective-permute-done.2 = bf16[2,66,128]{2,1,0:T(8,128)(2,1)S(1)} collective-permute-done((bf16[2,66,128]{2,1,0:T(8,128)(2,1)S(1)}, bf16[2,66,128]{2,1,0:T(8,128)(2,1)S(1)}, u32[]{:S(2)}, u32[]{:S(2)}) %collective-permute-start.2) | collective-permute-done | bytes 33824 | tf_op jit(solution)/shard_map/ppermute | solution.py:292
  15.4 0.4 collective-permute-done.1
  15.9 0.0 collective-permute-done.5.other_ref
  15.9 0.0 collective-permute-done.4.got_gram_ref
  15.9 0.1 collective-permute-start.6
  16.0 1.4 %collective-permute-done.6.got_ref = bf16[8,66,128]{2,1,0:T(8,128)(2,1)S(1)} collective-permute-done((bf16[8,66,128]{2,1,0:T(8,128)(2,1)S(1)}, bf16[8,66,128]{2,1,0:T(8,128)(2,1)S(1)}, u32[]{:S(2)}, u32[]{:S(2)}) %collective-permute-start.6) | collective-permute-done | bytes 135200 | tf_op jit(solution)/shard_map/ppermute | solution.py:292
  17.4 0.0 collective-permute-done.7.more_hbm
  17.4 15.7 %shard_map.83 = (f32[8,66,128]{2,1,0:T(8,128)S(1)}, f32[8,66,128]{2,1,0:T(8,128)S(1)}) custom-call(s32[133]{0:T(256)S(1)} %pad_add_fusion.mine_ref, s32[133]{0:T(256)S(1)} %collective-permute-done.5.other_ref, bf16[8,66,128]{2,1,0:T(8,128)(2,1)S(1)} %pad_maximum_fusion.own_ref, bf16[8,66,128]{2,1,0:T(8,128)(2,1)S(1)} %collective-permute-done.6.got_ref, ...), custom_call_target="tpu_custom_call" | custom-call | flops 1712848896 | bytes 8650752 | tf_op jit(solution)/shard_map/pallas_call | solution.py:266
  33.1 0.2 collective-permute-start.8
  33.3 1.5 %collective-permute-done.8 = f32[8,66,128]{2,1,0:T(8,128)S(1)} collective-permute-done((f32[8,66,128]{2,1,0:T(8,128)S(1)}, f32[8,66,128]{2,1,0:T(8,128)S(1)}, u32[]{:S(2)}, u32[]{:S(2)}) %collective-permute-start.8) | collective-permute-done | bytes 270368 | tf_op jit(solution)/shard_map/ppermute | solution.py:292
  34.8 0.6 %collective-permute-start.9 = (f32[2,66,128]{2,1,0:T(8,128)S(1)}, f32[2,66,128]{2,1,0:T(8,128)S(1)}, u32[]{:S(2)}, u32[]{:S(2)}) collective-permute-start(f32[2,66,128]{2,1,0:T(8,128)S(1)} %get-tuple-element.19), channel_id=1, source_target_pairs={{0,2},{1,3},{2,0},{3,1},{4,6},{5,7},{6,4},{7,5},{8,10},{9,11},{10,... | collective-permute-start | bytes 202760 | tf_op jit(solution)/shard_map/ppermute | solution.py:292
  35.4 4.5 %collective-permute-start.11 = (f32[2,66,128]{2,1,0:T(8,128)S(1)}, f32[2,66,128]{2,1,0:T(8,128)S(1)}, u32[]{:S(2)}, u32[]{:S(2)}) collective-permute-start(f32[2,66,128]{2,1,0:T(8,128)S(1)} %get-tuple-element.20), channel_id=1, source_target_pairs={{0,6},{1,7},{2,4},{3,5},{4,2},{5,3},{6,0},{7,1},{8,14},{9,15},{10,... | collective-permute-start | bytes 202760 | tf_op jit(solution)/shard_map/ppermute | solution.py:292
  39.9 0.5 collective-permute-start.10
  40.4 0.0 collective-permute-done.9
  40.4 2.1 %collective-permute-done.11 = f32[2,66,128]{2,1,0:T(8,128)S(1)} collective-permute-done((f32[2,66,128]{2,1,0:T(8,128)S(1)}, f32[2,66,128]{2,1,0:T(8,128)S(1)}, u32[]{:S(2)}, u32[]{:S(2)}) %collective-permute-start.11) | collective-permute-done | bytes 67616 | tf_op jit(solution)/shard_map/ppermute | solution.py:292
  42.6 1.8 %collective-permute-done.10 = f32[2,66,128]{2,1,0:T(8,128)S(1)} collective-permute-done((f32[2,66,128]{2,1,0:T(8,128)S(1)}, f32[2,66,128]{2,1,0:T(8,128)S(1)}, u32[]{:S(2)}, u32[]{:S(2)}) %collective-permute-start.10) | collective-permute-done | bytes 67616 | tf_op jit(solution)/shard_map/ppermute | solution.py:292
  44.4 0.6 %collective-permute-start.12 = (f32[1,66,128]{2,1,0:T(8,128)S(1)}, f32[1,66,128]{2,1,0:T(8,128)S(1)}, u32[]{:S(2)}, u32[]{:S(2)}) collective-permute-start(f32[1,66,128]{2,1,0:T(8,128)S(1)} %slice.33), channel_id=1, source_target_pairs={{0,8},{1,9},{2,10},{3,11},{4,12},{5,13},{6,14},{7,15},{8,0},{9,1},... | collective-permute-start | bytes 101384 | tf_op jit(solution)/shard_map/ppermute | solution.py:292
  44.9 4.3 %collective-permute-done.12 = f32[1,66,128]{2,1,0:T(8,128)S(1)} collective-permute-done((f32[1,66,128]{2,1,0:T(8,128)S(1)}, f32[1,66,128]{2,1,0:T(8,128)S(1)}, u32[]{:S(2)}, u32[]{:S(2)}) %collective-permute-start.12) | collective-permute-done | bytes 33824 | tf_op jit(solution)/shard_map/ppermute | solution.py:292
  49.3 0.6 %fusion.2 = f32[66,128]{1,0:T(8,128)} fusion(f32[1,66,128]{2,1,0:T(8,128)S(1)} %collective-permute-done.12, f32[2,66,128]{2,1,0:T(8,128)S(1)} %fusion.1), kind=kLoop, calls=%fused_computation.5 | loop fusion | flops 8448 | bytes 101376 | tf_op jit(solution)/shard_map/squeeze | solution.py:324
  (6 shorter events, 0.1 us)
Async XLA Ops:
  0.0 2.4 %copy-start.3 = (bf16[66,128]{1,0:T(8,128)(2,1)S(1)}, bf16[66,128]{1,0:T(8,128)(2,1)}, u32[]{:S(2)}) copy-start(bf16[66,128]{1,0:T(8,128)(2,1)} %param.8) | copy-start | bytes 50692
  0.0 6.1 %copy-start.2 = (f32[16,256]{1,0:T(8,128)S(1)}, f32[16,256]{1,0:T(8,128)}, u32[]{:S(2)}) copy-start(f32[16,256]{1,0:T(8,128)} %flux_ref.1) | copy-start | bytes 49156
  0.0 6.1 %copy-start.1 = (s32[16,256]{1,0:T(8,128)S(1)}, s32[16,256]{1,0:T(8,128)}, u32[]{:S(2)}) copy-start(s32[16,256]{1,0:T(8,128)} %pos_ref.1) | copy-start | bytes 49156
  0.0 6.1 %copy-start = (bf16[66,4096]{1,0:T(8,128)(2,1)S(1)}, bf16[66,4096]{1,0:T(8,128)(2,1)}, u32[]{:S(2)}) copy-start(bf16[66,4096]{1,0:T(8,128)(2,1)} %table_ref.1) | copy-start | bytes 1622020
  1.8 10.6 %copy-start.4 = (s32[66]{0:T(128)S(1)}, s32[66]{0:T(128)}, u32[]{:S(2)}) copy-start(s32[66]{0:T(128)} %param.14) | copy-start | bytes 796
  1.9 10.6 %copy-start.5 = (s32[66]{0:T(128)S(1)}, s32[66]{0:T(128)}, u32[]{:S(2)}) copy-start(s32[66]{0:T(128)} %param.13) | copy-start | bytes 796
  1.9 15.5 %collective-permute-start.7 = (bf16[17,16,4096]{2,1,0:T(8,128)(2,1)S(1)}, bf16[17,16,4096]{2,1,0:T(8,128)(2,1)S(1)}, u32[]{:S(2)}, u32[]{:S(2)}) collective-permute-start(bf16[17,16,4096]{2,1,0:T(8,128)(2,1)S(1)} %slice.21), channel_id=1, source_target_pairs={{0,1},{1,0},{2,3},{3,2},{4,5},{5,4},{6,7},{7,6},{8,9},{9,8},{10,11... | collective-permute-start | bytes 6684680 | tf_op jit(solution)/shard_map/ppermute | solution.py:292
  2.4 5.6 %collective-permute-start = (bf16[1,66,128]{2,1,0:T(8,128)(2,1)S(1)}, bf16[1,66,128]{2,1,0:T(8,128)(2,1)S(1)}, u32[]{:S(2)}, u32[]{:S(2)}) collective-permute-start(bf16[1,66,128]{2,1,0:T(8,128)(2,1)S(1)} %bitcast.3), channel_id=1, source_target_pairs={{0,8},{1,9},{2,10},{3,11},{4,12},{5,13},{6,14},{7,15},{8,0},{9,1},... | collective-permute-start | bytes 50696 | tf_op jit(solution)/shard_map/ppermute | solution.py:292
  8.0 7.9 %collective-permute-start.4 = (bf16[592,256]{1,0:T(8,128)(2,1)S(1)}, bf16[592,256]{1,0:T(8,128)(2,1)S(1)}, u32[]{:S(2)}, u32[]{:S(2)}) collective-permute-start(bf16[592,256]{1,0:T(8,128)(2,1)S(1)} %shard_map.82.own_gram_ref), channel_id=1, source_target_pairs={{0,1},{1,0},{2,3},{3,2},{4,5},{5,4},{6,7},{7,6},{8,9},{9,8},{10,11... | collective-permute-start | bytes 909320 | tf_op jit(solution)/shard_map/ppermute | solution.py:292
  8.9 4.9 %collective-permute-start.3 = (bf16[2,66,128]{2,1,0:T(8,128)(2,1)S(1)}, bf16[2,66,128]{2,1,0:T(8,128)(2,1)S(1)}, u32[]{:S(2)}, u32[]{:S(2)}) collective-permute-start(bf16[2,66,128]{2,1,0:T(8,128)(2,1)S(1)} %pad_maximum_fusion.1), channel_id=1, source_target_pairs={{0,6},{1,7},{2,4},{3,5},{4,2},{5,3},{6,0},{7,1},{8,14},{9,15},{10,... | collective-permute-start | bytes 101384 | tf_op jit(solution)/shard_map/ppermute | solution.py:292
  11.5 4.0 %collective-permute-start.2 = (bf16[2,66,128]{2,1,0:T(8,128)(2,1)S(1)}, bf16[2,66,128]{2,1,0:T(8,128)(2,1)S(1)}, u32[]{:S(2)}, u32[]{:S(2)}) collective-permute-start(bf16[2,66,128]{2,1,0:T(8,128)(2,1)S(1)} %pad_maximum_fusion.1), channel_id=1, source_target_pairs={{0,4},{1,5},{2,6},{3,7},{4,0},{5,1},{6,2},{7,3},{8,12},{9,13},{10,... | collective-permute-start | bytes 101384 | tf_op jit(solution)/shard_map/ppermute | solution.py:292
  11.9 4.0 %collective-permute-start.1 = (bf16[2,66,128]{2,1,0:T(8,128)(2,1)S(1)}, bf16[2,66,128]{2,1,0:T(8,128)(2,1)S(1)}, u32[]{:S(2)}, u32[]{:S(2)}) collective-permute-start(bf16[2,66,128]{2,1,0:T(8,128)(2,1)S(1)} %pad_maximum_fusion.1), channel_id=1, source_target_pairs={{0,2},{1,3},{2,0},{3,1},{4,6},{5,7},{6,4},{7,5},{8,10},{9,11},{10,... | collective-permute-start | bytes 101384 | tf_op jit(solution)/shard_map/ppermute | solution.py:292
  13.8 2.1 %collective-permute-start.5 = (s32[133]{0:T(256)S(1)}, s32[133]{0:T(256)S(1)}, u32[]{:S(2)}, u32[]{:S(2)}) collective-permute-start(s32[133]{0:T(256)S(1)} %pad_add_fusion.mine_ref), channel_id=1, source_target_pairs={{0,1},{1,0},{2,3},{3,2},{4,5},{5,4},{6,7},{7,6},{8,9},{9,8},{10,11... | collective-permute-start | bytes 1604 | tf_op jit(solution)/shard_map/ppermute | solution.py:292
  15.9 1.4 %collective-permute-start.6 = (bf16[8,66,128]{2,1,0:T(8,128)(2,1)S(1)}, bf16[8,66,128]{2,1,0:T(8,128)(2,1)S(1)}, u32[]{:S(2)}, u32[]{:S(2)}) collective-permute-start(bf16[8,66,128]{2,1,0:T(8,128)(2,1)S(1)} %pad_maximum_fusion.own_ref), channel_id=1, source_target_pairs={{0,1},{1,0},{2,3},{3,2},{4,5},{5,4},{6,7},{7,6},{8,9},{9,8},{10,11... | collective-permute-start | bytes 405512 | tf_op jit(solution)/shard_map/ppermute | solution.py:292
  33.1 1.6 %collective-permute-start.8 = (f32[8,66,128]{2,1,0:T(8,128)S(1)}, f32[8,66,128]{2,1,0:T(8,128)S(1)}, u32[]{:S(2)}, u32[]{:S(2)}) collective-permute-start(f32[8,66,128]{2,1,0:T(8,128)S(1)} %get-tuple-element.18), channel_id=1, source_target_pairs={{0,1},{1,0},{2,3},{3,2},{4,5},{5,4},{6,7},{7,6},{8,9},{9,8},{10,11... | collective-permute-start | bytes 811016 | tf_op jit(solution)/shard_map/ppermute | solution.py:292
  34.8 5.6 %collective-permute-start.9 = (f32[2,66,128]{2,1,0:T(8,128)S(1)}, f32[2,66,128]{2,1,0:T(8,128)S(1)}, u32[]{:S(2)}, u32[]{:S(2)}) collective-permute-start(f32[2,66,128]{2,1,0:T(8,128)S(1)} %get-tuple-element.19), channel_id=1, source_target_pairs={{0,2},{1,3},{2,0},{3,1},{4,6},{5,7},{6,4},{7,5},{8,10},{9,11},{10,... | collective-permute-start | bytes 202760 | tf_op jit(solution)/shard_map/ppermute | solution.py:292
  35.4 7.1 %collective-permute-start.11 = (f32[2,66,128]{2,1,0:T(8,128)S(1)}, f32[2,66,128]{2,1,0:T(8,128)S(1)}, u32[]{:S(2)}, u32[]{:S(2)}) collective-permute-start(f32[2,66,128]{2,1,0:T(8,128)S(1)} %get-tuple-element.20), channel_id=1, source_target_pairs={{0,6},{1,7},{2,4},{3,5},{4,2},{5,3},{6,0},{7,1},{8,14},{9,15},{10,... | collective-permute-start | bytes 202760 | tf_op jit(solution)/shard_map/ppermute | solution.py:292
  39.9 4.4 %collective-permute-start.10 = (f32[2,66,128]{2,1,0:T(8,128)S(1)}, f32[2,66,128]{2,1,0:T(8,128)S(1)}, u32[]{:S(2)}, u32[]{:S(2)}) collective-permute-start(f32[2,66,128]{2,1,0:T(8,128)S(1)} %get-tuple-element.21), channel_id=1, source_target_pairs={{0,4},{1,5},{2,6},{3,7},{4,0},{5,1},{6,2},{7,3},{8,12},{9,13},{10,... | collective-permute-start | bytes 202760 | tf_op jit(solution)/shard_map/ppermute | solution.py:292
  44.4 4.9 %collective-permute-start.12 = (f32[1,66,128]{2,1,0:T(8,128)S(1)}, f32[1,66,128]{2,1,0:T(8,128)S(1)}, u32[]{:S(2)}, u32[]{:S(2)}) collective-permute-start(f32[1,66,128]{2,1,0:T(8,128)S(1)} %slice.33), channel_id=1, source_target_pairs={{0,8},{1,9},{2,10},{3,11},{4,12},{5,13},{6,14},{7,15},{8,0},{9,1},... | collective-permute-start | bytes 101384 | tf_op jit(solution)/shard_map/ppermute | solution.py:292

commit v6 on v5

--- a/solution.py
+++ b/solution.py
@@ -9,6 +9,7 @@
 from jax.sharding import PartitionSpec as P
 
 BLK = 64
+PITCH = 18
 UNROLL = 7
 LANES = 128
 PIXELS = 256
@@ -196,7 +197,7 @@
             leasts.append(jnp.where(turn < n_live, jnp.where(row == col, 0, -BLK), BLK))
         for u, slot in enumerate(slot_ids):
             for c in range(BLK // 2):
-                stage[u, c * channels : (c + 1) * channels, :] = vis[
+                stage[u, c * PITCH : c * PITCH + channels, :] = vis[
                     slot, :, c * LANES : (c + 1) * LANES
                 ].astype(F32)
         models = [
@@ -207,15 +208,16 @@
             keep = ahead > leasts[u]
             residual = []
             for p in range(pairs):
-                first = stage[u, pl.ds(2 * p, BLK // 2, stride=channels), :]
-                second = stage[u, pl.ds(2 * p + 1, BLK // 2, stride=channels), :]
+                first = stage[u, pl.ds(2 * p, BLK // 2, stride=PITCH), :]
+                second = stage[u, pl.ds(2 * p + 1, BLK // 2, stride=PITCH), :]
+                first, second = first.astype(BF), second.astype(BF)
                 seen = jnp.concatenate(
                     [
-                        jnp.where(low, first, pltpu.roll(second, BLK, 1)),
-                        jnp.where(low, pltpu.roll(first, BLK, 1), second),
+                        jnp.concatenate([first[:, :BLK], second[:, :BLK]], 1),
+                        jnp.concatenate([first[:, BLK:], second[:, BLK:]], 1),
                     ],
                     0,
-                )
+                ).astype(F32)
                 difference = models[u][:, p * LANES : (p + 1) * LANES] - seen
                 residual.append(jnp.where(keep, difference, 0.0).astype(BF))
             residuals.append(residual)
@@ -270,7 +272,7 @@
         out_specs=(vmem, vmem),
         scratch_shapes=[
             pltpu.VMEM((slots, channels, BLK * BLK), BF),
-            pltpu.VMEM((up(max(unroll, 2 * half * LANES // (channels * BLK // 2)), 1), channels * BLK // 2, LANES), F32),
+            pltpu.VMEM((max(unroll, -(-2 * half // (PITCH * BLK // 2 // LANES))), PITCH * BLK // 2, LANES), F32),
             pltpu.VMEM((2 * half, LANES, LANES), F32),
             pltpu.VMEM((half, 2 * LANES, 4 * LANES), BF),
             pltpu.VMEM((2,) + own_gram.shape, BF),
@@ -310,7 +312,7 @@
         held, own_gram = lax.optimization_barrier((held, own_gram))
         more, other = from_partner(to_move, 1), from_partner(mine, 1)
         got_gram = from_partner(own_gram, 1)
-        held = jnp.concatenate([held] + [from_partner(held, mask) for mask in (2, 4, 6)], 0)
+        held = jnp.concatenate([held] + [from_partner(held, mask) for mask in (6, 4, 2)][::-1], 0)
         held, got_gram, other = lax.optimization_barrier((held, got_gram, other))
         got = from_partner(held, 1)
         total, sent = tile_terms(
@@ -318,7 +320,7 @@
         )
         total = total + from_partner(sent, 1)
         total = sum(
-            [from_partner(total[mask : mask + 2], mask) for mask in (2, 4, 6)], total[:2]
+            [from_partner(total[mask : mask + 2], mask) for mask in (6, 4, 2)], total[:2]
         )
         total = total[:1] + from_partner(total[1:], 8)
         return total[0]

time: 50.1 us -> 46.2 us (0.922)
  Pallas kernels: 17.6 us -> 15.1 us
  waiting for transfers between devices: 14.4 us -> 12.1 us
  starting transfers between devices: 14.5 us -> 15.5 us
    pallas_call x1, Pallas kernels: 15.7 us -> 13.2 us  [tile_terms(): pl.pallas_call(functools.partial(tiles_kernel, relative, unroll, scale),...]
    ppermute x13, waiting for transfers between devices: 14.4 us -> 12.1 us  [from_partner(): lax.ppermute(array, 'tile', [(i, i ^ mask) for i in range(lax.axis_size('...]
    ppermute x13, starting transfers between devices: 14.5 us -> 15.5 us  [from_partner(): lax.ppermute(array, 'tile', [(i, i ^ mask) for i in range(lax.axis_size('...]
  transfers between devices with their start and end apart: 13 -> 13, of which waited for: 8 -> 9; matrix products, arithmetic and copies ran while one was open for 0% -> 0% of each run, Pallas kernels for 4% -> 4%
where the time goes in v6:
time: 46.2 us; the launch traced here: 46.1 us
  starting transfers between devices  15.5 us (34%)
  Pallas kernels  15.1 us (33%)
  waiting for transfers between devices  12.1 us (26%)
  local copies, waits for them, and re-layouts  1.88 us (4%)
  other arithmetic  0.79 us (2%)
  between operations  0.76 us (2%)
    ppermute x13, starting transfers between devices, from_partner(): lax.ppermute(array, 'tile', [(i, i ^ mask) for i in range(lax.axis_size('...  15.5 us
    pallas_call x1, Pallas kernels, tile_terms(): pl.pallas_call(functools.partial(tiles_kernel, relative, unroll, scale),...  13.2 us
    ppermute x13, waiting for transfers between devices, from_partner(): lax.ppermute(array, 'tile', [(i, i ^ mask) for i in range(lax.axis_size('...  12.1 us
    pallas_call x1, Pallas kernels, gram_of(): pl.pallas_call(functools.partial(gram_kernel, math.sqrt(sources)), out_sh...  1.87 us
    slice x1, local copies, waits for them, and re-layouts, on_device(): to_move = observed[slots - moved:]  1.83 us
  transfers between devices with their start and end apart: 13, of which 9 were waited for; matrix products, arithmetic and copies ran while one was open for 0% of the time, Pallas kernels for 4%

profile of v6, /device:TPU:0, one launch (start us, length us, event | category | flops | bytes accessed | tf_op | source)
XLA Modules:
  0.0 46.1 jit_solution(13585715144602882903)
XLA Ops:
  0.0 0.0 copy-start.3
  0.0 0.0 copy-start.2
  0.0 0.0 copy-start.1
  0.0 0.0 copy-start
  0.0 1.8 %slice.21 = bf16[17,16,4096]{2,1,0:T(8,128)(2,1)S(1)} slice(bf16[66,16,4096]{2,1,0:T(8,128)(2,1)} %vis_hbm.1), slice={[49:66], [0:16], [0:4096]} | slice | bytes 4456448 | tf_op jit(solution)/shard_map/slice | solution.py:307
  1.8 0.0 copy-start.4
  1.9 0.0 copy-start.5
  1.9 0.5 %collective-permute-start.7 = (bf16[17,16,4096]{2,1,0:T(8,128)(2,1)S(1)}, bf16[17,16,4096]{2,1,0:T(8,128)(2,1)S(1)}, u32[]{:S(2)}, u32[]{:S(2)}) collective-permute-start(bf16[17,16,4096]{2,1,0:T(8,128)(2,1)S(1)} %slice.21), channel_id=1, source_target_pairs={{0,1},{1,0},{2,3},{3,2},{4,5},{5,4},{6,7},{7,6},{8,9},{9,8},{10,11... | collective-permute-start | bytes 6684680 | tf_op jit(solution)/shard_map/ppermute | solution.py:294
  2.4 0.0 copy-done.3
  2.4 3.7 %collective-permute-start = (bf16[1,66,128]{2,1,0:T(8,128)(2,1)S(1)}, bf16[1,66,128]{2,1,0:T(8,128)(2,1)S(1)}, u32[]{:S(2)}, u32[]{:S(2)}) collective-permute-start(bf16[1,66,128]{2,1,0:T(8,128)(2,1)S(1)} %bitcast.3), channel_id=1, source_target_pairs={{0,8},{1,9},{2,10},{3,11},{4,12},{5,13},{6,14},{7,15},{8,0},{9,1},... | collective-permute-start | bytes 50696 | tf_op jit(solution)/shard_map/ppermute | solution.py:294
  6.1 0.0 copy-done.2
  6.1 0.0 copy-done.1
  6.1 0.0 copy-done
  6.1 1.9 %shard_map.82.own_gram_ref = bf16[592,256]{1,0:T(8,128)(2,1)S(1)} custom-call(bf16[66,4096]{1,0:T(8,128)(2,1)S(1)} %copy-done, s32[16,256]{1,0:T(8,128)S(1)} %copy-done.1, f32[16,256]{1,0:T(8,128)S(1)} %copy-done.2), custom_call_target="tpu_custom_call" | custom-call | flops 1107296256 | bytes 1048576 | tf_op jit(solution)/shard_map/pallas_call | solution.py:73
  8.0 0.0 collective-permute-done
  8.0 0.2 collective-permute-start.4
  8.9 2.6 %collective-permute-start.3 = (bf16[2,66,128]{2,1,0:T(8,128)(2,1)S(1)}, bf16[2,66,128]{2,1,0:T(8,128)(2,1)S(1)}, u32[]{:S(2)}, u32[]{:S(2)}) collective-permute-start(bf16[2,66,128]{2,1,0:T(8,128)(2,1)S(1)} %pad_maximum_fusion.1), channel_id=1, source_target_pairs={{0,6},{1,7},{2,4},{3,5},{4,2},{5,3},{6,0},{7,1},{8,14},{9,15},{10,... | collective-permute-start | bytes 101384 | tf_op jit(solution)/shard_map/ppermute | solution.py:294
  11.5 0.4 collective-permute-start.2
  11.9 0.5 %collective-permute-start.1 = (bf16[2,66,128]{2,1,0:T(8,128)(2,1)S(1)}, bf16[2,66,128]{2,1,0:T(8,128)(2,1)S(1)}, u32[]{:S(2)}, u32[]{:S(2)}) collective-permute-start(bf16[2,66,128]{2,1,0:T(8,128)(2,1)S(1)} %pad_maximum_fusion.1), channel_id=1, source_target_pairs={{0,2},{1,3},{2,0},{3,1},{4,6},{5,7},{6,4},{7,5},{8,10},{9,11},{10,... | collective-permute-start | bytes 101384 | tf_op jit(solution)/shard_map/ppermute | solution.py:294
  12.4 0.0 copy-done.4
  12.4 0.0 copy-done.5
  12.4 0.1 pad_add_fusion.mine_ref
  12.5 1.3 %collective-permute-done.3 = bf16[2,66,128]{2,1,0:T(8,128)(2,1)S(1)} collective-permute-done((bf16[2,66,128]{2,1,0:T(8,128)(2,1)S(1)}, bf16[2,66,128]{2,1,0:T(8,128)(2,1)S(1)}, u32[]{:S(2)}, u32[]{:S(2)}) %collective-permute-start.3) | collective-permute-done | bytes 33824 | tf_op jit(solution)/shard_map/ppermute | solution.py:294
  13.8 0.0 collective-permute-start.5
  13.8 1.6 %collective-permute-done.2 = bf16[2,66,128]{2,1,0:T(8,128)(2,1)S(1)} collective-permute-done((bf16[2,66,128]{2,1,0:T(8,128)(2,1)S(1)}, bf16[2,66,128]{2,1,0:T(8,128)(2,1)S(1)}, u32[]{:S(2)}, u32[]{:S(2)}) %collective-permute-start.2) | collective-permute-done | bytes 33824 | tf_op jit(solution)/shard_map/ppermute | solution.py:294
  15.4 0.4 collective-permute-done.1
  15.9 0.0 collective-permute-done.5.other_ref
  15.9 0.0 collective-permute-done.4.got_gram_ref
  15.9 0.1 collective-permute-start.6
  16.0 1.4 %collective-permute-done.6.got_ref = bf16[8,66,128]{2,1,0:T(8,128)(2,1)S(1)} collective-permute-done((bf16[8,66,128]{2,1,0:T(8,128)(2,1)S(1)}, bf16[8,66,128]{2,1,0:T(8,128)(2,1)S(1)}, u32[]{:S(2)}, u32[]{:S(2)}) %collective-permute-start.6) | collective-permute-done | bytes 135200 | tf_op jit(solution)/shard_map/ppermute | solution.py:294
  17.4 0.0 collective-permute-done.7.more_hbm
  17.4 13.2 %shard_map.83 = (f32[8,66,128]{2,1,0:T(8,128)S(1)}, f32[8,66,128]{2,1,0:T(8,128)S(1)}) custom-call(s32[133]{0:T(256)S(1)} %pad_add_fusion.mine_ref, s32[133]{0:T(256)S(1)} %collective-permute-done.5.other_ref, bf16[8,66,128]{2,1,0:T(8,128)(2,1)S(1)} %pad_maximum_fusion.own_ref, bf16[8,66,128]{2,1,0:T(8,128)(2,1)S(1)} %collective-permute-done.6.got_ref, ...), custom_call_target="tpu_custom_call" | custom-call | flops 1712848896 | bytes 8650752 | tf_op jit(solution)/shard_map/pallas_call | solution.py:268
  30.6 0.2 collective-permute-start.8
  30.8 1.4 %collective-permute-done.8 = f32[8,66,128]{2,1,0:T(8,128)S(1)} collective-permute-done((f32[8,66,128]{2,1,0:T(8,128)S(1)}, f32[8,66,128]{2,1,0:T(8,128)S(1)}, u32[]{:S(2)}, u32[]{:S(2)}) %collective-permute-start.8) | collective-permute-done | bytes 270368 | tf_op jit(solution)/shard_map/ppermute | solution.py:294
  32.3 1.8 %collective-permute-start.9 = (f32[2,66,128]{2,1,0:T(8,128)S(1)}, f32[2,66,128]{2,1,0:T(8,128)S(1)}, u32[]{:S(2)}, u32[]{:S(2)}) collective-permute-start(f32[2,66,128]{2,1,0:T(8,128)S(1)} %get-tuple-element.19), channel_id=1, source_target_pairs={{0,6},{1,7},{2,4},{3,5},{4,2},{5,3},{6,0},{7,1},{8,14},{9,15},{10,... | collective-permute-start | bytes 202760 | tf_op jit(solution)/shard_map/ppermute | solution.py:294
  34.1 1.3 %collective-permute-start.11 = (f32[2,66,128]{2,1,0:T(8,128)S(1)}, f32[2,66,128]{2,1,0:T(8,128)S(1)}, u32[]{:S(2)}, u32[]{:S(2)}) collective-permute-start(f32[2,66,128]{2,1,0:T(8,128)S(1)} %get-tuple-element.20), channel_id=1, source_target_pairs={{0,2},{1,3},{2,0},{3,1},{4,6},{5,7},{6,4},{7,5},{8,10},{9,11},{10,... | collective-permute-start | bytes 202760 | tf_op jit(solution)/shard_map/ppermute | solution.py:294
  35.4 0.4 collective-permute-start.10
  35.8 1.8 %collective-permute-done.9 = f32[2,66,128]{2,1,0:T(8,128)S(1)} collective-permute-done((f32[2,66,128]{2,1,0:T(8,128)S(1)}, f32[2,66,128]{2,1,0:T(8,128)S(1)}, u32[]{:S(2)}, u32[]{:S(2)}) %collective-permute-start.9) | collective-permute-done | bytes 67616 | tf_op jit(solution)/shard_map/ppermute | solution.py:294
  37.7 1.5 %collective-permute-done.11 = f32[2,66,128]{2,1,0:T(8,128)S(1)} collective-permute-done((f32[2,66,128]{2,1,0:T(8,128)S(1)}, f32[2,66,128]{2,1,0:T(8,128)S(1)}, u32[]{:S(2)}, u32[]{:S(2)}) %collective-permute-start.11) | collective-permute-done | bytes 67616 | tf_op jit(solution)/shard_map/ppermute | solution.py:294
  39.2 0.6 %collective-permute-done.10 = f32[2,66,128]{2,1,0:T(8,128)S(1)} collective-permute-done((f32[2,66,128]{2,1,0:T(8,128)S(1)}, f32[2,66,128]{2,1,0:T(8,128)S(1)}, u32[]{:S(2)}, u32[]{:S(2)}) %collective-permute-start.10) | collective-permute-done | bytes 67616 | tf_op jit(solution)/shard_map/ppermute | solution.py:294
  39.8 3.7 %collective-permute-start.12 = (f32[1,66,128]{2,1,0:T(8,128)S(1)}, f32[1,66,128]{2,1,0:T(8,128)S(1)}, u32[]{:S(2)}, u32[]{:S(2)}) collective-permute-start(f32[1,66,128]{2,1,0:T(8,128)S(1)} %slice.33), channel_id=1, source_target_pairs={{0,8},{1,9},{2,10},{3,11},{4,12},{5,13},{6,14},{7,15},{8,0},{9,1},... | collective-permute-start | bytes 101384 | tf_op jit(solution)/shard_map/ppermute | solution.py:294
  43.5 2.1 %collective-permute-done.12 = f32[1,66,128]{2,1,0:T(8,128)S(1)} collective-permute-done((f32[1,66,128]{2,1,0:T(8,128)S(1)}, f32[1,66,128]{2,1,0:T(8,128)S(1)}, u32[]{:S(2)}, u32[]{:S(2)}) %collective-permute-start.12) | collective-permute-done | bytes 33824 | tf_op jit(solution)/shard_map/ppermute | solution.py:294
  45.5 0.6 %fusion.2 = f32[66,128]{1,0:T(8,128)} fusion(f32[1,66,128]{2,1,0:T(8,128)S(1)} %collective-permute-done.12, f32[2,66,128]{2,1,0:T(8,128)S(1)} %fusion.1), kind=kLoop, calls=%fused_computation.5 | loop fusion | flops 8448 | bytes 101376 | tf_op jit(solution)/shard_map/squeeze | solution.py:326
  (6 shorter events, 0.1 us)
Async XLA Ops:
  0.0 2.4 %copy-start.3 = (bf16[66,128]{1,0:T(8,128)(2,1)S(1)}, bf16[66,128]{1,0:T(8,128)(2,1)}, u32[]{:S(2)}) copy-start(bf16[66,128]{1,0:T(8,128)(2,1)} %param.8) | copy-start | bytes 50692
  0.0 6.1 %copy-start.2 = (f32[16,256]{1,0:T(8,128)S(1)}, f32[16,256]{1,0:T(8,128)}, u32[]{:S(2)}) copy-start(f32[16,256]{1,0:T(8,128)} %flux_ref.1) | copy-start | bytes 49156
  0.0 6.1 %copy-start.1 = (s32[16,256]{1,0:T(8,128)S(1)}, s32[16,256]{1,0:T(8,128)}, u32[]{:S(2)}) copy-start(s32[16,256]{1,0:T(8,128)} %pos_ref.1) | copy-start | bytes 49156
  0.0 6.1 %copy-start = (bf16[66,4096]{1,0:T(8,128)(2,1)S(1)}, bf16[66,4096]{1,0:T(8,128)(2,1)}, u32[]{:S(2)}) copy-start(bf16[66,4096]{1,0:T(8,128)(2,1)} %table_ref.1) | copy-start | bytes 1622020
  1.8 10.6 %copy-start.4 = (s32[66]{0:T(128)S(1)}, s32[66]{0:T(128)}, u32[]{:S(2)}) copy-start(s32[66]{0:T(128)} %param.14) | copy-start | bytes 796
  1.9 10.6 %copy-start.5 = (s32[66]{0:T(128)S(1)}, s32[66]{0:T(128)}, u32[]{:S(2)}) copy-start(s32[66]{0:T(128)} %param.13) | copy-start | bytes 796
  1.9 15.5 %collective-permute-start.7 = (bf16[17,16,4096]{2,1,0:T(8,128)(2,1)S(1)}, bf16[17,16,4096]{2,1,0:T(8,128)(2,1)S(1)}, u32[]{:S(2)}, u32[]{:S(2)}) collective-permute-start(bf16[17,16,4096]{2,1,0:T(8,128)(2,1)S(1)} %slice.21), channel_id=1, source_target_pairs={{0,1},{1,0},{2,3},{3,2},{4,5},{5,4},{6,7},{7,6},{8,9},{9,8},{10,11... | collective-permute-start | bytes 6684680 | tf_op jit(solution)/shard_map/ppermute | solution.py:294
  2.4 5.6 %collective-permute-start = (bf16[1,66,128]{2,1,0:T(8,128)(2,1)S(1)}, bf16[1,66,128]{2,1,0:T(8,128)(2,1)S(1)}, u32[]{:S(2)}, u32[]{:S(2)}) collective-permute-start(bf16[1,66,128]{2,1,0:T(8,128)(2,1)S(1)} %bitcast.3), channel_id=1, source_target_pairs={{0,8},{1,9},{2,10},{3,11},{4,12},{5,13},{6,14},{7,15},{8,0},{9,1},... | collective-permute-start | bytes 50696 | tf_op jit(solution)/shard_map/ppermute | solution.py:294
  8.0 7.9 %collective-permute-start.4 = (bf16[592,256]{1,0:T(8,128)(2,1)S(1)}, bf16[592,256]{1,0:T(8,128)(2,1)S(1)}, u32[]{:S(2)}, u32[]{:S(2)}) collective-permute-start(bf16[592,256]{1,0:T(8,128)(2,1)S(1)} %shard_map.82.own_gram_ref), channel_id=1, source_target_pairs={{0,1},{1,0},{2,3},{3,2},{4,5},{5,4},{6,7},{7,6},{8,9},{9,8},{10,11... | collective-permute-start | bytes 909320 | tf_op jit(solution)/shard_map/ppermute | solution.py:294
  8.9 4.9 %collective-permute-start.3 = (bf16[2,66,128]{2,1,0:T(8,128)(2,1)S(1)}, bf16[2,66,128]{2,1,0:T(8,128)(2,1)S(1)}, u32[]{:S(2)}, u32[]{:S(2)}) collective-permute-start(bf16[2,66,128]{2,1,0:T(8,128)(2,1)S(1)} %pad_maximum_fusion.1), channel_id=1, source_target_pairs={{0,6},{1,7},{2,4},{3,5},{4,2},{5,3},{6,0},{7,1},{8,14},{9,15},{10,... | collective-permute-start | bytes 101384 | tf_op jit(solution)/shard_map/ppermute | solution.py:294
  11.5 4.0 %collective-permute-start.2 = (bf16[2,66,128]{2,1,0:T(8,128)(2,1)S(1)}, bf16[2,66,128]{2,1,0:T(8,128)(2,1)S(1)}, u32[]{:S(2)}, u32[]{:S(2)}) collective-permute-start(bf16[2,66,128]{2,1,0:T(8,128)(2,1)S(1)} %pad_maximum_fusion.1), channel_id=1, source_target_pairs={{0,4},{1,5},{2,6},{3,7},{4,0},{5,1},{6,2},{7,3},{8,12},{9,13},{10,... | collective-permute-start | bytes 101384 | tf_op jit(solution)/shard_map/ppermute | solution.py:294
  11.9 4.0 %collective-permute-start.1 = (bf16[2,66,128]{2,1,0:T(8,128)(2,1)S(1)}, bf16[2,66,128]{2,1,0:T(8,128)(2,1)S(1)}, u32[]{:S(2)}, u32[]{:S(2)}) collective-permute-start(bf16[2,66,128]{2,1,0:T(8,128)(2,1)S(1)} %pad_maximum_fusion.1), channel_id=1, source_target_pairs={{0,2},{1,3},{2,0},{3,1},{4,6},{5,7},{6,4},{7,5},{8,10},{9,11},{10,... | collective-permute-start | bytes 101384 | tf_op jit(solution)/shard_map/ppermute | solution.py:294
  13.8 2.1 %collective-permute-start.5 = (s32[133]{0:T(256)S(1)}, s32[133]{0:T(256)S(1)}, u32[]{:S(2)}, u32[]{:S(2)}) collective-permute-start(s32[133]{0:T(256)S(1)} %pad_add_fusion.mine_ref), channel_id=1, source_target_pairs={{0,1},{1,0},{2,3},{3,2},{4,5},{5,4},{6,7},{7,6},{8,9},{9,8},{10,11... | collective-permute-start | bytes 1604 | tf_op jit(solution)/shard_map/ppermute | solution.py:294
  15.9 1.4 %collective-permute-start.6 = (bf16[8,66,128]{2,1,0:T(8,128)(2,1)S(1)}, bf16[8,66,128]{2,1,0:T(8,128)(2,1)S(1)}, u32[]{:S(2)}, u32[]{:S(2)}) collective-permute-start(bf16[8,66,128]{2,1,0:T(8,128)(2,1)S(1)} %pad_maximum_fusion.own_ref), channel_id=1, source_target_pairs={{0,1},{1,0},{2,3},{3,2},{4,5},{5,4},{6,7},{7,6},{8,9},{9,8},{10,11... | collective-permute-start | bytes 405512 | tf_op jit(solution)/shard_map/ppermute | solution.py:294
  30.6 1.6 %collective-permute-start.8 = (f32[8,66,128]{2,1,0:T(8,128)S(1)}, f32[8,66,128]{2,1,0:T(8,128)S(1)}, u32[]{:S(2)}, u32[]{:S(2)}) collective-permute-start(f32[8,66,128]{2,1,0:T(8,128)S(1)} %get-tuple-element.18), channel_id=1, source_target_pairs={{0,1},{1,0},{2,3},{3,2},{4,5},{5,4},{6,7},{7,6},{8,9},{9,8},{10,11... | collective-permute-start | bytes 811016 | tf_op jit(solution)/shard_map/ppermute | solution.py:294
  32.3 5.4 %collective-permute-start.9 = (f32[2,66,128]{2,1,0:T(8,128)S(1)}, f32[2,66,128]{2,1,0:T(8,128)S(1)}, u32[]{:S(2)}, u32[]{:S(2)}) collective-permute-start(f32[2,66,128]{2,1,0:T(8,128)S(1)} %get-tuple-element.19), channel_id=1, source_target_pairs={{0,6},{1,7},{2,4},{3,5},{4,2},{5,3},{6,0},{7,1},{8,14},{9,15},{10,... | collective-permute-start | bytes 202760 | tf_op jit(solution)/shard_map/ppermute | solution.py:294
  34.1 5.0 %collective-permute-start.11 = (f32[2,66,128]{2,1,0:T(8,128)S(1)}, f32[2,66,128]{2,1,0:T(8,128)S(1)}, u32[]{:S(2)}, u32[]{:S(2)}) collective-permute-start(f32[2,66,128]{2,1,0:T(8,128)S(1)} %get-tuple-element.20), channel_id=1, source_target_pairs={{0,2},{1,3},{2,0},{3,1},{4,6},{5,7},{6,4},{7,5},{8,10},{9,11},{10,... | collective-permute-start | bytes 202760 | tf_op jit(solution)/shard_map/ppermute | solution.py:294
  35.4 4.4 %collective-permute-start.10 = (f32[2,66,128]{2,1,0:T(8,128)S(1)}, f32[2,66,128]{2,1,0:T(8,128)S(1)}, u32[]{:S(2)}, u32[]{:S(2)}) collective-permute-start(f32[2,66,128]{2,1,0:T(8,128)S(1)} %get-tuple-element.21), channel_id=1, source_target_pairs={{0,4},{1,5},{2,6},{3,7},{4,0},{5,1},{6,2},{7,3},{8,12},{9,13},{10,... | collective-permute-start | bytes 202760 | tf_op jit(solution)/shard_map/ppermute | solution.py:294
  39.8 5.7 %collective-permute-start.12 = (f32[1,66,128]{2,1,0:T(8,128)S(1)}, f32[1,66,128]{2,1,0:T(8,128)S(1)}, u32[]{:S(2)}, u32[]{:S(2)}) collective-permute-start(f32[1,66,128]{2,1,0:T(8,128)S(1)} %slice.33), channel_id=1, source_target_pairs={{0,8},{1,9},{2,10},{3,11},{4,12},{5,13},{6,14},{7,15},{8,0},{9,1},... | collective-permute-start | bytes 101384 | tf_op jit(solution)/shard_map/ppermute | solution.py:294

commit v7 on v6

--- a/solution.py
+++ b/solution.py
@@ -20,6 +20,14 @@
 
 def up(size, unit):
     return -(-size // unit) * unit
+
+
+def sorting(size, transposed=False):
+    natural = lax.broadcasted_iota(jnp.int32, (size, size), 1 if transposed else 0)
+    place = lax.broadcasted_iota(jnp.int32, (size, size), 0 if transposed else 1)
+    inside = place % BLK
+    source = place - inside + inside % (BLK // 2) * 2 + inside // (BLK // 2)
+    return jnp.where(natural == source, 1.0, 0.0).astype(BF)
 
 
 def low_lanes(rows):
@@ -95,7 +103,7 @@
     relative, unroll, scale,
     mine_ref, other_ref, own_ref, got_ref, vis_hbm, more_hbm, own_gram_ref, got_gram_ref,
     keep_ref, send_ref,
-    vis, stage, spread, both, gram, turned, right, left, row_sum, col_sum, sems,
+    vis, stage, both, gram, turned, right, left, row_sum, col_sum, sems,
 ):
     slots, channels = vis.shape[0], vis.shape[1]
     kept = slots - more_hbm.shape[0]
@@ -115,31 +123,26 @@
     col_sum[...] = jnp.zeros_like(col_sum)
     both[...] = jnp.zeros_like(both)
     per_tile = stage.shape[1] // LANES
-    spread[...] = jnp.zeros_like(spread)
 
     for part, ref in enumerate((own_ref, got_ref)):
         for r in range(half):
             where = part * half + r
             chunk, lanes = where // 2, slice(where % 2 * LANES, (where % 2 + 1) * LANES)
-            block = ref[r]
-            both[chunk, 0:terms, lanes] = block
-            both[chunk, LANES : LANES + terms, lanes] = block
-            spread[where, 0:terms, :] = block.astype(F32)
-            buf, base = where // per_tile, where % per_tile * LANES
-            stage[buf, base : base + LANES, :] = spread[where].T
-            sorted_rows = jnp.concatenate(
-                [
-                    stage[buf, pl.ds(base + start, BLK // 2, stride=2), :]
-                    for start in (0, 1, BLK, BLK + 1)
-                ],
-                0,
-            )
-            turned[2 * where] = sorted_rows[0:BLK].astype(BF)
-            turned[2 * where + 1] = sorted_rows[BLK:].astype(BF)
-            back = sorted_rows.T.astype(BF)
-            lanes = slice((where % 2 + 2) * LANES, (where % 2 + 3) * LANES)
-            both[chunk, 0:LANES, lanes] = back
-            both[chunk, LANES:, lanes] = back
+            both[chunk, 0:terms, lanes] = ref[r]
+            both[chunk, LANES : LANES + terms, lanes] = ref[r]
+    order, order_of = sorting(2 * LANES), sorting(LANES, True)
+    halves = jnp.concatenate([both[chunk, 0:LANES, 0 : 2 * LANES] for chunk in range(half)], 0)
+    mixed = jnp.dot(halves, order, preferred_element_type=F32).astype(BF)
+    for chunk in range(half):
+        piece = mixed[chunk * LANES : (chunk + 1) * LANES]
+        both[chunk, 0:LANES, 2 * LANES :] = piece
+        both[chunk, LANES:, 2 * LANES :] = piece
+    for chunk in range(half):
+        for side in range(2):
+            block = both[chunk, 0:LANES, side * LANES : (side + 1) * LANES]
+            sorted_rows = lax.dot_general(order_of, block, NT, preferred_element_type=F32).astype(BF)
+            turned[4 * chunk + 2 * side] = sorted_rows[0:BLK]
+            turned[4 * chunk + 2 * side + 1] = sorted_rows[BLK:]
 
     here = lax.axis_index("tile")
     gram[here % 2] = own_gram_ref[...]
@@ -147,7 +150,7 @@
     low_r = low_lanes(tall)
     low_l = low_lanes(2 * rows)
 
-    @pl.loop(0, half, unroll=4)
+    @pl.loop(0, half, unroll=8)
     def _(chunk):
         weights = both[chunk]
         for p in range(0, pairs, 2):
@@ -164,13 +167,15 @@
                     first = part[2 * e * rows : 2 * e * rows + tall]
                     second = part[(2 * e + 1) * rows : (2 * e + 1) * rows + tall]
                     lanes = slice((p + e) * LANES, (p + e + 1) * LANES)
-                    right[block, :, lanes] = jnp.where(low_r, first, pltpu.roll(second, BLK, 1)).astype(BF)
-                    right[block + 1, :, lanes] = jnp.where(low_r, pltpu.roll(first, BLK, 1), second).astype(BF)
+                    first, second = first.astype(BF), second.astype(BF)
+                    right[block, :, lanes] = jnp.concatenate([first[:, :BLK], second[:, :BLK]], 1)
+                    right[block + 1, :, lanes] = jnp.concatenate([first[:, BLK:], second[:, BLK:]], 1)
                 part = found[:, (side + 2) * LANES : (side + 3) * LANES]
                 first, second = part[0 : 2 * rows], part[2 * rows : 4 * rows]
                 lanes = slice(p * BLK, p * BLK + LANES)
-                left[block, :, lanes] = jnp.where(low_l, first, pltpu.roll(second, BLK, 1)).astype(BF)
-                left[block + 1, :, lanes] = jnp.where(low_l, pltpu.roll(first, BLK, 1), second).astype(BF)
+                first, second = first.astype(BF), second.astype(BF)
+                left[block, :, lanes] = jnp.concatenate([first[:, :BLK], second[:, :BLK]], 1)
+                left[block + 1, :, lanes] = jnp.concatenate([first[:, BLK:], second[:, BLK:]], 1)
 
     row_pos = lax.broadcasted_iota(jnp.int32, (BLK, LANES), 0)
     row_dish = row_pos % (BLK // 2) * 2 + row_pos // (BLK // 2)
@@ -244,11 +249,10 @@
     for where in range(2 * half):
         buf, base = where // per_tile, where % per_tile * LANES
         from_rows = stage[buf, base : base + LANES, :].T[0:rows]
-        cols = []
-        for side in range(2):
-            total = col_sum[2 * where + side]
-            cols.append(total[0:rows] + pltpu.roll(total[rows:], BLK, 1))
-        from_cols = jnp.where(low_out, cols[0], pltpu.roll(cols[1], BLK, 1))
+        first, second = col_sum[2 * where], col_sum[2 * where + 1]
+        straight = jnp.where(low_out, first[0:rows], second[rows:])
+        crossed = jnp.where(low_out, second[0:rows], first[rows:])
+        from_cols = straight + pltpu.roll(crossed, BLK, 1)
         result = ((from_rows + from_cols) * scale)[0:terms]
         if where < half:
             keep_ref[where] = result
@@ -273,7 +277,6 @@
         scratch_shapes=[
             pltpu.VMEM((slots, channels, BLK * BLK), BF),
             pltpu.VMEM((max(unroll, -(-2 * half // (PITCH * BLK // 2 // LANES))), PITCH * BLK // 2, LANES), F32),
-            pltpu.VMEM((2 * half, LANES, LANES), F32),
             pltpu.VMEM((half, 2 * LANES, 4 * LANES), BF),
             pltpu.VMEM((2,) + own_gram.shape, BF),
             pltpu.VMEM((blocks, BLK, LANES), BF),

time: 46.2 us -> 43.7 us (0.946)
  Pallas kernels: 15.1 us -> 12.6 us
    pallas_call x1, Pallas kernels: 13.2 us -> 10.7 us  [tile_terms(): pl.pallas_call(functools.partial(tiles_kernel, relative, unroll, scale),...]
where the time goes in v7:
time: 43.7 us; the launch traced here: 43.4 us
  starting transfers between devices  15.1 us (35%)
  Pallas kernels  12.6 us (29%)
  waiting for transfers between devices  12.3 us (28%)
  local copies, waits for them, and re-layouts  1.88 us (4%)
  other arithmetic  0.79 us (2%)
  between operations  0.76 us (2%)
    ppermute x13, starting transfers between devices, from_partner(): lax.ppermute(array, 'tile', [(i, i ^ mask) for i in range(lax.axis_size('...  15.1 us
    ppermute x13, waiting for transfers between devices, from_partner(): lax.ppermute(array, 'tile', [(i, i ^ mask) for i in range(lax.axis_size('...  12.3 us
    pallas_call x1, Pallas kernels, tile_terms(): pl.pallas_call(functools.partial(tiles_kernel, relative, unroll, scale),...  10.7 us
    pallas_call x1, Pallas kernels, gram_of(): pl.pallas_call(functools.partial(gram_kernel, math.sqrt(sources)), out_sh...  1.87 us
    slice x1, local copies, waits for them, and re-layouts, on_device(): to_move = observed[slots - moved:]  1.83 us
  transfers between devices with their start and end apart: 13, of which 9 were waited for; matrix products, arithmetic and copies ran while one was open for 0% of the time, Pallas kernels for 4%

profile of v7, /device:TPU:0, one launch (start us, length us, event | category | flops | bytes accessed | tf_op | source)
XLA Modules:
  0.0 43.4 jit_solution(5242481487675633689)
XLA Ops:
  0.0 0.0 copy-start.3
  0.0 0.0 copy-start.2
  0.0 0.0 copy-start.1
  0.0 0.0 copy-start
  0.0 1.8 %slice.21 = bf16[17,16,4096]{2,1,0:T(8,128)(2,1)S(1)} slice(bf16[66,16,4096]{2,1,0:T(8,128)(2,1)} %vis_hbm.1), slice={[49:66], [0:16], [0:4096]} | slice | bytes 4456448 | tf_op jit(solution)/shard_map/slice | solution.py:310
  1.8 0.0 copy-start.4
  1.9 0.0 copy-start.5
  1.9 0.5 %collective-permute-start.7 = (bf16[17,16,4096]{2,1,0:T(8,128)(2,1)S(1)}, bf16[17,16,4096]{2,1,0:T(8,128)(2,1)S(1)}, u32[]{:S(2)}, u32[]{:S(2)}) collective-permute-start(bf16[17,16,4096]{2,1,0:T(8,128)(2,1)S(1)} %slice.21), channel_id=1, source_target_pairs={{0,1},{1,0},{2,3},{3,2},{4,5},{5,4},{6,7},{7,6},{8,9},{9,8},{10,11... | collective-permute-start | bytes 6684680 | tf_op jit(solution)/shard_map/ppermute | solution.py:297
  2.4 0.0 copy-done.3
  2.4 3.7 %collective-permute-start = (bf16[1,66,128]{2,1,0:T(8,128)(2,1)S(1)}, bf16[1,66,128]{2,1,0:T(8,128)(2,1)S(1)}, u32[]{:S(2)}, u32[]{:S(2)}) collective-permute-start(bf16[1,66,128]{2,1,0:T(8,128)(2,1)S(1)} %bitcast.3), channel_id=1, source_target_pairs={{0,8},{1,9},{2,10},{3,11},{4,12},{5,13},{6,14},{7,15},{8,0},{9,1},... | collective-permute-start | bytes 50696 | tf_op jit(solution)/shard_map/ppermute | solution.py:297
  6.1 0.0 copy-done.2
  6.1 0.0 copy-done.1
  6.1 0.0 copy-done
  6.1 1.9 %shard_map.82.own_gram_ref = bf16[592,256]{1,0:T(8,128)(2,1)S(1)} custom-call(bf16[66,4096]{1,0:T(8,128)(2,1)S(1)} %copy-done, s32[16,256]{1,0:T(8,128)S(1)} %copy-done.1, f32[16,256]{1,0:T(8,128)S(1)} %copy-done.2), custom_call_target="tpu_custom_call" | custom-call | flops 1107296256 | bytes 1048576 | tf_op jit(solution)/shard_map/pallas_call | solution.py:81
  8.0 0.0 collective-permute-done
  8.0 0.2 collective-permute-start.4
  8.9 2.6 %collective-permute-start.3 = (bf16[2,66,128]{2,1,0:T(8,128)(2,1)S(1)}, bf16[2,66,128]{2,1,0:T(8,128)(2,1)S(1)}, u32[]{:S(2)}, u32[]{:S(2)}) collective-permute-start(bf16[2,66,128]{2,1,0:T(8,128)(2,1)S(1)} %pad_maximum_fusion.1), channel_id=1, source_target_pairs={{0,6},{1,7},{2,4},{3,5},{4,2},{5,3},{6,0},{7,1},{8,14},{9,15},{10,... | collective-permute-start | bytes 101384 | tf_op jit(solution)/shard_map/ppermute | solution.py:297
  11.5 0.4 %collective-permute-start.2 = (bf16[2,66,128]{2,1,0:T(8,128)(2,1)S(1)}, bf16[2,66,128]{2,1,0:T(8,128)(2,1)S(1)}, u32[]{:S(2)}, u32[]{:S(2)}) collective-permute-start(bf16[2,66,128]{2,1,0:T(8,128)(2,1)S(1)} %pad_maximum_fusion.1), channel_id=1, source_target_pairs={{0,4},{1,5},{2,6},{3,7},{4,0},{5,1},{6,2},{7,3},{8,12},{9,13},{10,... | collective-permute-start | bytes 101384 | tf_op jit(solution)/shard_map/ppermute | solution.py:297
  11.9 0.5 %collective-permute-start.1 = (bf16[2,66,128]{2,1,0:T(8,128)(2,1)S(1)}, bf16[2,66,128]{2,1,0:T(8,128)(2,1)S(1)}, u32[]{:S(2)}, u32[]{:S(2)}) collective-permute-start(bf16[2,66,128]{2,1,0:T(8,128)(2,1)S(1)} %pad_maximum_fusion.1), channel_id=1, source_target_pairs={{0,2},{1,3},{2,0},{3,1},{4,6},{5,7},{6,4},{7,5},{8,10},{9,11},{10,... | collective-permute-start | bytes 101384 | tf_op jit(solution)/shard_map/ppermute | solution.py:297
  12.4 0.0 copy-done.4
  12.4 0.0 copy-done.5
  12.4 0.1 pad_add_fusion.mine_ref
  12.5 1.3 %collective-permute-done.3 = bf16[2,66,128]{2,1,0:T(8,128)(2,1)S(1)} collective-permute-done((bf16[2,66,128]{2,1,0:T(8,128)(2,1)S(1)}, bf16[2,66,128]{2,1,0:T(8,128)(2,1)S(1)}, u32[]{:S(2)}, u32[]{:S(2)}) %collective-permute-start.3) | collective-permute-done | bytes 33824 | tf_op jit(solution)/shard_map/ppermute | solution.py:297
  13.8 0.0 collective-permute-start.5
  13.8 1.6 %collective-permute-done.2 = bf16[2,66,128]{2,1,0:T(8,128)(2,1)S(1)} collective-permute-done((bf16[2,66,128]{2,1,0:T(8,128)(2,1)S(1)}, bf16[2,66,128]{2,1,0:T(8,128)(2,1)S(1)}, u32[]{:S(2)}, u32[]{:S(2)}) %collective-permute-start.2) | collective-permute-done | bytes 33824 | tf_op jit(solution)/shard_map/ppermute | solution.py:297
  15.4 0.4 %collective-permute-done.1 = bf16[2,66,128]{2,1,0:T(8,128)(2,1)S(1)} collective-permute-done((bf16[2,66,128]{2,1,0:T(8,128)(2,1)S(1)}, bf16[2,66,128]{2,1,0:T(8,128)(2,1)S(1)}, u32[]{:S(2)}, u32[]{:S(2)}) %collective-permute-start.1) | collective-permute-done | bytes 33824 | tf_op jit(solution)/shard_map/ppermute | solution.py:297
  15.9 0.0 collective-permute-done.5.other_ref
  15.9 0.0 collective-permute-done.4.got_gram_ref
  15.9 0.1 collective-permute-start.6
  16.0 1.4 %collective-permute-done.6.got_ref = bf16[8,66,128]{2,1,0:T(8,128)(2,1)S(1)} collective-permute-done((bf16[8,66,128]{2,1,0:T(8,128)(2,1)S(1)}, bf16[8,66,128]{2,1,0:T(8,128)(2,1)S(1)}, u32[]{:S(2)}, u32[]{:S(2)}) %collective-permute-start.6) | collective-permute-done | bytes 135200 | tf_op jit(solution)/shard_map/ppermute | solution.py:297
  17.4 0.0 collective-permute-done.7.more_hbm
  17.4 10.7 %shard_map.83 = (f32[8,66,128]{2,1,0:T(8,128)S(1)}, f32[8,66,128]{2,1,0:T(8,128)S(1)}) custom-call(s32[133]{0:T(256)S(1)} %pad_add_fusion.mine_ref, s32[133]{0:T(256)S(1)} %collective-permute-done.5.other_ref, bf16[8,66,128]{2,1,0:T(8,128)(2,1)S(1)} %pad_maximum_fusion.own_ref, bf16[8,66,128]{2,1,0:T(8,128)(2,1)S(1)} %collective-permute-done.6.got_ref, ...), custom_call_target="tpu_custom_call" | custom-call | flops 1712848896 | bytes 8650752 | tf_op jit(solution)/shard_map/pallas_call | solution.py:272
  28.1 0.2 collective-permute-start.8
  28.3 1.5 %collective-permute-done.8 = f32[8,66,128]{2,1,0:T(8,128)S(1)} collective-permute-done((f32[8,66,128]{2,1,0:T(8,128)S(1)}, f32[8,66,128]{2,1,0:T(8,128)S(1)}, u32[]{:S(2)}, u32[]{:S(2)}) %collective-permute-start.8) | collective-permute-done | bytes 270368 | tf_op jit(solution)/shard_map/ppermute | solution.py:297
  29.8 1.8 %collective-permute-start.9 = (f32[2,66,128]{2,1,0:T(8,128)S(1)}, f32[2,66,128]{2,1,0:T(8,128)S(1)}, u32[]{:S(2)}, u32[]{:S(2)}) collective-permute-start(f32[2,66,128]{2,1,0:T(8,128)S(1)} %get-tuple-element.19), channel_id=1, source_target_pairs={{0,6},{1,7},{2,4},{3,5},{4,2},{5,3},{6,0},{7,1},{8,14},{9,15},{10,... | collective-permute-start | bytes 202760 | tf_op jit(solution)/shard_map/ppermute | solution.py:297
  31.6 1.3 %collective-permute-start.11 = (f32[2,66,128]{2,1,0:T(8,128)S(1)}, f32[2,66,128]{2,1,0:T(8,128)S(1)}, u32[]{:S(2)}, u32[]{:S(2)}) collective-permute-start(f32[2,66,128]{2,1,0:T(8,128)S(1)} %get-tuple-element.20), channel_id=1, source_target_pairs={{0,2},{1,3},{2,0},{3,1},{4,6},{5,7},{6,4},{7,5},{8,10},{9,11},{10,... | collective-permute-start | bytes 202760 | tf_op jit(solution)/shard_map/ppermute | solution.py:297
  32.9 0.4 %collective-permute-start.10 = (f32[2,66,128]{2,1,0:T(8,128)S(1)}, f32[2,66,128]{2,1,0:T(8,128)S(1)}, u32[]{:S(2)}, u32[]{:S(2)}) collective-permute-start(f32[2,66,128]{2,1,0:T(8,128)S(1)} %get-tuple-element.21), channel_id=1, source_target_pairs={{0,4},{1,5},{2,6},{3,7},{4,0},{5,1},{6,2},{7,3},{8,12},{9,13},{10,... | collective-permute-start | bytes 202760 | tf_op jit(solution)/shard_map/ppermute | solution.py:297
  33.3 1.8 %collective-permute-done.9 = f32[2,66,128]{2,1,0:T(8,128)S(1)} collective-permute-done((f32[2,66,128]{2,1,0:T(8,128)S(1)}, f32[2,66,128]{2,1,0:T(8,128)S(1)}, u32[]{:S(2)}, u32[]{:S(2)}) %collective-permute-start.9) | collective-permute-done | bytes 67616 | tf_op jit(solution)/shard_map/ppermute | solution.py:297
  35.1 1.5 %collective-permute-done.11 = f32[2,66,128]{2,1,0:T(8,128)S(1)} collective-permute-done((f32[2,66,128]{2,1,0:T(8,128)S(1)}, f32[2,66,128]{2,1,0:T(8,128)S(1)}, u32[]{:S(2)}, u32[]{:S(2)}) %collective-permute-start.11) | collective-permute-done | bytes 67616 | tf_op jit(solution)/shard_map/ppermute | solution.py:297
  36.6 0.6 %collective-permute-done.10 = f32[2,66,128]{2,1,0:T(8,128)S(1)} collective-permute-done((f32[2,66,128]{2,1,0:T(8,128)S(1)}, f32[2,66,128]{2,1,0:T(8,128)S(1)}, u32[]{:S(2)}, u32[]{:S(2)}) %collective-permute-start.10) | collective-permute-done | bytes 67616 | tf_op jit(solution)/shard_map/ppermute | solution.py:297
  37.3 3.3 %collective-permute-start.12 = (f32[1,66,128]{2,1,0:T(8,128)S(1)}, f32[1,66,128]{2,1,0:T(8,128)S(1)}, u32[]{:S(2)}, u32[]{:S(2)}) collective-permute-start(f32[1,66,128]{2,1,0:T(8,128)S(1)} %slice.33), channel_id=1, source_target_pairs={{0,8},{1,9},{2,10},{3,11},{4,12},{5,13},{6,14},{7,15},{8,0},{9,1},... | collective-permute-start | bytes 101384 | tf_op jit(solution)/shard_map/ppermute | solution.py:297
  40.5 2.2 %collective-permute-done.12 = f32[1,66,128]{2,1,0:T(8,128)S(1)} collective-permute-done((f32[1,66,128]{2,1,0:T(8,128)S(1)}, f32[1,66,128]{2,1,0:T(8,128)S(1)}, u32[]{:S(2)}, u32[]{:S(2)}) %collective-permute-start.12) | collective-permute-done | bytes 33824 | tf_op jit(solution)/shard_map/ppermute | solution.py:297
  42.8 0.6 %fusion.2 = f32[66,128]{1,0:T(8,128)} fusion(f32[1,66,128]{2,1,0:T(8,128)S(1)} %collective-permute-done.12, f32[2,66,128]{2,1,0:T(8,128)S(1)} %fusion.1), kind=kLoop, calls=%fused_computation.5 | loop fusion | flops 8448 | bytes 101376 | tf_op jit(solution)/shard_map/squeeze | solution.py:329
  (6 shorter events, 0.1 us)
Async XLA Ops:
  0.0 2.4 %copy-start.3 = (bf16[66,128]{1,0:T(8,128)(2,1)S(1)}, bf16[66,128]{1,0:T(8,128)(2,1)}, u32[]{:S(2)}) copy-start(bf16[66,128]{1,0:T(8,128)(2,1)} %param.8) | copy-start | bytes 50692
  0.0 6.1 %copy-start.2 = (f32[16,256]{1,0:T(8,128)S(1)}, f32[16,256]{1,0:T(8,128)}, u32[]{:S(2)}) copy-start(f32[16,256]{1,0:T(8,128)} %flux_ref.1) | copy-start | bytes 49156
  0.0 6.1 %copy-start.1 = (s32[16,256]{1,0:T(8,128)S(1)}, s32[16,256]{1,0:T(8,128)}, u32[]{:S(2)}) copy-start(s32[16,256]{1,0:T(8,128)} %pos_ref.1) | copy-start | bytes 49156
  0.0 6.1 %copy-start = (bf16[66,4096]{1,0:T(8,128)(2,1)S(1)}, bf16[66,4096]{1,0:T(8,128)(2,1)}, u32[]{:S(2)}) copy-start(bf16[66,4096]{1,0:T(8,128)(2,1)} %table_ref.1) | copy-start | bytes 1622020
  1.8 10.6 %copy-start.4 = (s32[66]{0:T(128)S(1)}, s32[66]{0:T(128)}, u32[]{:S(2)}) copy-start(s32[66]{0:T(128)} %param.14) | copy-start | bytes 796
  1.9 10.6 %copy-start.5 = (s32[66]{0:T(128)S(1)}, s32[66]{0:T(128)}, u32[]{:S(2)}) copy-start(s32[66]{0:T(128)} %param.13) | copy-start | bytes 796
  1.9 15.5 %collective-permute-start.7 = (bf16[17,16,4096]{2,1,0:T(8,128)(2,1)S(1)}, bf16[17,16,4096]{2,1,0:T(8,128)(2,1)S(1)}, u32[]{:S(2)}, u32[]{:S(2)}) collective-permute-start(bf16[17,16,4096]{2,1,0:T(8,128)(2,1)S(1)} %slice.21), channel_id=1, source_target_pairs={{0,1},{1,0},{2,3},{3,2},{4,5},{5,4},{6,7},{7,6},{8,9},{9,8},{10,11... | collective-permute-start | bytes 6684680 | tf_op jit(solution)/shard_map/ppermute | solution.py:297
  2.4 5.6 %collective-permute-start = (bf16[1,66,128]{2,1,0:T(8,128)(2,1)S(1)}, bf16[1,66,128]{2,1,0:T(8,128)(2,1)S(1)}, u32[]{:S(2)}, u32[]{:S(2)}) collective-permute-start(bf16[1,66,128]{2,1,0:T(8,128)(2,1)S(1)} %bitcast.3), channel_id=1, source_target_pairs={{0,8},{1,9},{2,10},{3,11},{4,12},{5,13},{6,14},{7,15},{8,0},{9,1},... | collective-permute-start | bytes 50696 | tf_op jit(solution)/shard_map/ppermute | solution.py:297
  8.0 7.9 %collective-permute-start.4 = (bf16[592,256]{1,0:T(8,128)(2,1)S(1)}, bf16[592,256]{1,0:T(8,128)(2,1)S(1)}, u32[]{:S(2)}, u32[]{:S(2)}) collective-permute-start(bf16[592,256]{1,0:T(8,128)(2,1)S(1)} %shard_map.82.own_gram_ref), channel_id=1, source_target_pairs={{0,1},{1,0},{2,3},{3,2},{4,5},{5,4},{6,7},{7,6},{8,9},{9,8},{10,11... | collective-permute-start | bytes 909320 | tf_op jit(solution)/shard_map/ppermute | solution.py:297
  8.9 4.9 %collective-permute-start.3 = (bf16[2,66,128]{2,1,0:T(8,128)(2,1)S(1)}, bf16[2,66,128]{2,1,0:T(8,128)(2,1)S(1)}, u32[]{:S(2)}, u32[]{:S(2)}) collective-permute-start(bf16[2,66,128]{2,1,0:T(8,128)(2,1)S(1)} %pad_maximum_fusion.1), channel_id=1, source_target_pairs={{0,6},{1,7},{2,4},{3,5},{4,2},{5,3},{6,0},{7,1},{8,14},{9,15},{10,... | collective-permute-start | bytes 101384 | tf_op jit(solution)/shard_map/ppermute | solution.py:297
  11.5 4.0 %collective-permute-start.2 = (bf16[2,66,128]{2,1,0:T(8,128)(2,1)S(1)}, bf16[2,66,128]{2,1,0:T(8,128)(2,1)S(1)}, u32[]{:S(2)}, u32[]{:S(2)}) collective-permute-start(bf16[2,66,128]{2,1,0:T(8,128)(2,1)S(1)} %pad_maximum_fusion.1), channel_id=1, source_target_pairs={{0,4},{1,5},{2,6},{3,7},{4,0},{5,1},{6,2},{7,3},{8,12},{9,13},{10,... | collective-permute-start | bytes 101384 | tf_op jit(solution)/shard_map/ppermute | solution.py:297
  11.9 4.0 %collective-permute-start.1 = (bf16[2,66,128]{2,1,0:T(8,128)(2,1)S(1)}, bf16[2,66,128]{2,1,0:T(8,128)(2,1)S(1)}, u32[]{:S(2)}, u32[]{:S(2)}) collective-permute-start(bf16[2,66,128]{2,1,0:T(8,128)(2,1)S(1)} %pad_maximum_fusion.1), channel_id=1, source_target_pairs={{0,2},{1,3},{2,0},{3,1},{4,6},{5,7},{6,4},{7,5},{8,10},{9,11},{10,... | collective-permute-start | bytes 101384 | tf_op jit(solution)/shard_map/ppermute | solution.py:297
  13.8 2.1 %collective-permute-start.5 = (s32[133]{0:T(256)S(1)}, s32[133]{0:T(256)S(1)}, u32[]{:S(2)}, u32[]{:S(2)}) collective-permute-start(s32[133]{0:T(256)S(1)} %pad_add_fusion.mine_ref), channel_id=1, source_target_pairs={{0,1},{1,0},{2,3},{3,2},{4,5},{5,4},{6,7},{7,6},{8,9},{9,8},{10,11... | collective-permute-start | bytes 1604 | tf_op jit(solution)/shard_map/ppermute | solution.py:297
  15.9 1.4 %collective-permute-start.6 = (bf16[8,66,128]{2,1,0:T(8,128)(2,1)S(1)}, bf16[8,66,128]{2,1,0:T(8,128)(2,1)S(1)}, u32[]{:S(2)}, u32[]{:S(2)}) collective-permute-start(bf16[8,66,128]{2,1,0:T(8,128)(2,1)S(1)} %pad_maximum_fusion.own_ref), channel_id=1, source_target_pairs={{0,1},{1,0},{2,3},{3,2},{4,5},{5,4},{6,7},{7,6},{8,9},{9,8},{10,11... | collective-permute-start | bytes 405512 | tf_op jit(solution)/shard_map/ppermute | solution.py:297
  28.1 1.6 %collective-permute-start.8 = (f32[8,66,128]{2,1,0:T(8,128)S(1)}, f32[8,66,128]{2,1,0:T(8,128)S(1)}, u32[]{:S(2)}, u32[]{:S(2)}) collective-permute-start(f32[8,66,128]{2,1,0:T(8,128)S(1)} %get-tuple-element.18), channel_id=1, source_target_pairs={{0,1},{1,0},{2,3},{3,2},{4,5},{5,4},{6,7},{7,6},{8,9},{9,8},{10,11... | collective-permute-start | bytes 811016 | tf_op jit(solution)/shard_map/ppermute | solution.py:297
  29.8 5.4 %collective-permute-start.9 = (f32[2,66,128]{2,1,0:T(8,128)S(1)}, f32[2,66,128]{2,1,0:T(8,128)S(1)}, u32[]{:S(2)}, u32[]{:S(2)}) collective-permute-start(f32[2,66,128]{2,1,0:T(8,128)S(1)} %get-tuple-element.19), channel_id=1, source_target_pairs={{0,6},{1,7},{2,4},{3,5},{4,2},{5,3},{6,0},{7,1},{8,14},{9,15},{10,... | collective-permute-start | bytes 202760 | tf_op jit(solution)/shard_map/ppermute | solution.py:297
  31.6 5.0 %collective-permute-start.11 = (f32[2,66,128]{2,1,0:T(8,128)S(1)}, f32[2,66,128]{2,1,0:T(8,128)S(1)}, u32[]{:S(2)}, u32[]{:S(2)}) collective-permute-start(f32[2,66,128]{2,1,0:T(8,128)S(1)} %get-tuple-element.20), channel_id=1, source_target_pairs={{0,2},{1,3},{2,0},{3,1},{4,6},{5,7},{6,4},{7,5},{8,10},{9,11},{10,... | collective-permute-start | bytes 202760 | tf_op jit(solution)/shard_map/ppermute | solution.py:297
  32.9 4.4 %collective-permute-start.10 = (f32[2,66,128]{2,1,0:T(8,128)S(1)}, f32[2,66,128]{2,1,0:T(8,128)S(1)}, u32[]{:S(2)}, u32[]{:S(2)}) collective-permute-start(f32[2,66,128]{2,1,0:T(8,128)S(1)} %get-tuple-element.21), channel_id=1, source_target_pairs={{0,4},{1,5},{2,6},{3,7},{4,0},{5,1},{6,2},{7,3},{8,12},{9,13},{10,... | collective-permute-start | bytes 202760 | tf_op jit(solution)/shard_map/ppermute | solution.py:297
  37.3 5.5 %collective-permute-start.12 = (f32[1,66,128]{2,1,0:T(8,128)S(1)}, f32[1,66,128]{2,1,0:T(8,128)S(1)}, u32[]{:S(2)}, u32[]{:S(2)}) collective-permute-start(f32[1,66,128]{2,1,0:T(8,128)S(1)} %slice.33), channel_id=1, source_target_pairs={{0,8},{1,9},{2,10},{3,11},{4,12},{5,13},{6,14},{7,15},{8,0},{9,1},... | collective-permute-start | bytes 101384 | tf_op jit(solution)/shard_map/ppermute | solution.py:297

commit v8 on v7

--- a/solution.py
+++ b/solution.py
@@ -323,7 +323,8 @@
         )
         total = total + from_partner(sent, 1)
         total = sum(
-            [from_partner(total[mask : mask + 2], mask) for mask in (6, 4, 2)], total[:2]
+            [from_partner(total[mask : mask + 2].astype(BF), mask).astype(F32) for mask in (6, 4, 2)],
+            total[:2],
         )
         total = total[:1] + from_partner(total[1:], 8)
         return total[0]

time: 43.7 us -> 42.8 us (0.979)
  starting transfers between devices: 15.1 us -> 14.5 us
    ppermute x13, starting transfers between devices: 15.1 us -> 14.5 us  [from_partner(): lax.ppermute(array, 'tile', [(i, i ^ mask) for i in range(lax.axis_size('...]
where the time goes in v8:
time: 42.8 us
  starting transfers between devices  14.5 us (34%)
  Pallas kernels  12.5 us (29%)
  waiting for transfers between devices  12.3 us (29%)
  local copies, waits for them, and re-layouts  1.88 us (4%)
  other arithmetic  0.79 us (2%)
  between operations  0.77 us (2%)
    ppermute x13, starting transfers between devices, from_partner(): lax.ppermute(array, 'tile', [(i, i ^ mask) for i in range(lax.axis_size('...  14.5 us
    ppermute x13, waiting for transfers between devices, from_partner(): lax.ppermute(array, 'tile', [(i, i ^ mask) for i in range(lax.axis_size('...  12.3 us
    pallas_call x1, Pallas kernels, tile_terms(): pl.pallas_call(functools.partial(tiles_kernel, relative, unroll, scale),...  10.7 us
    pallas_call x1, Pallas kernels, gram_of(): pl.pallas_call(functools.partial(gram_kernel, math.sqrt(sources)), out_sh...  1.87 us
    slice x1, local copies, waits for them, and re-layouts, on_device(): to_move = observed[slots - moved:]  1.83 us
  transfers between devices with their start and end apart: 13, of which 9 were waited for; matrix products, arithmetic and copies ran while one was open for 0% of the time, Pallas kernels for 4%

profile of v8, /device:TPU:0, one launch (start us, length us, event | category | flops | bytes accessed | tf_op | source)
XLA Modules:
  0.0 42.8 jit_solution(14865691662396445177)
XLA Ops:
  0.0 0.0 copy-start.3
  0.0 0.0 copy-start.2
  0.0 0.0 copy-start.1
  0.0 0.0 copy-start
  0.0 1.8 %slice.24 = bf16[17,16,4096]{2,1,0:T(8,128)(2,1)S(1)} slice(bf16[66,16,4096]{2,1,0:T(8,128)(2,1)} %vis_hbm.1), slice={[49:66], [0:16], [0:4096]} | slice | bytes 4456448 | tf_op jit(solution)/shard_map/slice | solution.py:310
  1.8 0.0 copy-start.4
  1.9 0.0 copy-start.5
  1.9 0.5 %collective-permute-start.7 = (bf16[17,16,4096]{2,1,0:T(8,128)(2,1)S(1)}, bf16[17,16,4096]{2,1,0:T(8,128)(2,1)S(1)}, u32[]{:S(2)}, u32[]{:S(2)}) collective-permute-start(bf16[17,16,4096]{2,1,0:T(8,128)(2,1)S(1)} %slice.24), channel_id=1, source_target_pairs={{0,1},{1,0},{2,3},{3,2},{4,5},{5,4},{6,7},{7,6},{8,9},{9,8},{10,11... | collective-permute-start | bytes 6684680 | tf_op jit(solution)/shard_map/ppermute | solution.py:297
  2.4 0.0 copy-done.3
  2.4 3.7 %collective-permute-start = (bf16[1,66,128]{2,1,0:T(8,128)(2,1)S(1)}, bf16[1,66,128]{2,1,0:T(8,128)(2,1)S(1)}, u32[]{:S(2)}, u32[]{:S(2)}) collective-permute-start(bf16[1,66,128]{2,1,0:T(8,128)(2,1)S(1)} %bitcast.3), channel_id=1, source_target_pairs={{0,8},{1,9},{2,10},{3,11},{4,12},{5,13},{6,14},{7,15},{8,0},{9,1},... | collective-permute-start | bytes 50696 | tf_op jit(solution)/shard_map/ppermute | solution.py:297
  6.1 0.0 copy-done.2
  6.1 0.0 copy-done.1
  6.1 0.0 copy-done
  6.1 1.9 %shard_map.82.own_gram_ref = bf16[592,256]{1,0:T(8,128)(2,1)S(1)} custom-call(bf16[66,4096]{1,0:T(8,128)(2,1)S(1)} %copy-done, s32[16,256]{1,0:T(8,128)S(1)} %copy-done.1, f32[16,256]{1,0:T(8,128)S(1)} %copy-done.2), custom_call_target="tpu_custom_call" | custom-call | flops 1107296256 | bytes 1048576 | tf_op jit(solution)/shard_map/pallas_call | solution.py:81
  8.0 0.0 collective-permute-done
  8.0 0.2 collective-permute-start.4
  8.9 2.6 %collective-permute-start.3 = (bf16[2,66,128]{2,1,0:T(8,128)(2,1)S(1)}, bf16[2,66,128]{2,1,0:T(8,128)(2,1)S(1)}, u32[]{:S(2)}, u32[]{:S(2)}) collective-permute-start(bf16[2,66,128]{2,1,0:T(8,128)(2,1)S(1)} %pad_maximum_fusion.1), channel_id=1, source_target_pairs={{0,6},{1,7},{2,4},{3,5},{4,2},{5,3},{6,0},{7,1},{8,14},{9,15},{10,... | collective-permute-start | bytes 101384 | tf_op jit(solution)/shard_map/ppermute | solution.py:297
  11.5 0.4 %collective-permute-start.2 = (bf16[2,66,128]{2,1,0:T(8,128)(2,1)S(1)}, bf16[2,66,128]{2,1,0:T(8,128)(2,1)S(1)}, u32[]{:S(2)}, u32[]{:S(2)}) collective-permute-start(bf16[2,66,128]{2,1,0:T(8,128)(2,1)S(1)} %pad_maximum_fusion.1), channel_id=1, source_target_pairs={{0,4},{1,5},{2,6},{3,7},{4,0},{5,1},{6,2},{7,3},{8,12},{9,13},{10,... | collective-permute-start | bytes 101384 | tf_op jit(solution)/shard_map/ppermute | solution.py:297
  11.9 0.5 %collective-permute-start.1 = (bf16[2,66,128]{2,1,0:T(8,128)(2,1)S(1)}, bf16[2,66,128]{2,1,0:T(8,128)(2,1)S(1)}, u32[]{:S(2)}, u32[]{:S(2)}) collective-permute-start(bf16[2,66,128]{2,1,0:T(8,128)(2,1)S(1)} %pad_maximum_fusion.1), channel_id=1, source_target_pairs={{0,2},{1,3},{2,0},{3,1},{4,6},{5,7},{6,4},{7,5},{8,10},{9,11},{10,... | collective-permute-start | bytes 101384 | tf_op jit(solution)/shard_map/ppermute | solution.py:297
  12.4 0.0 copy-done.4
  12.4 0.0 copy-done.5
  12.4 0.1 pad_add_fusion.mine_ref
  12.5 1.3 %collective-permute-done.3 = bf16[2,66,128]{2,1,0:T(8,128)(2,1)S(1)} collective-permute-done((bf16[2,66,128]{2,1,0:T(8,128)(2,1)S(1)}, bf16[2,66,128]{2,1,0:T(8,128)(2,1)S(1)}, u32[]{:S(2)}, u32[]{:S(2)}) %collective-permute-start.3) | collective-permute-done | bytes 33824 | tf_op jit(solution)/shard_map/ppermute | solution.py:297
  13.8 0.0 collective-permute-start.5
  13.8 1.6 %collective-permute-done.2 = bf16[2,66,128]{2,1,0:T(8,128)(2,1)S(1)} collective-permute-done((bf16[2,66,128]{2,1,0:T(8,128)(2,1)S(1)}, bf16[2,66,128]{2,1,0:T(8,128)(2,1)S(1)}, u32[]{:S(2)}, u32[]{:S(2)}) %collective-permute-start.2) | collective-permute-done | bytes 33824 | tf_op jit(solution)/shard_map/ppermute | solution.py:297
  15.4 0.4 %collective-permute-done.1 = bf16[2,66,128]{2,1,0:T(8,128)(2,1)S(1)} collective-permute-done((bf16[2,66,128]{2,1,0:T(8,128)(2,1)S(1)}, bf16[2,66,128]{2,1,0:T(8,128)(2,1)S(1)}, u32[]{:S(2)}, u32[]{:S(2)}) %collective-permute-start.1) | collective-permute-done | bytes 33824 | tf_op jit(solution)/shard_map/ppermute | solution.py:297
  15.9 0.0 collective-permute-done.5.other_ref
  15.9 0.0 collective-permute-done.4.got_gram_ref
  15.9 0.1 collective-permute-start.6
  16.0 1.4 %collective-permute-done.6.got_ref = bf16[8,66,128]{2,1,0:T(8,128)(2,1)S(1)} collective-permute-done((bf16[8,66,128]{2,1,0:T(8,128)(2,1)S(1)}, bf16[8,66,128]{2,1,0:T(8,128)(2,1)S(1)}, u32[]{:S(2)}, u32[]{:S(2)}) %collective-permute-start.6) | collective-permute-done | bytes 135200 | tf_op jit(solution)/shard_map/ppermute | solution.py:297
  17.4 0.0 collective-permute-done.7.more_hbm
  17.4 10.7 %shard_map.83 = (f32[8,66,128]{2,1,0:T(8,128)S(1)}, f32[8,66,128]{2,1,0:T(8,128)S(1)}) custom-call(s32[133]{0:T(256)S(1)} %pad_add_fusion.mine_ref, s32[133]{0:T(256)S(1)} %collective-permute-done.5.other_ref, bf16[8,66,128]{2,1,0:T(8,128)(2,1)S(1)} %pad_maximum_fusion.own_ref, bf16[8,66,128]{2,1,0:T(8,128)(2,1)S(1)} %collective-permute-done.6.got_ref, ...), custom_call_target="tpu_custom_call" | custom-call | flops 1712848896 | bytes 8650752 | tf_op jit(solution)/shard_map/pallas_call | solution.py:272
  28.0 0.2 collective-permute-start.8
  28.3 1.4 %collective-permute-done.8 = f32[8,66,128]{2,1,0:T(8,128)S(1)} collective-permute-done((f32[8,66,128]{2,1,0:T(8,128)S(1)}, f32[8,66,128]{2,1,0:T(8,128)S(1)}, u32[]{:S(2)}, u32[]{:S(2)}) %collective-permute-start.8) | collective-permute-done | bytes 270368 | tf_op jit(solution)/shard_map/ppermute | solution.py:297
  29.8 1.9 %collective-permute-start.9 = (bf16[2,66,128]{2,1,0:T(8,128)(2,1)S(1)}, bf16[2,66,128]{2,1,0:T(8,128)(2,1)S(1)}, u32[]{:S(2)}, u32[]{:S(2)}) collective-permute-start(bf16[2,66,128]{2,1,0:T(8,128)(2,1)S(1)} %get-tuple-element.21), channel_id=1, source_target_pairs={{0,6},{1,7},{2,4},{3,5},{4,2},{5,3},{6,0},{7,1},{8,14},{9,15},{10,... | collective-permute-start | bytes 101384 | tf_op jit(solution)/shard_map/ppermute | solution.py:297
  31.6 1.3 %collective-permute-start.11 = (bf16[2,66,128]{2,1,0:T(8,128)(2,1)S(1)}, bf16[2,66,128]{2,1,0:T(8,128)(2,1)S(1)}, u32[]{:S(2)}, u32[]{:S(2)}) collective-permute-start(bf16[2,66,128]{2,1,0:T(8,128)(2,1)S(1)} %get-tuple-element.22), channel_id=1, source_target_pairs={{0,2},{1,3},{2,0},{3,1},{4,6},{5,7},{6,4},{7,5},{8,10},{9,11},{10,... | collective-permute-start | bytes 101384 | tf_op jit(solution)/shard_map/ppermute | solution.py:297
  32.9 0.4 collective-permute-start.10
  33.3 1.5 %collective-permute-done.9 = bf16[2,66,128]{2,1,0:T(8,128)(2,1)S(1)} collective-permute-done((bf16[2,66,128]{2,1,0:T(8,128)(2,1)S(1)}, bf16[2,66,128]{2,1,0:T(8,128)(2,1)S(1)}, u32[]{:S(2)}, u32[]{:S(2)}) %collective-permute-start.9) | collective-permute-done | bytes 33824 | tf_op jit(solution)/shard_map/ppermute | solution.py:297
  34.8 0.8 %collective-permute-done.11 = bf16[2,66,128]{2,1,0:T(8,128)(2,1)S(1)} collective-permute-done((bf16[2,66,128]{2,1,0:T(8,128)(2,1)S(1)}, bf16[2,66,128]{2,1,0:T(8,128)(2,1)S(1)}, u32[]{:S(2)}, u32[]{:S(2)}) %collective-permute-start.11) | collective-permute-done | bytes 33824 | tf_op jit(solution)/shard_map/ppermute | solution.py:297
  35.6 1.3 %collective-permute-done.10 = bf16[2,66,128]{2,1,0:T(8,128)(2,1)S(1)} collective-permute-done((bf16[2,66,128]{2,1,0:T(8,128)(2,1)S(1)}, bf16[2,66,128]{2,1,0:T(8,128)(2,1)S(1)}, u32[]{:S(2)}, u32[]{:S(2)}) %collective-permute-start.10) | collective-permute-done | bytes 33824 | tf_op jit(solution)/shard_map/ppermute | solution.py:297
  36.9 2.7 %collective-permute-start.12 = (f32[1,66,128]{2,1,0:T(8,128)S(1)}, f32[1,66,128]{2,1,0:T(8,128)S(1)}, u32[]{:S(2)}, u32[]{:S(2)}) collective-permute-start(f32[1,66,128]{2,1,0:T(8,128)S(1)} %slice.36), channel_id=1, source_target_pairs={{0,8},{1,9},{2,10},{3,11},{4,12},{5,13},{6,14},{7,15},{8,0},{9,1},... | collective-permute-start | bytes 101384 | tf_op jit(solution)/shard_map/ppermute | solution.py:297
  39.5 2.7 %collective-permute-done.12 = f32[1,66,128]{2,1,0:T(8,128)S(1)} collective-permute-done((f32[1,66,128]{2,1,0:T(8,128)S(1)}, f32[1,66,128]{2,1,0:T(8,128)S(1)}, u32[]{:S(2)}, u32[]{:S(2)}) %collective-permute-start.12) | collective-permute-done | bytes 33824 | tf_op jit(solution)/shard_map/ppermute | solution.py:297
  42.2 0.6 %fusion.2 = f32[66,128]{1,0:T(8,128)} fusion(f32[1,66,128]{2,1,0:T(8,128)S(1)} %collective-permute-done.12, f32[2,66,128]{2,1,0:T(8,128)S(1)} %fusion.1), kind=kLoop, calls=%fused_computation.5 | loop fusion | flops 8448 | bytes 101376 | tf_op jit(solution)/shard_map/squeeze | solution.py:330
  (6 shorter events, 0.1 us)
Async XLA Ops:
  0.0 2.4 %copy-start.3 = (bf16[66,128]{1,0:T(8,128)(2,1)S(1)}, bf16[66,128]{1,0:T(8,128)(2,1)}, u32[]{:S(2)}) copy-start(bf16[66,128]{1,0:T(8,128)(2,1)} %param.8) | copy-start | bytes 50692
  0.0 6.1 %copy-start.2 = (f32[16,256]{1,0:T(8,128)S(1)}, f32[16,256]{1,0:T(8,128)}, u32[]{:S(2)}) copy-start(f32[16,256]{1,0:T(8,128)} %flux_ref.1) | copy-start | bytes 49156
  0.0 6.1 %copy-start.1 = (s32[16,256]{1,0:T(8,128)S(1)}, s32[16,256]{1,0:T(8,128)}, u32[]{:S(2)}) copy-start(s32[16,256]{1,0:T(8,128)} %pos_ref.1) | copy-start | bytes 49156
  0.0 6.1 %copy-start = (bf16[66,4096]{1,0:T(8,128)(2,1)S(1)}, bf16[66,4096]{1,0:T(8,128)(2,1)}, u32[]{:S(2)}) copy-start(bf16[66,4096]{1,0:T(8,128)(2,1)} %table_ref.1) | copy-start | bytes 1622020
  1.8 10.6 %copy-start.4 = (s32[66]{0:T(128)S(1)}, s32[66]{0:T(128)}, u32[]{:S(2)}) copy-start(s32[66]{0:T(128)} %param.14) | copy-start | bytes 796
  1.9 10.6 %copy-start.5 = (s32[66]{0:T(128)S(1)}, s32[66]{0:T(128)}, u32[]{:S(2)}) copy-start(s32[66]{0:T(128)} %param.13) | copy-start | bytes 796
  1.9 15.5 %collective-permute-start.7 = (bf16[17,16,4096]{2,1,0:T(8,128)(2,1)S(1)}, bf16[17,16,4096]{2,1,0:T(8,128)(2,1)S(1)}, u32[]{:S(2)}, u32[]{:S(2)}) collective-permute-start(bf16[17,16,4096]{2,1,0:T(8,128)(2,1)S(1)} %slice.24), channel_id=1, source_target_pairs={{0,1},{1,0},{2,3},{3,2},{4,5},{5,4},{6,7},{7,6},{8,9},{9,8},{10,11... | collective-permute-start | bytes 6684680 | tf_op jit(solution)/shard_map/ppermute | solution.py:297
  2.4 5.6 %collective-permute-start = (bf16[1,66,128]{2,1,0:T(8,128)(2,1)S(1)}, bf16[1,66,128]{2,1,0:T(8,128)(2,1)S(1)}, u32[]{:S(2)}, u32[]{:S(2)}) collective-permute-start(bf16[1,66,128]{2,1,0:T(8,128)(2,1)S(1)} %bitcast.3), channel_id=1, source_target_pairs={{0,8},{1,9},{2,10},{3,11},{4,12},{5,13},{6,14},{7,15},{8,0},{9,1},... | collective-permute-start | bytes 50696 | tf_op jit(solution)/shard_map/ppermute | solution.py:297
  8.0 7.9 %collective-permute-start.4 = (bf16[592,256]{1,0:T(8,128)(2,1)S(1)}, bf16[592,256]{1,0:T(8,128)(2,1)S(1)}, u32[]{:S(2)}, u32[]{:S(2)}) collective-permute-start(bf16[592,256]{1,0:T(8,128)(2,1)S(1)} %shard_map.82.own_gram_ref), channel_id=1, source_target_pairs={{0,1},{1,0},{2,3},{3,2},{4,5},{5,4},{6,7},{7,6},{8,9},{9,8},{10,11... | collective-permute-start | bytes 909320 | tf_op jit(solution)/shard_map/ppermute | solution.py:297
  8.9 4.9 %collective-permute-start.3 = (bf16[2,66,128]{2,1,0:T(8,128)(2,1)S(1)}, bf16[2,66,128]{2,1,0:T(8,128)(2,1)S(1)}, u32[]{:S(2)}, u32[]{:S(2)}) collective-permute-start(bf16[2,66,128]{2,1,0:T(8,128)(2,1)S(1)} %pad_maximum_fusion.1), channel_id=1, source_target_pairs={{0,6},{1,7},{2,4},{3,5},{4,2},{5,3},{6,0},{7,1},{8,14},{9,15},{10,... | collective-permute-start | bytes 101384 | tf_op jit(solution)/shard_map/ppermute | solution.py:297
  11.5 4.0 %collective-permute-start.2 = (bf16[2,66,128]{2,1,0:T(8,128)(2,1)S(1)}, bf16[2,66,128]{2,1,0:T(8,128)(2,1)S(1)}, u32[]{:S(2)}, u32[]{:S(2)}) collective-permute-start(bf16[2,66,128]{2,1,0:T(8,128)(2,1)S(1)} %pad_maximum_fusion.1), channel_id=1, source_target_pairs={{0,4},{1,5},{2,6},{3,7},{4,0},{5,1},{6,2},{7,3},{8,12},{9,13},{10,... | collective-permute-start | bytes 101384 | tf_op jit(solution)/shard_map/ppermute | solution.py:297
  11.9 4.0 %collective-permute-start.1 = (bf16[2,66,128]{2,1,0:T(8,128)(2,1)S(1)}, bf16[2,66,128]{2,1,0:T(8,128)(2,1)S(1)}, u32[]{:S(2)}, u32[]{:S(2)}) collective-permute-start(bf16[2,66,128]{2,1,0:T(8,128)(2,1)S(1)} %pad_maximum_fusion.1), channel_id=1, source_target_pairs={{0,2},{1,3},{2,0},{3,1},{4,6},{5,7},{6,4},{7,5},{8,10},{9,11},{10,... | collective-permute-start | bytes 101384 | tf_op jit(solution)/shard_map/ppermute | solution.py:297
  13.8 2.1 %collective-permute-start.5 = (s32[133]{0:T(256)S(1)}, s32[133]{0:T(256)S(1)}, u32[]{:S(2)}, u32[]{:S(2)}) collective-permute-start(s32[133]{0:T(256)S(1)} %pad_add_fusion.mine_ref), channel_id=1, source_target_pairs={{0,1},{1,0},{2,3},{3,2},{4,5},{5,4},{6,7},{7,6},{8,9},{9,8},{10,11... | collective-permute-start | bytes 1604 | tf_op jit(solution)/shard_map/ppermute | solution.py:297
  15.9 1.4 %collective-permute-start.6 = (bf16[8,66,128]{2,1,0:T(8,128)(2,1)S(1)}, bf16[8,66,128]{2,1,0:T(8,128)(2,1)S(1)}, u32[]{:S(2)}, u32[]{:S(2)}) collective-permute-start(bf16[8,66,128]{2,1,0:T(8,128)(2,1)S(1)} %pad_maximum_fusion.own_ref), channel_id=1, source_target_pairs={{0,1},{1,0},{2,3},{3,2},{4,5},{5,4},{6,7},{7,6},{8,9},{9,8},{10,11... | collective-permute-start | bytes 405512 | tf_op jit(solution)/shard_map/ppermute | solution.py:297
  28.0 1.6 %collective-permute-start.8 = (f32[8,66,128]{2,1,0:T(8,128)S(1)}, f32[8,66,128]{2,1,0:T(8,128)S(1)}, u32[]{:S(2)}, u32[]{:S(2)}) collective-permute-start(f32[8,66,128]{2,1,0:T(8,128)S(1)} %get-tuple-element.18), channel_id=1, source_target_pairs={{0,1},{1,0},{2,3},{3,2},{4,5},{5,4},{6,7},{7,6},{8,9},{9,8},{10,11... | collective-permute-start | bytes 811016 | tf_op jit(solution)/shard_map/ppermute | solution.py:297
  29.8 5.0 %collective-permute-start.9 = (bf16[2,66,128]{2,1,0:T(8,128)(2,1)S(1)}, bf16[2,66,128]{2,1,0:T(8,128)(2,1)S(1)}, u32[]{:S(2)}, u32[]{:S(2)}) collective-permute-start(bf16[2,66,128]{2,1,0:T(8,128)(2,1)S(1)} %get-tuple-element.21), channel_id=1, source_target_pairs={{0,6},{1,7},{2,4},{3,5},{4,2},{5,3},{6,0},{7,1},{8,14},{9,15},{10,... | collective-permute-start | bytes 101384 | tf_op jit(solution)/shard_map/ppermute | solution.py:297
  31.6 4.0 %collective-permute-start.11 = (bf16[2,66,128]{2,1,0:T(8,128)(2,1)S(1)}, bf16[2,66,128]{2,1,0:T(8,128)(2,1)S(1)}, u32[]{:S(2)}, u32[]{:S(2)}) collective-permute-start(bf16[2,66,128]{2,1,0:T(8,128)(2,1)S(1)} %get-tuple-element.22), channel_id=1, source_target_pairs={{0,2},{1,3},{2,0},{3,1},{4,6},{5,7},{6,4},{7,5},{8,10},{9,11},{10,... | collective-permute-start | bytes 101384 | tf_op jit(solution)/shard_map/ppermute | solution.py:297
  32.9 4.0 %collective-permute-start.10 = (bf16[2,66,128]{2,1,0:T(8,128)(2,1)S(1)}, bf16[2,66,128]{2,1,0:T(8,128)(2,1)S(1)}, u32[]{:S(2)}, u32[]{:S(2)}) collective-permute-start(bf16[2,66,128]{2,1,0:T(8,128)(2,1)S(1)} %get-tuple-element.23), channel_id=1, source_target_pairs={{0,4},{1,5},{2,6},{3,7},{4,0},{5,1},{6,2},{7,3},{8,12},{9,13},{10,... | collective-permute-start | bytes 101384 | tf_op jit(solution)/shard_map/ppermute | solution.py:297
  36.9 5.3 %collective-permute-start.12 = (f32[1,66,128]{2,1,0:T(8,128)S(1)}, f32[1,66,128]{2,1,0:T(8,128)S(1)}, u32[]{:S(2)}, u32[]{:S(2)}) collective-permute-start(f32[1,66,128]{2,1,0:T(8,128)S(1)} %slice.36), channel_id=1, source_target_pairs={{0,8},{1,9},{2,10},{3,11},{4,12},{5,13},{6,14},{7,15},{8,0},{9,1},... | collective-permute-start | bytes 101384 | tf_op jit(solution)/shard_map/ppermute | solution.py:297

commit v9 on v8

--- a/solution.py
+++ b/solution.py
@@ -226,14 +226,12 @@
                 difference = models[u][:, p * LANES : (p + 1) * LANES] - seen
                 residual.append(jnp.where(keep, difference, 0.0).astype(BF))
             residuals.append(residual)
-        to_rows = [
-            lax.dot_general(jnp.concatenate(residual, 1), right[b], NT, preferred_element_type=F32)
-            for (a, b), residual in zip(pairs_of, residuals)
-        ]
-        to_cols = [
-            jnp.dot(left[a], jnp.concatenate(residual, 0), preferred_element_type=F32)
-            for (a, b), residual in zip(pairs_of, residuals)
-        ]
+        to_rows, to_cols = [], []
+        for (a, b), residual in zip(pairs_of, residuals):
+            to_cols.append(jnp.dot(left[a], jnp.concatenate(residual, 0), preferred_element_type=F32))
+            to_rows.append(
+                lax.dot_general(jnp.concatenate(residual, 1), right[b], NT, preferred_element_type=F32)
+            )
         for (a, b), to_row, to_col in zip(pairs_of, to_rows, to_cols):
             row_sum[a, :, 0:tall] += to_row
             col_sum[b] += to_col
@@ -265,6 +263,7 @@
     half, terms, _ = own.shape
     rows, tall = up(terms, 8), up(terms, 16)
     blocks = 4 * half
+    staged = up(PITCH * (BLK // 2 + 1), 8)
     unroll = UNROLL
     smem = pl.BlockSpec(memory_space=pltpu.SMEM)
     vmem = pl.BlockSpec(memory_space=pltpu.VMEM)
@@ -276,7 +275,7 @@
         out_specs=(vmem, vmem),
         scratch_shapes=[
             pltpu.VMEM((slots, channels, BLK * BLK), BF),
-            pltpu.VMEM((max(unroll, -(-2 * half // (PITCH * BLK // 2 // LANES))), PITCH * BLK // 2, LANES), F32),
+            pltpu.VMEM((max(unroll, -(-2 * half // (staged // LANES))), staged, LANES), F32),
             pltpu.VMEM((half, 2 * LANES, 4 * LANES), BF),
             pltpu.VMEM((2,) + own_gram.shape, BF),
             pltpu.VMEM((blocks, BLK, LANES), BF),

time: 42.8 us -> 44.1 us (1.030)
  waiting for transfers between devices: 12.3 us -> 13.1 us
    ppermute x13, waiting for transfers between devices: 12.3 us -> 13.1 us  [from_partner(): lax.ppermute(array, 'tile', [(i, i ^ mask) for i in range(lax.axis_size('...]
  transfers between devices with their start and end apart: 13 -> 13, of which waited for: 9 -> 8; matrix products, arithmetic and copies ran while one was open for 0% -> 0% of each run, Pallas kernels for 4% -> 4%
where the time goes in v9:
time: 44.1 us; the launch traced here: 44 us
  starting transfers between devices  14.7 us (33%)
  waiting for transfers between devices  13.1 us (30%)
  Pallas kernels  12.7 us (29%)
  local copies, waits for them, and re-layouts  1.88 us (4%)
  other arithmetic  0.79 us (2%)
  between operations  0.77 us (2%)
    ppermute x13, starting transfers between devices, from_partner(): lax.ppermute(array, 'tile', [(i, i ^ mask) for i in range(lax.axis_size('...  14.7 us
    ppermute x13, waiting for transfers between devices, from_partner(): lax.ppermute(array, 'tile', [(i, i ^ mask) for i in range(lax.axis_size('...  13.1 us
    pallas_call x1, Pallas kernels, tile_terms(): pl.pallas_call(functools.partial(tiles_kernel, relative, unroll, scale),...  10.8 us
    pallas_call x1, Pallas kernels, gram_of(): pl.pallas_call(functools.partial(gram_kernel, math.sqrt(sources)), out_sh...  1.87 us
    slice x1, local copies, waits for them, and re-layouts, on_device(): to_move = observed[slots - moved:]  1.83 us
  transfers between devices with their start and end apart: 13, of which 8 were waited for; matrix products, arithmetic and copies ran while one was open for 0% of the time, Pallas kernels for 4%

profile of v9, /device:TPU:0, one launch (start us, length us, event | category | flops | bytes accessed | tf_op | source)
XLA Modules:
  0.0 44.0 jit_solution(810790916221289058)
XLA Ops:
  0.0 0.0 copy-start.3
  0.0 0.0 copy-start.2
  0.0 0.0 copy-start.1
  0.0 0.0 copy-start
  0.0 1.8 %slice.24 = bf16[17,16,4096]{2,1,0:T(8,128)(2,1)S(1)} slice(bf16[66,16,4096]{2,1,0:T(8,128)(2,1)} %vis_hbm.1), slice={[49:66], [0:16], [0:4096]} | slice | bytes 4456448 | tf_op jit(solution)/shard_map/slice | solution.py:309
  1.8 0.0 copy-start.4
  1.9 0.0 copy-start.5
  1.9 0.5 %collective-permute-start.7 = (bf16[17,16,4096]{2,1,0:T(8,128)(2,1)S(1)}, bf16[17,16,4096]{2,1,0:T(8,128)(2,1)S(1)}, u32[]{:S(2)}, u32[]{:S(2)}) collective-permute-start(bf16[17,16,4096]{2,1,0:T(8,128)(2,1)S(1)} %slice.24), channel_id=1, source_target_pairs={{0,1},{1,0},{2,3},{3,2},{4,5},{5,4},{6,7},{7,6},{8,9},{9,8},{10,11... | collective-permute-start | bytes 6684680 | tf_op jit(solution)/shard_map/ppermute | solution.py:296
  2.4 0.0 copy-done.3
  2.4 3.7 %collective-permute-start = (bf16[1,66,128]{2,1,0:T(8,128)(2,1)S(1)}, bf16[1,66,128]{2,1,0:T(8,128)(2,1)S(1)}, u32[]{:S(2)}, u32[]{:S(2)}) collective-permute-start(bf16[1,66,128]{2,1,0:T(8,128)(2,1)S(1)} %bitcast.3), channel_id=1, source_target_pairs={{0,8},{1,9},{2,10},{3,11},{4,12},{5,13},{6,14},{7,15},{8,0},{9,1},... | collective-permute-start | bytes 50696 | tf_op jit(solution)/shard_map/ppermute | solution.py:296
  6.1 0.0 copy-done.2
  6.1 0.0 copy-done.1
  6.1 0.0 copy-done
  6.1 1.9 %shard_map.82.own_gram_ref = bf16[592,256]{1,0:T(8,128)(2,1)S(1)} custom-call(bf16[66,4096]{1,0:T(8,128)(2,1)S(1)} %copy-done, s32[16,256]{1,0:T(8,128)S(1)} %copy-done.1, f32[16,256]{1,0:T(8,128)S(1)} %copy-done.2), custom_call_target="tpu_custom_call" | custom-call | flops 1107296256 | bytes 1048576 | tf_op jit(solution)/shard_map/pallas_call | solution.py:81
  8.0 0.0 collective-permute-done
  8.0 0.2 collective-permute-start.4
  8.9 2.6 %collective-permute-start.3 = (bf16[2,66,128]{2,1,0:T(8,128)(2,1)S(1)}, bf16[2,66,128]{2,1,0:T(8,128)(2,1)S(1)}, u32[]{:S(2)}, u32[]{:S(2)}) collective-permute-start(bf16[2,66,128]{2,1,0:T(8,128)(2,1)S(1)} %pad_maximum_fusion.1), channel_id=1, source_target_pairs={{0,6},{1,7},{2,4},{3,5},{4,2},{5,3},{6,0},{7,1},{8,14},{9,15},{10,... | collective-permute-start | bytes 101384 | tf_op jit(solution)/shard_map/ppermute | solution.py:296
  11.5 0.4 %collective-permute-start.2 = (bf16[2,66,128]{2,1,0:T(8,128)(2,1)S(1)}, bf16[2,66,128]{2,1,0:T(8,128)(2,1)S(1)}, u32[]{:S(2)}, u32[]{:S(2)}) collective-permute-start(bf16[2,66,128]{2,1,0:T(8,128)(2,1)S(1)} %pad_maximum_fusion.1), channel_id=1, source_target_pairs={{0,4},{1,5},{2,6},{3,7},{4,0},{5,1},{6,2},{7,3},{8,12},{9,13},{10,... | collective-permute-start | bytes 101384 | tf_op jit(solution)/shard_map/ppermute | solution.py:296
  11.9 0.5 %collective-permute-start.1 = (bf16[2,66,128]{2,1,0:T(8,128)(2,1)S(1)}, bf16[2,66,128]{2,1,0:T(8,128)(2,1)S(1)}, u32[]{:S(2)}, u32[]{:S(2)}) collective-permute-start(bf16[2,66,128]{2,1,0:T(8,128)(2,1)S(1)} %pad_maximum_fusion.1), channel_id=1, source_target_pairs={{0,2},{1,3},{2,0},{3,1},{4,6},{5,7},{6,4},{7,5},{8,10},{9,11},{10,... | collective-permute-start | bytes 101384 | tf_op jit(solution)/shard_map/ppermute | solution.py:296
  12.4 0.0 copy-done.4
  12.4 0.0 copy-done.5
  12.4 0.1 pad_add_fusion.mine_ref
  12.5 1.3 %collective-permute-done.3 = bf16[2,66,128]{2,1,0:T(8,128)(2,1)S(1)} collective-permute-done((bf16[2,66,128]{2,1,0:T(8,128)(2,1)S(1)}, bf16[2,66,128]{2,1,0:T(8,128)(2,1)S(1)}, u32[]{:S(2)}, u32[]{:S(2)}) %collective-permute-start.3) | collective-permute-done | bytes 33824 | tf_op jit(solution)/shard_map/ppermute | solution.py:296
  13.8 0.0 collective-permute-start.5
  13.8 1.6 %collective-permute-done.2 = bf16[2,66,128]{2,1,0:T(8,128)(2,1)S(1)} collective-permute-done((bf16[2,66,128]{2,1,0:T(8,128)(2,1)S(1)}, bf16[2,66,128]{2,1,0:T(8,128)(2,1)S(1)}, u32[]{:S(2)}, u32[]{:S(2)}) %collective-permute-start.2) | collective-permute-done | bytes 33824 | tf_op jit(solution)/shard_map/ppermute | solution.py:296
  15.4 0.4 %collective-permute-done.1 = bf16[2,66,128]{2,1,0:T(8,128)(2,1)S(1)} collective-permute-done((bf16[2,66,128]{2,1,0:T(8,128)(2,1)S(1)}, bf16[2,66,128]{2,1,0:T(8,128)(2,1)S(1)}, u32[]{:S(2)}, u32[]{:S(2)}) %collective-permute-start.1) | collective-permute-done | bytes 33824 | tf_op jit(solution)/shard_map/ppermute | solution.py:296
  15.9 0.0 collective-permute-done.5.other_ref
  15.9 0.0 collective-permute-done.4.got_gram_ref
  15.9 0.1 collective-permute-start.6
  16.0 1.4 %collective-permute-done.6.got_ref = bf16[8,66,128]{2,1,0:T(8,128)(2,1)S(1)} collective-permute-done((bf16[8,66,128]{2,1,0:T(8,128)(2,1)S(1)}, bf16[8,66,128]{2,1,0:T(8,128)(2,1)S(1)}, u32[]{:S(2)}, u32[]{:S(2)}) %collective-permute-start.6) | collective-permute-done | bytes 135200 | tf_op jit(solution)/shard_map/ppermute | solution.py:296
  17.4 0.0 collective-permute-done.7.more_hbm
  17.4 10.8 %shard_map.83 = (f32[8,66,128]{2,1,0:T(8,128)S(1)}, f32[8,66,128]{2,1,0:T(8,128)S(1)}) custom-call(s32[133]{0:T(256)S(1)} %pad_add_fusion.mine_ref, s32[133]{0:T(256)S(1)} %collective-permute-done.5.other_ref, bf16[8,66,128]{2,1,0:T(8,128)(2,1)S(1)} %pad_maximum_fusion.own_ref, bf16[8,66,128]{2,1,0:T(8,128)(2,1)S(1)} %collective-permute-done.6.got_ref, ...), custom_call_target="tpu_custom_call" | custom-call | flops 1712848896 | bytes 8650752 | tf_op jit(solution)/shard_map/pallas_call | solution.py:271
  28.2 0.2 collective-permute-start.8
  28.4 1.4 %collective-permute-done.8 = f32[8,66,128]{2,1,0:T(8,128)S(1)} collective-permute-done((f32[8,66,128]{2,1,0:T(8,128)S(1)}, f32[8,66,128]{2,1,0:T(8,128)S(1)}, u32[]{:S(2)}, u32[]{:S(2)}) %collective-permute-start.8) | collective-permute-done | bytes 270368 | tf_op jit(solution)/shard_map/ppermute | solution.py:296
  29.9 4.1 %collective-permute-start.9 = (bf16[2,66,128]{2,1,0:T(8,128)(2,1)S(1)}, bf16[2,66,128]{2,1,0:T(8,128)(2,1)S(1)}, u32[]{:S(2)}, u32[]{:S(2)}) collective-permute-start(bf16[2,66,128]{2,1,0:T(8,128)(2,1)S(1)} %get-tuple-element.21), channel_id=1, source_target_pairs={{0,6},{1,7},{2,4},{3,5},{4,2},{5,3},{6,0},{7,1},{8,14},{9,15},{10,... | collective-permute-start | bytes 101384 | tf_op jit(solution)/shard_map/ppermute | solution.py:296
  34.0 0.0 collective-permute-start.11
  34.0 0.6 %collective-permute-start.10 = (bf16[2,66,128]{2,1,0:T(8,128)(2,1)S(1)}, bf16[2,66,128]{2,1,0:T(8,128)(2,1)S(1)}, u32[]{:S(2)}, u32[]{:S(2)}) collective-permute-start(bf16[2,66,128]{2,1,0:T(8,128)(2,1)S(1)} %get-tuple-element.23), channel_id=1, source_target_pairs={{0,4},{1,5},{2,6},{3,7},{4,0},{5,1},{6,2},{7,3},{8,12},{9,13},{10,... | collective-permute-start | bytes 101384 | tf_op jit(solution)/shard_map/ppermute | solution.py:296
  34.7 1.3 %collective-permute-done.9 = bf16[2,66,128]{2,1,0:T(8,128)(2,1)S(1)} collective-permute-done((bf16[2,66,128]{2,1,0:T(8,128)(2,1)S(1)}, bf16[2,66,128]{2,1,0:T(8,128)(2,1)S(1)}, u32[]{:S(2)}, u32[]{:S(2)}) %collective-permute-start.9) | collective-permute-done | bytes 33824 | tf_op jit(solution)/shard_map/ppermute | solution.py:296
  36.0 2.0 %collective-permute-done.11 = bf16[2,66,128]{2,1,0:T(8,128)(2,1)S(1)} collective-permute-done((bf16[2,66,128]{2,1,0:T(8,128)(2,1)S(1)}, bf16[2,66,128]{2,1,0:T(8,128)(2,1)S(1)}, u32[]{:S(2)}, u32[]{:S(2)}) %collective-permute-start.11) | collective-permute-done | bytes 33824 | tf_op jit(solution)/shard_map/ppermute | solution.py:296
  38.0 0.0 collective-permute-done.10
  38.0 1.7 %collective-permute-start.12 = (f32[1,66,128]{2,1,0:T(8,128)S(1)}, f32[1,66,128]{2,1,0:T(8,128)S(1)}, u32[]{:S(2)}, u32[]{:S(2)}) collective-permute-start(f32[1,66,128]{2,1,0:T(8,128)S(1)} %slice.36), channel_id=1, source_target_pairs={{0,8},{1,9},{2,10},{3,11},{4,12},{5,13},{6,14},{7,15},{8,0},{9,1},... | collective-permute-start | bytes 101384 | tf_op jit(solution)/shard_map/ppermute | solution.py:296
  39.7 3.7 %collective-permute-done.12 = f32[1,66,128]{2,1,0:T(8,128)S(1)} collective-permute-done((f32[1,66,128]{2,1,0:T(8,128)S(1)}, f32[1,66,128]{2,1,0:T(8,128)S(1)}, u32[]{:S(2)}, u32[]{:S(2)}) %collective-permute-start.12) | collective-permute-done | bytes 33824 | tf_op jit(solution)/shard_map/ppermute | solution.py:296
  43.3 0.6 %fusion.2 = f32[66,128]{1,0:T(8,128)} fusion(f32[1,66,128]{2,1,0:T(8,128)S(1)} %collective-permute-done.12, f32[2,66,128]{2,1,0:T(8,128)S(1)} %fusion.1), kind=kLoop, calls=%fused_computation.5 | loop fusion | flops 8448 | bytes 101376 | tf_op jit(solution)/shard_map/squeeze | solution.py:329
  (6 shorter events, 0.1 us)
Async XLA Ops:
  0.0 2.4 %copy-start.3 = (bf16[66,128]{1,0:T(8,128)(2,1)S(1)}, bf16[66,128]{1,0:T(8,128)(2,1)}, u32[]{:S(2)}) copy-start(bf16[66,128]{1,0:T(8,128)(2,1)} %param.8) | copy-start | bytes 50692
  0.0 6.1 %copy-start.2 = (f32[16,256]{1,0:T(8,128)S(1)}, f32[16,256]{1,0:T(8,128)}, u32[]{:S(2)}) copy-start(f32[16,256]{1,0:T(8,128)} %flux_ref.1) | copy-start | bytes 49156
  0.0 6.1 %copy-start.1 = (s32[16,256]{1,0:T(8,128)S(1)}, s32[16,256]{1,0:T(8,128)}, u32[]{:S(2)}) copy-start(s32[16,256]{1,0:T(8,128)} %pos_ref.1) | copy-start | bytes 49156
  0.0 6.1 %copy-start = (bf16[66,4096]{1,0:T(8,128)(2,1)S(1)}, bf16[66,4096]{1,0:T(8,128)(2,1)}, u32[]{:S(2)}) copy-start(bf16[66,4096]{1,0:T(8,128)(2,1)} %table_ref.1) | copy-start | bytes 1622020
  1.8 10.6 %copy-start.4 = (s32[66]{0:T(128)S(1)}, s32[66]{0:T(128)}, u32[]{:S(2)}) copy-start(s32[66]{0:T(128)} %param.14) | copy-start | bytes 796
  1.9 10.6 %copy-start.5 = (s32[66]{0:T(128)S(1)}, s32[66]{0:T(128)}, u32[]{:S(2)}) copy-start(s32[66]{0:T(128)} %param.13) | copy-start | bytes 796
  1.9 15.5 %collective-permute-start.7 = (bf16[17,16,4096]{2,1,0:T(8,128)(2,1)S(1)}, bf16[17,16,4096]{2,1,0:T(8,128)(2,1)S(1)}, u32[]{:S(2)}, u32[]{:S(2)}) collective-permute-start(bf16[17,16,4096]{2,1,0:T(8,128)(2,1)S(1)} %slice.24), channel_id=1, source_target_pairs={{0,1},{1,0},{2,3},{3,2},{4,5},{5,4},{6,7},{7,6},{8,9},{9,8},{10,11... | collective-permute-start | bytes 6684680 | tf_op jit(solution)/shard_map/ppermute | solution.py:296
  2.4 5.6 %collective-permute-start = (bf16[1,66,128]{2,1,0:T(8,128)(2,1)S(1)}, bf16[1,66,128]{2,1,0:T(8,128)(2,1)S(1)}, u32[]{:S(2)}, u32[]{:S(2)}) collective-permute-start(bf16[1,66,128]{2,1,0:T(8,128)(2,1)S(1)} %bitcast.3), channel_id=1, source_target_pairs={{0,8},{1,9},{2,10},{3,11},{4,12},{5,13},{6,14},{7,15},{8,0},{9,1},... | collective-permute-start | bytes 50696 | tf_op jit(solution)/shard_map/ppermute | solution.py:296
  8.0 7.9 %collective-permute-start.4 = (bf16[592,256]{1,0:T(8,128)(2,1)S(1)}, bf16[592,256]{1,0:T(8,128)(2,1)S(1)}, u32[]{:S(2)}, u32[]{:S(2)}) collective-permute-start(bf16[592,256]{1,0:T(8,128)(2,1)S(1)} %shard_map.82.own_gram_ref), channel_id=1, source_target_pairs={{0,1},{1,0},{2,3},{3,2},{4,5},{5,4},{6,7},{7,6},{8,9},{9,8},{10,11... | collective-permute-start | bytes 909320 | tf_op jit(solution)/shard_map/ppermute | solution.py:296
  8.9 4.9 %collective-permute-start.3 = (bf16[2,66,128]{2,1,0:T(8,128)(2,1)S(1)}, bf16[2,66,128]{2,1,0:T(8,128)(2,1)S(1)}, u32[]{:S(2)}, u32[]{:S(2)}) collective-permute-start(bf16[2,66,128]{2,1,0:T(8,128)(2,1)S(1)} %pad_maximum_fusion.1), channel_id=1, source_target_pairs={{0,6},{1,7},{2,4},{3,5},{4,2},{5,3},{6,0},{7,1},{8,14},{9,15},{10,... | collective-permute-start | bytes 101384 | tf_op jit(solution)/shard_map/ppermute | solution.py:296
  11.5 4.0 %collective-permute-start.2 = (bf16[2,66,128]{2,1,0:T(8,128)(2,1)S(1)}, bf16[2,66,128]{2,1,0:T(8,128)(2,1)S(1)}, u32[]{:S(2)}, u32[]{:S(2)}) collective-permute-start(bf16[2,66,128]{2,1,0:T(8,128)(2,1)S(1)} %pad_maximum_fusion.1), channel_id=1, source_target_pairs={{0,4},{1,5},{2,6},{3,7},{4,0},{5,1},{6,2},{7,3},{8,12},{9,13},{10,... | collective-permute-start | bytes 101384 | tf_op jit(solution)/shard_map/ppermute | solution.py:296
  11.9 4.0 %collective-permute-start.1 = (bf16[2,66,128]{2,1,0:T(8,128)(2,1)S(1)}, bf16[2,66,128]{2,1,0:T(8,128)(2,1)S(1)}, u32[]{:S(2)}, u32[]{:S(2)}) collective-permute-start(bf16[2,66,128]{2,1,0:T(8,128)(2,1)S(1)} %pad_maximum_fusion.1), channel_id=1, source_target_pairs={{0,2},{1,3},{2,0},{3,1},{4,6},{5,7},{6,4},{7,5},{8,10},{9,11},{10,... | collective-permute-start | bytes 101384 | tf_op jit(solution)/shard_map/ppermute | solution.py:296
  13.8 2.1 %collective-permute-start.5 = (s32[133]{0:T(256)S(1)}, s32[133]{0:T(256)S(1)}, u32[]{:S(2)}, u32[]{:S(2)}) collective-permute-start(s32[133]{0:T(256)S(1)} %pad_add_fusion.mine_ref), channel_id=1, source_target_pairs={{0,1},{1,0},{2,3},{3,2},{4,5},{5,4},{6,7},{7,6},{8,9},{9,8},{10,11... | collective-permute-start | bytes 1604 | tf_op jit(solution)/shard_map/ppermute | solution.py:296
  15.9 1.4 %collective-permute-start.6 = (bf16[8,66,128]{2,1,0:T(8,128)(2,1)S(1)}, bf16[8,66,128]{2,1,0:T(8,128)(2,1)S(1)}, u32[]{:S(2)}, u32[]{:S(2)}) collective-permute-start(bf16[8,66,128]{2,1,0:T(8,128)(2,1)S(1)} %pad_maximum_fusion.own_ref), channel_id=1, source_target_pairs={{0,1},{1,0},{2,3},{3,2},{4,5},{5,4},{6,7},{7,6},{8,9},{9,8},{10,11... | collective-permute-start | bytes 405512 | tf_op jit(solution)/shard_map/ppermute | solution.py:296
  28.2 1.6 %collective-permute-start.8 = (f32[8,66,128]{2,1,0:T(8,128)S(1)}, f32[8,66,128]{2,1,0:T(8,128)S(1)}, u32[]{:S(2)}, u32[]{:S(2)}) collective-permute-start(f32[8,66,128]{2,1,0:T(8,128)S(1)} %get-tuple-element.18), channel_id=1, source_target_pairs={{0,1},{1,0},{2,3},{3,2},{4,5},{5,4},{6,7},{7,6},{8,9},{9,8},{10,11... | collective-permute-start | bytes 811016 | tf_op jit(solution)/shard_map/ppermute | solution.py:296
  29.9 6.1 %collective-permute-start.9 = (bf16[2,66,128]{2,1,0:T(8,128)(2,1)S(1)}, bf16[2,66,128]{2,1,0:T(8,128)(2,1)S(1)}, u32[]{:S(2)}, u32[]{:S(2)}) collective-permute-start(bf16[2,66,128]{2,1,0:T(8,128)(2,1)S(1)} %get-tuple-element.21), channel_id=1, source_target_pairs={{0,6},{1,7},{2,4},{3,5},{4,2},{5,3},{6,0},{7,1},{8,14},{9,15},{10,... | collective-permute-start | bytes 101384 | tf_op jit(solution)/shard_map/ppermute | solution.py:296
  34.0 4.0 %collective-permute-start.11 = (bf16[2,66,128]{2,1,0:T(8,128)(2,1)S(1)}, bf16[2,66,128]{2,1,0:T(8,128)(2,1)S(1)}, u32[]{:S(2)}, u32[]{:S(2)}) collective-permute-start(bf16[2,66,128]{2,1,0:T(8,128)(2,1)S(1)} %get-tuple-element.22), channel_id=1, source_target_pairs={{0,2},{1,3},{2,0},{3,1},{4,6},{5,7},{6,4},{7,5},{8,10},{9,11},{10,... | collective-permute-start | bytes 101384 | tf_op jit(solution)/shard_map/ppermute | solution.py:296
  34.0 4.0 %collective-permute-start.10 = (bf16[2,66,128]{2,1,0:T(8,128)(2,1)S(1)}, bf16[2,66,128]{2,1,0:T(8,128)(2,1)S(1)}, u32[]{:S(2)}, u32[]{:S(2)}) collective-permute-start(bf16[2,66,128]{2,1,0:T(8,128)(2,1)S(1)} %get-tuple-element.23), channel_id=1, source_target_pairs={{0,4},{1,5},{2,6},{3,7},{4,0},{5,1},{6,2},{7,3},{8,12},{9,13},{10,... | collective-permute-start | bytes 101384 | tf_op jit(solution)/shard_map/ppermute | solution.py:296
  38.0 5.3 %collective-permute-start.12 = (f32[1,66,128]{2,1,0:T(8,128)S(1)}, f32[1,66,128]{2,1,0:T(8,128)S(1)}, u32[]{:S(2)}, u32[]{:S(2)}) collective-permute-start(f32[1,66,128]{2,1,0:T(8,128)S(1)} %slice.36), channel_id=1, source_target_pairs={{0,8},{1,9},{2,10},{3,11},{4,12},{5,13},{6,14},{7,15},{8,0},{9,1},... | collective-permute-start | bytes 101384 | tf_op jit(solution)/shard_map/ppermute | solution.py:296
